TPU v7x, 32 devices: a whole 2x2x4 slice. The times are simulated.
32 devices in a mesh: dp: 2 (over y), seq: 16 (over z, x, core).
Axes of the slice: x: 2, y: 2, z: 4, core: 2. Of those that a mesh axis runs over, the one named last changes fastest.
Arguments:
- tokens: bfloat16 [2, 4096, 768], P('dp', 'seq'), may hold values from -6 to 6
- segment_ids: int32 [2, 4096], P('dp', 'seq'), may hold values from 0 to 7, never falling along the last dimension, each value on 1 to 2048 neighbouring positions
- features: bfloat16 [12, 64, 256], replicated, may hold values from -6 to 6
- query_weight: bfloat16 [768, 768], replicated, may hold values from -0.15625 to 0.15625
- key_weight: bfloat16 [768, 768], replicated, may hold values from -0.15625 to 0.15625
- value_weight: bfloat16 [768, 768], replicated, may hold values from -0.21875 to 0.21875
- out_weight: bfloat16 [768, 768], replicated, may hold values from -0.875 to 0.875
- up_weight: bfloat16 [768, 3072], replicated, may hold values from -0.21875 to 0.21875
- down_weight: bfloat16 [3072, 768], replicated, may hold values from -0.109375 to 0.109375
- first_gain: float32 [768], replicated, may hold values from 0.1 to 1.9
- first_bias: float32 [768], replicated, may hold values from -3 to 3
- second_gain: float32 [768], replicated, may hold values from 0.1 to 1.9
- second_bias: float32 [768], replicated, may hold values from -3 to 3
- cotangent: bfloat16 [2, 4096, 768], P('dp', 'seq'), may hold values from -6 to 6
Outputs:
- output: bfloat16 [2, 4096, 768], P('dp', 'seq')
- grad_tokens: bfloat16 [2, 4096, 768], P('dp', 'seq')
- grad_query: float32 [768, 768], replicated
- grad_key: float32 [768, 768], replicated
- grad_value: float32 [768, 768], replicated
- grad_out: float32 [768, 768], replicated
- grad_up: float32 [768, 3072], replicated
- grad_down: float32 [3072, 768], replicated
- grad_first_gain: float32 [768], replicated
- grad_first_bias: float32 [768], replicated
- grad_second_gain: float32 [768], replicated
- grad_second_bias: float32 [768], replicated
Inputs may be any that keep to these rules, and one draw needn't show every extreme that they name: `segment_ids`: in each row the ids never fall, every id from 0 to 7 occurs, each on 1 to 2048 positions, and one on exactly 2048.
All inputs are finite; a program needn't handle non-finite values.
Results may differ from a plain program's by a relative error of at most 0.02.
Values sent between devices are 32-bit elements; how exact they have to be, the bound alone decides.
No kernel may reach another device: no remote copies, remote signals or barrier semaphores. Data moves between devices by JAX's collectives and lax.ppermute only.
A program may use at most 320 MiB of HBM per device.

v0:
```python
import jax
import jax.numpy as jnp
from jax import lax
from jax.experimental import pallas as pl
from jax.experimental.pallas import tpu as pltpu
from jax.sharding import PartitionSpec as P

SEG_MOST = 2048
SPARE_ROWS = 64
EPSILON = 1e-06
AXES = ("dp", "seq")
BF = jnp.bfloat16
F32 = jnp.float32
ANY = pl.BlockSpec(memory_space=pl.ANY)
HBM = pl.BlockSpec(memory_space=pltpu.HBM)
ROOM = 20 << 20
SMALL = 14 << 20


SCALE = 3


def cost(us):
    return pl.CostEstimate(flops=int(us * 1e9), bytes_accessed=1, transcendentals=0)


def shaped(*shape, dtype=F32):
    return jax.ShapeDtypeStruct(shape, dtype)


def mm(a, b):
    return jnp.dot(a, b, preferred_element_type=F32)


def mm_nt(a, b):
    return lax.dot_general(a, b, (((1,), (1,)), ((), ())), preferred_element_type=F32)


def mm_tn(a, b):
    return lax.dot_general(a, b, (((0,), (0,)), ((), ())), preferred_element_type=F32)


def dslice(a, start, size, axis=0):
    return lax.dynamic_slice_in_dim(a, start, size, axis)


class Net:
    def __init__(self, n_dp, n_seq):
        self.n_dp, self.n_seq = n_dp, n_seq
        self.nz = 4
        self.nx = n_seq // 8
        self.fast = n_dp == 2 and n_seq == 16
        seq = lax.axis_index("seq")
        self.y = lax.axis_index("dp")
        self.core = seq % 2
        self.x = (seq // 2) % self.nx
        self.z = seq // (2 * self.nx)
        self.seq = seq

    def perm(self, move):
        pairs = []
        for y in range(self.n_dp):
            for s in range(self.n_seq):
                target = move(y, s // (2 * self.nx), (s // 2) % self.nx, s % 2)
                if target is not None:
                    ty, tz, tx, tc = target
                    pairs.append((y * self.n_seq + s, ty * self.n_seq + (tz * self.nx + tx) * 2 + tc))
        return pairs

    def send(self, value, move):
        return lax.ppermute(value, AXES, self.perm(move))

    def over_core(self, value):
        return self.send(value, lambda y, z, x, c: (y, z, x, 1 - c))

    def over_x(self, value):
        return self.send(value, lambda y, z, x, c: (y, z, 1 - x, c))

    def z_up(self, value):
        return self.send(value, lambda y, z, x, c: (y, z + 1, x, c) if z < 3 else None)

    def z_down(self, value):
        return self.send(value, lambda y, z, x, c: (y, z - 1, x, c) if z > 0 else None)

    def shift(self, value, step):
        chips = self.n_seq // 2
        pairs = []
        for y in range(self.n_dp):
            for s in range(self.n_seq):
                if 0 <= s // 2 + step < chips:
                    pairs.append((y * self.n_seq + s, y * self.n_seq + s + 2 * step))
        return lax.ppermute(value, AXES, pairs)


ORDERS = ((("x", "y", "1", "2"), ("y", "x", "2", "1")), (("1", "2", "x", "y"), ("2", "1", "x", "y")))


def stage_move(net, value, stream, stage):
    def move(y, z, x, c):
        axis = ORDERS[stream][c][stage]
        return {
            "x": (y, z, 1 - x, c),
            "y": (1 - y, z, x, c),
            "1": (y, z ^ 1, x, c),
            "2": (y, z ^ 2, x, c),
        }[axis]

    return net.send(value, move)


def stage_bit(net, stream, stage, core):
    place = {"x": net.x, "y": net.y, "1": net.z % 2, "2": net.z // 2}
    zero, one = (place[ORDERS[stream][c][stage]] for c in (0, 1))
    return jnp.where(core == 0, zero, one)


def tie(value, *deps):
    def kernel(*refs):
        pass

    anywhere = pl.BlockSpec(memory_space=pl.ANY)
    return pl.pallas_call(
        kernel,
        in_specs=[anywhere] * (1 + len(deps)),
        out_specs=anywhere,
        out_shape=jax.ShapeDtypeStruct(value.shape, value.dtype),
        input_output_aliases={0: 0},
        compiler_params=pltpu.CompilerParams(vmem_limit_bytes=SMALL),
        cost_estimate=cost(0.1),
        name="tie",
    )(value, *deps)


def moves(net, parts, stage):
    return [stage_move(net, part, i, stage) for i, part in enumerate(parts)]


def stage_bits(net, stage, core=None):
    core = net.core if core is None else core
    return jnp.stack([stage_bit(net, i, stage, core) for i in range(2)]).astype(jnp.int32)


def add_stage(net, keeps, gots, stage, deps=()):
    steps = max(1, keeps[0].shape[0] // 288)

    def kernel(bits_ref, *refs):
        outs = refs[8 + len(deps) :]
        for i in range(4):
            outs[i][...] = refs[2 * i][...] + refs[2 * i + 1][...]

    in_specs, inputs, out_specs, shapes = [], [], [], []
    for side in (0, 1):
        for i, (keep, got) in enumerate(zip(keeps, gots)):
            half, width = keep.shape[0] // 2, keep.shape[1]
            block = (half // steps, width)
            spec = pl.BlockSpec(
                block,
                lambda r, bits, i=i, side=side: (
                    (bits[i] if side else 1 - bits[i]) * steps + r,
                    0,
                ),
            )
            in_specs += [spec, spec]
            inputs += [keep, got]
            out_specs.append(pl.BlockSpec(block, lambda r, bits: (r, 0)))
            shapes.append(shaped(half, width))
    in_specs += [ANY] * len(deps)
    outs = pl.pallas_call(
        kernel,
        grid_spec=pltpu.PrefetchScalarGridSpec(
            num_scalar_prefetch=1, grid=(steps,), in_specs=in_specs, out_specs=out_specs
        ),
        out_shape=shapes,
        compiler_params=pltpu.CompilerParams(vmem_limit_bytes=SMALL),
        cost_estimate=cost(4 * SCALE),
        name="add_stage",
    )(stage_bits(net, stage), *inputs, *deps)
    return outs[:2], outs[2:]


def last_add(keeps, gots, deps=()):
    def kernel(*refs):
        outs = refs[4 + len(deps) :]
        for i in range(2):
            outs[i][...] = refs[i][...] + refs[2 + i][...]

    whole = pl.BlockSpec(memory_space=pltpu.VMEM)
    return pl.pallas_call(
        kernel,
        in_specs=[whole] * 4 + [ANY] * len(deps),
        out_specs=[whole] * 2,
        out_shape=[shaped(*k.shape) for k in keeps],
        compiler_params=pltpu.CompilerParams(vmem_limit_bytes=SMALL),
        cost_estimate=cost(1.5 * SCALE),
        name="last_add",
    )(*keeps, *gots, *deps)


def join_stage(net, parts, gots, stage, deps=()):
    steps = max(1, parts[0].shape[0] // 144)

    def kernel(bits_ref, *refs):
        outs = refs[4 + len(deps) :]
        for i in range(2):
            bit = bits_ref[i]
            outs[i][pl.ds(bit, 1)] = refs[2 * i][...][None]
            outs[i][pl.ds(1 - bit, 1)] = refs[2 * i + 1][...][None]

    in_specs, out_specs, shapes = [], [], []
    for part in parts:
        n, width = part.shape
        rows = n // steps
        in_specs += [pl.BlockSpec((rows, width), lambda r, bits: (r, 0))] * 2
        out_specs.append(pl.BlockSpec((2, rows, width), lambda r, bits: (0, r, 0)))
        shapes.append(shaped(2, n, width))
    outs = pl.pallas_call(
        kernel,
        grid_spec=pltpu.PrefetchScalarGridSpec(
            num_scalar_prefetch=1,
            grid=(steps,),
            in_specs=in_specs + [ANY] * len(deps),
            out_specs=out_specs,
        ),
        out_shape=shapes,
        compiler_params=pltpu.CompilerParams(vmem_limit_bytes=SMALL),
        cost_estimate=cost(3 * SCALE),
        name="join_stage",
    )(stage_bits(net, stage), *[v for pair in zip(parts, gots) for v in pair], *deps)
    return [out.reshape(2 * out.shape[1], out.shape[2]) for out in outs]


def tn(a, a_other, b, b_other):
    return mm_tn(a, b) + mm_tn(a_other.astype(BF), b_other.astype(BF))


def picked_columns(count, size, index):
    return pl.BlockSpec((count, size), lambda g, bits: (0, index(bits)))


def whole_of(array):
    return pl.BlockSpec(array.shape, lambda g, bits: (0,) * array.ndim)


def down_products(bits, act, act_other, gz, gz_other, deps=()):
    count, width = gz.shape
    unit = act.shape[1] // 12
    sizes = (5 * unit, unit)

    def kernel(bits_ref, a0, a0o, a1, a1o, gz_r, gzo_r, *rest):
        outs, scratch, sems = rest[len(deps) : -2], rest[-2], rest[-1]
        scratch[: sizes[0], :] = tn(a0[...], a0o[...], gz_r[...], gzo_r[...])
        scratch[sizes[0] :, :] = tn(a1[...], a1o[...], gz_r[...], gzo_r[...])
        copies = [
            pltpu.make_async_copy(
                scratch.at[: sizes[0]], outs[0].at[outs[0].shape[0] - sizes[0] :], sems.at[0]
            ),
            pltpu.make_async_copy(
                scratch.at[sizes[0] :], outs[1].at[outs[1].shape[0] - sizes[1] :], sems.at[1]
            ),
        ]
        for copy in copies:
            copy.start()
        for copy in copies:
            copy.wait()

    first = picked_columns(count, sizes[0], lambda bits: bits[0])
    second = picked_columns(count, sizes[1], lambda bits: 10 + bits[1])
    up_rows = act.shape[1] // width * (width // 6)
    return pl.pallas_call(
        kernel,
        grid_spec=pltpu.PrefetchScalarGridSpec(
            num_scalar_prefetch=1,
            grid=(1,),
            in_specs=[first, first, second, second, whole_of(gz), whole_of(gz_other)]
            + [ANY] * len(deps),
            out_specs=[ANY, ANY],
            scratch_shapes=[
                pltpu.VMEM((6 * unit, width), F32),
                pltpu.SemaphoreType.DMA((2,)),
            ],
        ),
        out_shape=[shaped(2 * up_rows + sizes[0], width), shaped(up_rows + sizes[1], width)],
        compiler_params=pltpu.CompilerParams(vmem_limit_bytes=ROOM),
        cost_estimate=cost(4 * SCALE),
        name="down_products",
    )(bits, act, act_other, act, act_other, gz, gz_other, *deps)


def up_products(bits, y1, y1_other, gi, gi_other, outs, big):
    count, width = y1.shape
    u = width // 6
    parts = gi.shape[1] // width

    def kernel(bits_ref, y1_r, y1o_r, gi_r, gio_r, *rest):
        outs = rest[2:]

        def fill(out):
            y, yo = y1_r[...], y1o_r[...]
            for part in range(parts):
                cut = slice(part * width, (part + 1) * width)
                out[part * u : (part + 1) * u, :] = tn(y, yo, gi_r[:, cut], gio_r[:, cut])

        pl.when(pl.program_id(0) < 2)(lambda: fill(outs[0]))
        pl.when(pl.program_id(0) == 2)(lambda: fill(outs[1]))

    picked = pl.BlockSpec(
        (count, u), lambda i, bits: (0, jnp.where(i < 2, 2 * bits[0] + i, 4 + bits[1]))
    )
    return pl.pallas_call(
        kernel,
        grid_spec=pltpu.PrefetchScalarGridSpec(
            num_scalar_prefetch=1,
            grid=(3,),
            in_specs=[picked, picked, whole_of(gi), whole_of(gi_other), ANY, ANY],
            out_specs=[
                pl.BlockSpec((parts * u, width), lambda i, bits: (jnp.minimum(i, 1), 0)),
                pl.BlockSpec((parts * u, width), lambda i, bits: (0, 0)),
            ],
        ),
        out_shape=[shaped(*o.shape) for o in outs],
        input_output_aliases={5: 0, 6: 1},
        compiler_params=pltpu.CompilerParams(vmem_limit_bytes=ROOM),
        cost_estimate=cost(big),
        name="up_products",
    )(bits, y1, y1_other, gi, gi_other, *outs)


def attn_products(bits, x, x_other, dq, dk, dv, attn, go, go_other, small, deps=()):
    count, width = x.shape
    mine = attn.shape[1]
    cut = 2 * mine // 3

    def kernel(
        bits_ref, x0, x0o, x1, x1o, dq_r, dk_r, dv_r, attn_r, go_r, goo_r, small_r, *rest
    ):
        one, two = rest[len(deps) :]
        x, xo = x0[...], x0o[...].astype(BF)
        one[:mine, :] = tn(x, xo, dq_r[:count], dq_r[count:])
        one[mine : 2 * mine, :] = tn(x, xo, dk_r[:count], dk_r[count:])
        part = attn_r[...].astype(BF)
        one[2 * mine : 3 * mine, :] = tn(part[:count], part[count:], go_r[...], goo_r[...])
        one[3 * mine :, :] = tn(x[:, :cut], xo[:, :cut], dv_r[:count], dv_r[count:])
        rest_rows = mine - cut
        two[:rest_rows, :] = tn(x1[:, cut:], x1o[:, cut:], dv_r[:count], dv_r[count:])
        two[rest_rows:, :] = jnp.zeros((SPARE_ROWS, mine), F32)
        two[rest_rows : rest_rows + 8, :] = small_r[...]

    first = picked_columns(count, mine, lambda bits: bits[0])
    second = picked_columns(count, mine, lambda bits: bits[1])
    return pl.pallas_call(
        kernel,
        grid_spec=pltpu.PrefetchScalarGridSpec(
            num_scalar_prefetch=1,
            grid=(1,),
            in_specs=[first, first, second, second]
            + [whole_of(v) for v in (dq, dk, dv, attn)]
            + [first, first, whole_of(small)]
            + [ANY] * len(deps),
            out_specs=[
                pl.BlockSpec((3 * mine + cut, mine), lambda g, bits: (0, 0)),
                pl.BlockSpec((mine - cut + SPARE_ROWS, mine), lambda g, bits: (0, 0)),
            ],
        ),
        out_shape=[shaped(3 * mine + cut, mine), shaped(mine - cut + SPARE_ROWS, mine)],
        compiler_params=pltpu.CompilerParams(vmem_limit_bytes=ROOM),
        cost_estimate=cost(4 * SCALE),
        name="attn_products",
    )(bits, x, x_other, x, x_other, dq, dk, dv, attn, go, go_other, small, *deps)


def place_pieces(net, pieces, outs, copies, deps=()):
    fresh = isinstance(outs[0], jax.ShapeDtypeStruct)
    n_out, n = len(outs), len(pieces)
    inputs = [part for piece in pieces for part in piece[0]]
    scalars = []
    for _, other_core, other_first, other_second in pieces:
        core = 1 - net.core if other_core else net.core
        scalars.append(core)
        for i in range(2):
            for stage, flip in ((0, other_first), (1, other_second)):
                bit = stage_bit(net, i, stage, core)
                scalars.append(1 - bit if flip else bit)
    where = jnp.stack(scalars).astype(jnp.int32)

    def kernel(where_ref, *refs):
        srcs = refs[: 2 * n]
        dests = refs[-(2 * n + 3 + n_out) : -(2 * n + 3)]
        refs[-(2 * n + 3)][...] = jnp.zeros((8, 128), F32)
        held, (arrive, sems) = refs[-(2 * n + 2) : -2], refs[-2:]
        loads = [pltpu.make_async_copy(srcs[j], held[j], arrive.at[j]) for j in range(2 * n)]
        for load in loads:
            load.start()

        def each(j, act):
            piece, i = j // 2, j % 2
            core = where_ref[5 * piece]
            first, second = where_ref[5 * piece + 1 + 2 * i], where_ref[5 * piece + 2 + 2 * i]
            for quarter in (0, 1):

                @pl.when(second == quarter)
                def _():
                    for k, (src, dest) in enumerate(copies(i, quarter, core, first, held[j], dests)):
                        act(pltpu.make_async_copy(src, dest, sems.at[j, k]))

        for j in range(2 * n):
            loads[j].wait()
            each(j, lambda copy: copy.start())
        for j in range(2 * n):
            each(j, lambda copy: copy.wait())

    operands = inputs + ([] if fresh else list(outs)) + list(deps)
    *outs, done = pl.pallas_call(
        kernel,
        grid_spec=pltpu.PrefetchScalarGridSpec(
            num_scalar_prefetch=1,
            grid=(1,),
            in_specs=[ANY] * len(inputs) + [HBM] * (0 if fresh else n_out) + [ANY] * len(deps),
            out_specs=[HBM] * n_out + [pl.BlockSpec((8, 128), lambda g, where: (0, 0))],
            scratch_shapes=[pltpu.VMEM(part.shape, F32) for part in inputs] + [
                pltpu.SemaphoreType.DMA((2 * n,)),
                pltpu.SemaphoreType.DMA((2 * n, 6)),
            ],
        ),
        out_shape=[shaped(*o.shape) for o in outs] + [shaped(8, 128)],
        input_output_aliases={} if fresh else {1 + 2 * n + i: i for i in range(n_out)},
        compiler_params=pltpu.CompilerParams(vmem_limit_bytes=ROOM),
        cost_estimate=cost(4.5 * SCALE),
        name="place_pieces",
    )(where, *operands)
    return outs, [done]


def rows_at(ref, start, size, step, lanes=None):
    start = pl.multiple_of(start, step)
    return ref.at[pl.ds(start, size)] if lanes is None else ref.at[pl.ds(start, size), lanes]


def spans(sizes, at, length):
    start = 0
    for k, size in enumerate(sizes):
        low, high = max(start, at), min(start + size, at + length)
        if low < high:
            yield k, low - start, low - at, high - low
        start += size


def ffn_copies(width, ff_half):
    u, unit = width // 6, ff_half // 12
    parts = ff_half // width

    def copies(i, quarter, c, b, src, dests):
        up, down = dests
        blocks = 1 if i else 2
        sizes = [u] * (parts * blocks) + [unit if i else 5 * unit]
        length = src.shape[0]
        for k, row, at, n in spans(sizes, quarter * length, length):
            if k < parts * blocks:
                block = 4 + b if i else 2 * b + k // parts
                lanes = pl.ds(pl.multiple_of(c * ff_half + k % parts * width, 128), width)
                dest = rows_at(up, block * u + row, n, 8, lanes)
            else:
                start = 10 * unit + b * unit if i else 5 * unit * b
                dest = rows_at(down, c * ff_half + start + row, n, 8)
            yield src.at[at : at + n], dest

    return copies


def attn_copies(mine):
    def copies(i, quarter, c, b, src, dests):
        own = pl.ds(pl.multiple_of(c * mine, 128), mine)
        half = pl.ds(pl.multiple_of(b * mine, 128), mine)
        cut = 2 * mine // 3
        sizes = [mine - cut] if i else [mine] * 3 + [cut]
        length = src.shape[0]
        for k, row, at, n in spans(sizes, quarter * length, length):
            if i:
                dest = rows_at(dests[2], b * mine + cut + row, n, 8, own)
            elif k != 2:
                dest = rows_at(dests[min(k, 2)], b * mine + row, n, 8, own)
            else:
                dest = rows_at(dests[3], c * mine + row, n, 8, half)
            yield src.at[at : at + n], dest

    return copies


def total(net, half, axis):
    size = half.shape[axis]
    shape = tuple(2 * n if i == axis else n for i, n in enumerate(half.shape))
    own = lax.dynamic_update_slice_in_dim(jnp.zeros(shape, F32), half, net.core * size, axis)
    return lax.psum(own, AXES)


def per_row(array):
    rest = array.shape[1:]
    return pl.BlockSpec((1, *rest), lambda r, info: (r, *(0 for _ in rest)))


COSTS = {"keys": 10, "queries": 8, "attend": 6, "grads_one": 3, "grads_two": 12, "grads_three": 8, "shares": 3 * SCALE, "join_plane": 3, "split_plane": 3}


def row_call(kernel, name, info, inputs, in_specs, outs, deps=(), flops=0):
    n_in = len(inputs)
    rows = outs[0].shape[0]

    def run(info_ref, *refs):
        kernel(info_ref, *refs[:n_in], *refs[n_in + len(deps) :])

    size = sum(v.size * v.dtype.itemsize for v in [*inputs, *outs])
    return pl.pallas_call(
        run,
        grid_spec=pltpu.PrefetchScalarGridSpec(
            num_scalar_prefetch=1,
            grid=(rows,),
            in_specs=list(in_specs) + [ANY] * len(deps),
            out_specs=[per_row(o) for o in outs],
        ),
        out_shape=outs,
        compiler_params=pltpu.CompilerParams(vmem_limit_bytes=ROOM),
        cost_estimate=cost(COSTS[name]),
        name=name,
    )(info, *inputs, *deps)


def edges(idc_ref, idr_ref):
    row = idr_ref[0]
    first = jnp.min(row, axis=1, keepdims=True)
    last = jnp.max(row, axis=1, keepdims=True)
    return idc_ref[0] == first, idc_ref[0] == last, first, last


def phi(part, feats):
    head_dim, feat_count = feats.shape
    wide = part.astype(F32)
    square = jnp.sum(wide * wide, -1, keepdims=True)
    inner = mm(part, feats) * head_dim ** (-0.25) - square * (0.5 * head_dim ** (-0.5))
    return (jnp.exp(inner) * feat_count ** (-0.5)).astype(BF)


def put_edges(info_ref, keep, send, h, heads, sums, lead_z, tail_z):
    half = heads // 2
    group, at = h // half, h % half
    e = sums.shape[0] // 2

    def put(ref):
        ref[0, 0, at * e : (at + 1) * e, :] = sums[:e]
        ref[0, 1, at * e : (at + 1) * e, :] = sums[e:]
        ref[0, 0, half * e + at : half * e + at + 1, :] = lead_z
        ref[0, 1, half * e + at : half * e + at + 1, :] = tail_z

    @pl.when(info_ref[1] == group)
    def _():
        put(keep)

    @pl.when(info_ref[1] != group)
    def _():
        put(send)


def put_tags(keep, send, spare, first, last):
    n, m = keep.shape[2:]
    for ref in (keep, send):
        ref[0, 0, spare:, :] = jnp.broadcast_to(first, (n - spare, m))
        ref[0, 1, spare:, :] = jnp.broadcast_to(last, (n - spare, m))


def weight_columns(weight, mine):
    return pl.BlockSpec((weight.shape[0], mine), lambda r, info: (0, info[0]))


def head_features(features, heads):
    return pl.BlockSpec((heads, *features.shape[1:]), lambda r, info: (info[0], 0, 0))


def keys_kernel(info, x, x_got, key_weight, value_weight, features, idc, idr):
    rows, length, width = x.shape
    mine, heads = width // 2, features.shape[0] // 2
    e, m = features.shape[1:]
    n = heads // 2 * e + 8
    spare = heads // 2 * e + heads // 2

    def kernel(info_ref, x_r, xg_r, wk_r, wv_r, f_r, idc_r, idr_r, k_o, v_o, fk_o, keep, send):
        chip = jnp.concatenate([x_r[0], xg_r[0].astype(BF)], 0)
        keys = mm(chip, wk_r[...]).astype(BF)
        values = mm(chip, wv_r[...]).astype(BF)
        k_o[0] = keys
        v_o[0] = values
        lead, tail, first, last = edges(idc_r, idr_r)
        masks = jnp.concatenate([lead.astype(F32), tail.astype(F32)], 1).astype(BF)
        lead_b, tail_b = masks[:, 0:1], masks[:, 1:2]
        for h in range(heads):
            cut = slice(h * e, (h + 1) * e)
            feat = phi(keys[:, cut], f_r[h])
            fk_o[0, h] = feat
            part = values[:, cut]
            sums = mm_tn(jnp.concatenate([part * lead_b, part * tail_b], 1), feat)
            zs = mm_tn(masks, feat)
            put_edges(info_ref, keep, send, h, heads, sums, zs[0:1], zs[1:2])
        put_tags(keep, send, spare, first, last)

    outs = [
        shaped(rows, 2 * length, mine, dtype=BF),
        shaped(rows, 2 * length, mine, dtype=BF),
        shaped(rows, heads, 2 * length, m, dtype=BF),
        shaped(rows, 2, n, m),
        shaped(rows, 2, n, m),
    ]
    specs = [
        per_row(x), per_row(x_got),
        weight_columns(key_weight, mine), weight_columns(value_weight, mine),
        head_features(features, heads), per_row(idc), per_row(idr),
    ]
    return row_call(
        kernel, "keys", info, [x, x_got, key_weight, value_weight, features, idc, idr], specs, outs,
        flops=rows * length * width * mine * 10,
    )


def queries_kernel(info, x, x_got, query_weight, features, fk, values, idc, idr, deps=()):
    rows, length, width = x.shape
    mine, heads = width // 2, features.shape[0] // 2
    e, m = features.shape[1:]

    def kernel(info_ref, x_r, xg_r, wq_r, f_r, fk_r, v_r, idc_r, idr_r, q_o, fq_o, num_o, den_o):
        chip = jnp.concatenate([x_r[0], xg_r[0].astype(BF)], 0)
        queries = mm(chip, wq_r[...]).astype(BF)
        q_o[0] = queries
        same = idc_r[0] == idr_r[0]
        lane = lax.broadcasted_iota(jnp.int32, (2 * length, 128), 1)
        dens = jnp.ones((2 * length, 128), F32)
        for h in range(heads):
            cut = slice(h * e, (h + 1) * e)
            feat = phi(queries[:, cut], f_r[h])
            fq_o[0, h] = feat
            scores = jnp.where(same, mm_nt(feat, fk_r[0, h]), 0.0)
            num_o[0, :, cut] = mm(scores.astype(BF), v_r[0, :, cut])
            dens = jnp.where(lane == h, jnp.sum(scores, -1, keepdims=True), dens)
        den_o[0] = dens

    outs = [
        shaped(rows, 2 * length, mine, dtype=BF),
        shaped(rows, heads, 2 * length, m, dtype=BF),
        shaped(rows, 2 * length, mine),
        shaped(rows, 2 * length, 128),
    ]
    specs = [
        per_row(x), per_row(x_got), weight_columns(query_weight, mine),
        head_features(features, heads), per_row(fk), per_row(values), per_row(idc), per_row(idr),
    ]
    return row_call(
        kernel, "queries", info,
        [x, x_got, query_weight, features, fk, values, idc, idr], specs, outs, deps,
        flops=rows * length * width * mine * 12,
    )


def carry_of(info_ref, own_r, got_r, h, heads, e):
    half = heads // 2
    group, at = h // half, h % half
    flag = info_ref[1] == group

    def picked(k, rows):
        return jnp.where(flag, own_r[0, k, rows, :], got_r[0, k, rows, :])

    kv = slice(at * e, (at + 1) * e)
    z = slice(half * e + at, half * e + at + 1)
    return picked(0, kv), picked(1, kv), picked(0, z), picked(1, z)


def attend_kernel(info, fq, num, den, own, got, idc, idr):
    rows, heads, chip_len, m = fq.shape
    mine = num.shape[2]
    e = mine // heads
    length = chip_len // 2

    def kernel(info_ref, fq_r, num_r, den_r, own_r, got_r, idc_r, idr_r, att_o, den_o, here_o, send_o):
        lead, tail, _, _ = edges(idc_r, idr_r)
        lead, tail = lead.astype(F32), tail.astype(F32)
        lane = lax.broadcasted_iota(jnp.int32, (chip_len, 128), 1)
        dens = den_r[0]
        for h in range(heads):
            cut = slice(h * e, (h + 1) * e)
            before, behind, zb, za = carry_of(info_ref, own_r, got_r, h, heads, e)
            feat = fq_r[0, h]
            more = mm_nt(feat, jnp.concatenate([before, behind], 0).astype(BF))
            numer = num_r[0, :, cut] + lead * more[:, :e] + tail * more[:, e:]
            extra = jnp.sum(feat.astype(F32) * (lead * zb + tail * za), -1, keepdims=True)
            denom = den_r[0, :, h : h + 1] + extra
            dens = jnp.where(lane == h, denom, dens)
            att = numer / denom
            att_o[0, :, cut] = att
            rounded = att.astype(BF)
            here_o[0, :, cut] = rounded[:length]
            send_o[0, :, cut] = rounded[length:].astype(F32)
        den_o[0] = dens

    outs = [
        shaped(rows, chip_len, mine),
        shaped(rows, chip_len, 128),
        shaped(rows, length, mine, dtype=BF),
        shaped(rows, length, mine),
    ]
    inputs = [fq, num, den, own, got, idc, idr]
    return row_call(
        kernel, "attend", info, inputs, [per_row(v) for v in inputs], outs,
        flops=rows * chip_len * mine * m * 6,
    )


def grads_one_kernel(info, go, go_got, out_weight, att, den, fq, idc, idr):
    rows, length, width = go.shape
    heads, m = fq.shape[1], fq.shape[3]
    mine = width // 2
    e = mine // heads
    n = heads // 2 * e + 8
    spare = heads // 2 * e + heads // 2

    def kernel(info_ref, go_r, gog_r, wo_r, att_r, den_r, fq_r, idc_r, idr_r, dn_o, dd_o, keep, send):
        chip = jnp.concatenate([go_r[0], gog_r[0].astype(BF)], 0)
        pulls = mm_nt(chip, wo_r[...])
        lead, tail, first, last = edges(idc_r, idr_r)
        lead, tail = lead.astype(F32), tail.astype(F32)
        lane = lax.broadcasted_iota(jnp.int32, (2 * length, 128), 1)
        dds = jnp.zeros((2 * length, 128), F32)
        for h in range(heads):
            cut = slice(h * e, (h + 1) * e)
            denom = den_r[0, :, h : h + 1]
            pull = pulls[:, cut]
            dn = (pull / denom).astype(BF)
            dn_o[0, :, cut] = dn
            dd = -jnp.sum(pull * att_r[0, :, cut], -1, keepdims=True) / denom
            dds = jnp.where(lane == h, dd, dds)
            wide = dn.astype(F32)
            sums = mm_tn(jnp.concatenate([wide * lead, wide * tail], 1).astype(BF), fq_r[0, h])
            high = dd.astype(BF).astype(F32)
            low = dd - high
            four = jnp.concatenate([high * lead, low * lead, high * tail, low * tail], 1)
            zs = mm_tn(four.astype(BF), fq_r[0, h])
            put_edges(info_ref, keep, send, h, heads, sums, zs[0:1] + zs[1:2], zs[2:3] + zs[3:4])
        dd_o[0] = dds
        put_tags(keep, send, spare, first, last)

    outs = [
        shaped(rows, 2 * length, mine, dtype=BF),
        shaped(rows, 2 * length, 128),
        shaped(rows, 2, n, m),
        shaped(rows, 2, n, m),
    ]
    specs = [
        per_row(go), per_row(go_got),
        pl.BlockSpec((mine, width), lambda r, info: (info[0], 0)),
        per_row(att), per_row(den), per_row(fq), per_row(idc), per_row(idr),
    ]
    return row_call(
        kernel, "grads_one", info, [go, go_got, out_weight, att, den, fq, idc, idr], specs, outs,
        flops=rows * length * width * mine * 6,
    )


def pulled_back(grad_feat, feat, part, feats):
    e = feats.shape[0]
    weighted = grad_feat * feat.astype(F32)
    inner = (weighted * e ** (-0.25)).astype(BF)
    folded = jnp.sum(weighted, -1, keepdims=True) * e ** (-0.5)
    return (mm_nt(inner, feats) - part.astype(F32) * folded).astype(BF)


def grads_two_kernel(info, fq, fk, queries, values, dn, dd, features, own, got, idc, idr, deps=()):
    rows, heads, chip_len, m = fq.shape
    mine = queries.shape[2]
    e = mine // heads

    def kernel(
        info_ref, fq_r, fk_r, q_r, v_r, dn_r, dd_r, f_r, own_r, got_r, idc_r, idr_r, dq_o, dfk_o, dv_o
    ):
        same = idc_r[0] == idr_r[0]
        lead, tail, _, _ = edges(idc_r, idr_r)
        lead, tail = lead.astype(F32), tail.astype(F32)
        for h in range(heads):
            cut = slice(h * e, (h + 1) * e)
            feat_q, feat_k = fq_r[0, h], fk_r[0, h]
            part, value = dn_r[0, :, cut], v_r[0, :, cut]
            denom = dd_r[0, :, h : h + 1]
            scores = jnp.where(same, mm_nt(feat_q, feat_k), 0.0).astype(BF)
            pulls = jnp.where(same, mm_nt(part, value) + denom, 0.0).astype(BF)
            dv_o[0, :, cut] = mm_tn(scores, part)
            dfk_o[0, h] = mm_tn(pulls, feat_q)
            before, behind, zb, za = carry_of(info_ref, own_r, got_r, h, heads, e)
            wide = part.astype(F32)
            both = jnp.concatenate([wide * lead, wide * tail], 1).astype(BF)
            grad = (
                mm(pulls, feat_k)
                + mm(both, jnp.concatenate([before, behind], 0).astype(BF))
                + denom * (lead * zb + tail * za)
            )
            dq_o[0, :, cut] = pulled_back(grad, feat_q, q_r[0, :, cut], f_r[h])

    outs = [
        shaped(rows, chip_len, mine, dtype=BF),
        shaped(rows, heads, chip_len, m),
        shaped(rows, chip_len, mine),
    ]
    inputs = [fq, fk, queries, values, dn, dd, features, own, got, idc, idr]
    specs = [per_row(v) for v in inputs]
    specs[6] = head_features(features, heads)
    return row_call(
        kernel, "grads_two", info, inputs, specs, outs, deps, flops=rows * chip_len * chip_len * mine * 30
    )


def grads_three_kernel(info, fk, keys, values, dfk, dv, features, own, got, idc, idr, deps=()):
    rows, heads, chip_len, m = fk.shape
    mine = keys.shape[2]
    e = mine // heads

    def kernel(
        info_ref, fk_r, k_r, v_r, dfk_r, dv_r, f_r, own_r, got_r, idc_r, idr_r, dk_o, dv_o
    ):
        lead, tail, _, _ = edges(idc_r, idr_r)
        lead, tail = lead.astype(F32), tail.astype(F32)
        for h in range(heads):
            cut = slice(h * e, (h + 1) * e)
            feat = fk_r[0, h]
            before, behind, zb, za = carry_of(info_ref, own_r, got_r, h, heads, e)
            kv = jnp.concatenate([before, behind], 0).astype(BF)
            wide = v_r[0, :, cut].astype(F32)
            both = jnp.concatenate([wide * lead, wide * tail], 1).astype(BF)
            grad = dfk_r[0, h] + mm(both, kv) + (lead * zb + tail * za)
            dk_o[0, :, cut] = pulled_back(grad, feat, k_r[0, :, cut], f_r[h])
            more = mm_nt(feat, kv)
            total_v = dv_r[0, :, cut] + lead * more[:, :e] + tail * more[:, e:]
            dv_o[0, :, cut] = total_v.astype(BF)

    outs = [shaped(rows, chip_len, mine, dtype=BF), shaped(rows, chip_len, mine, dtype=BF)]
    inputs = [fk, keys, values, dfk, dv, features, own, got, idc, idr]
    specs = [per_row(v) for v in inputs]
    specs[5] = head_features(features, heads)
    return row_call(
        kernel, "grads_three", info, inputs, specs, outs, deps, flops=rows * chip_len * m * mine * 8
    )


def shares_kernel(info, dq, dk, dv, query_weight, key_weight, value_weight, deps=()):
    rows, chip_len, mine = dq.shape
    width = query_weight.shape[0]
    length = chip_len // 2

    def kernel(info_ref, dq_r, dk_r, dv_r, wq_r, wk_r, wv_r, here_o, send_o):
        total_x = (
            mm_nt(dq_r[0], wq_r[...]) + mm_nt(dk_r[0], wk_r[...]) + mm_nt(dv_r[0], wv_r[...])
        )
        here_o[0] = total_x[:length]
        send_o[0] = total_x[length:]

    outs = [shaped(rows, length, width), shaped(rows, length, width)]
    specs = [per_row(dq), per_row(dk), per_row(dv)] + [
        weight_columns(w, mine) for w in (query_weight, key_weight, value_weight)
    ]
    return row_call(
        kernel, "shares", info, [dq, dk, dv, query_weight, key_weight, value_weight], specs, outs, deps,
        flops=rows * chip_len * mine * width * 6,
    )


def norm(hidden):
    mean = jnp.mean(hidden, -1, keepdims=True)
    centered = hidden - mean
    variance = jnp.mean(centered * centered, -1, keepdims=True)
    inv_std = lax.rsqrt(variance + EPSILON)
    return centered * inv_std, inv_std


def norm_back(upstream, normed, inv_std, gain):
    scaled = upstream * gain
    return inv_std * (
        scaled
        - jnp.mean(scaled, -1, keepdims=True)
        - normed * jnp.mean(scaled * normed, -1, keepdims=True)
    )


def put_sums(ref, upstream, normed):
    ref[...] = jnp.zeros_like(ref)
    ref[0:1, :] = jnp.sum(upstream * normed, 0, keepdims=True)
    ref[1:2, :] = jnp.sum(upstream, 0, keepdims=True)


def ffn_chunk(j, info, chunks):
    return lax.rem(j + (1 - info[0]) * (chunks // 2), chunks)


def ffn_forward(info, x, att, att_got, out_weight, first, up, down, second, cot, chunks=2):
    count, width = x.shape
    mine = att.shape[1]
    ff = up.shape[1]
    size = ff // chunks
    half = chunks // 2

    def kernel(
        info_ref, x_r, att_r, attg_r, wo_r, wog_r, first_r, up_r, down_r, second_r, cot_r,
        y_o, ys_o, here_o, send_o, slope_o, out_o, dz_o, dzs_o, dh_o, unit_o, inv_o, sums_o, y_s, acc,
    ):
        j = pl.program_id(0)

        @pl.when(j == 0)
        def _():
            hidden = (
                x_r[...].astype(F32)
                + mm(att_r[...], wo_r[...])
                + mm(attg_r[...].astype(BF), wog_r[...])
            )
            normed, inv_std = norm(hidden)
            unit_o[...] = normed
            inv_o[...] = jnp.broadcast_to(inv_std, inv_o.shape)
            y = normed * first_r[0:1, :] + first_r[1:2, :]
            acc[...] = y
            y_s[...] = y.astype(BF)
            y_o[...] = y_s[...]
            ys_o[...] = y_s[...].astype(F32)

        inner = mm(y_s[...], up_r[...])
        bell = 0.5 * (1.0 + lax.erf(inner * 0.7071067811865476))
        slope_o[...] = bell + inner * (jnp.exp(-0.5 * inner * inner) * 0.3989422804014327)
        act = (inner * bell).astype(BF)

        @pl.when(j < half)
        def _():
            send_o[...] = act.astype(F32)

        @pl.when(j >= half)
        def _():
            here_o[...] = act

        acc[...] += mm(act, down_r[...])

        @pl.when(j == chunks - 1)
        def _():
            normed, inv_std = norm(acc[...])
            gain = second_r[0:1, :]
            out_o[...] = (normed * gain + second_r[1:2, :]).astype(BF)
            upstream = cot_r[...].astype(F32)
            put_sums(sums_o, upstream, normed)
            grad = norm_back(upstream, normed, inv_std, gain)
            dh_o[...] = grad
            dz_o[...] = grad.astype(BF)
            dzs_o[...] = grad.astype(BF).astype(F32)

    def whole(array):
        return pl.BlockSpec(array.shape, lambda j, info: (0, 0))

    flat = pl.BlockSpec((count, width), lambda j, info: (0, 0))
    outs = [
        (shaped(count, width, dtype=BF), flat),
        (shaped(count, width), flat),
        (shaped(count, ff // 2, dtype=BF), pl.BlockSpec((count, size), lambda j, info: (0, jnp.maximum(j - half, 0)))),
        (shaped(count, ff // 2), pl.BlockSpec((count, size), lambda j, info: (0, jnp.minimum(j, half - 1)))),
        (shaped(count, ff), pl.BlockSpec((count, size), lambda j, info: (0, j))),
        (shaped(count, width, dtype=BF), flat),
        (shaped(count, width, dtype=BF), flat),
        (shaped(count, width), flat),
        (shaped(count, width), flat),
        (shaped(count, width), flat),
        (shaped(count, 128), pl.BlockSpec((count, 128), lambda j, info: (0, 0))),
        (shaped(8, width), pl.BlockSpec((8, width), lambda j, info: (0, 0))),
    ]
    return pl.pallas_call(
        kernel,
        grid_spec=pltpu.PrefetchScalarGridSpec(
            num_scalar_prefetch=1,
            grid=(chunks,),
            in_specs=[
                whole(x), whole(att), whole(att_got),
                pl.BlockSpec((mine, width), lambda j, info: (info[0], 0)),
                pl.BlockSpec((mine, width), lambda j, info: (1 - info[0], 0)),
                whole(first),
                pl.BlockSpec((width, size), lambda j, info: (0, ffn_chunk(j, info, chunks))),
                pl.BlockSpec((size, width), lambda j, info: (ffn_chunk(j, info, chunks), 0)),
                whole(second), whole(cot),
            ],
            out_specs=[spec for _, spec in outs],
            scratch_shapes=[pltpu.VMEM((count, width), BF), pltpu.VMEM((count, width), F32)],
        ),
        out_shape=[shape for shape, _ in outs],
        compiler_params=pltpu.CompilerParams(vmem_limit_bytes=ROOM),
        cost_estimate=cost(15),
        name="ffn_forward",
    )(info, x, att, att_got, out_weight, out_weight, first, up, down, second, cot)


def ffn_inner(info, dz, down, slope, chunks=2):
    count, width = dz.shape
    ff = down.shape[0]
    size = ff // chunks
    half = chunks // 2

    def kernel(info_ref, dz_r, down_r, slope_r, here_o, send_o):
        j = pl.program_id(0)
        grad = (mm_nt(dz_r[...], down_r[...]) * slope_r[...]).astype(BF)

        @pl.when(j < half)
        def _():
            send_o[...] = grad.astype(F32)

        @pl.when(j >= half)
        def _():
            here_o[...] = grad

    return pl.pallas_call(
        kernel,
        grid_spec=pltpu.PrefetchScalarGridSpec(
            num_scalar_prefetch=1,
            grid=(chunks,),
            in_specs=[
                pl.BlockSpec((count, width), lambda j, info: (0, 0)),
                pl.BlockSpec((size, width), lambda j, info: (ffn_chunk(j, info, chunks), 0)),
                pl.BlockSpec((count, size), lambda j, info: (0, j)),
            ],
            out_specs=[
                pl.BlockSpec((count, size), lambda j, info: (0, jnp.maximum(j - half, 0))),
                pl.BlockSpec((count, size), lambda j, info: (0, jnp.minimum(j, half - 1))),
            ],
        ),
        out_shape=[shaped(count, ff // 2, dtype=BF), shaped(count, ff // 2)],
        compiler_params=pltpu.CompilerParams(vmem_limit_bytes=ROOM),
        cost_estimate=cost(8),
        name="ffn_inner",
    )(info, dz, down, slope)


def ffn_back(info, here, send, up, dh, unit, inv, first, deps=(), chunks=2):
    count, width = dh.shape
    ff = up.shape[1]
    size = ff // chunks
    half = chunks // 2

    def kernel(info_ref, here_r, send_r, up_r, dh_r, unit_r, inv_r, first_r, *rest):
        dh_o, go_o, gos_o, sums_o, acc = rest[len(deps) :]
        j = pl.program_id(0)

        @pl.when(j == 0)
        def _():
            acc[...] = dh_r[...]

        @pl.when(j < half)
        def _():
            acc[...] += mm_nt(send_r[...].astype(BF), up_r[...])

        @pl.when(j >= half)
        def _():
            acc[...] += mm_nt(here_r[...], up_r[...])

        @pl.when(j == chunks - 1)
        def _():
            upstream, normed = acc[...], unit_r[...]
            put_sums(sums_o, upstream, normed)
            grad = norm_back(upstream, normed, inv_r[:, 0:1], first_r[0:1, :])
            dh_o[...] = grad
            go_o[...] = grad.astype(BF)
            gos_o[...] = grad.astype(BF).astype(F32)

    def whole(array):
        return pl.BlockSpec(array.shape, lambda j, info: (0, 0))

    flat = pl.BlockSpec((count, width), lambda j, info: (0, 0))
    return pl.pallas_call(
        kernel,
        grid_spec=pltpu.PrefetchScalarGridSpec(
            num_scalar_prefetch=1,
            grid=(chunks,),
            in_specs=[
                pl.BlockSpec((count, size), lambda j, info: (0, jnp.maximum(j - half, 0))),
                pl.BlockSpec((count, size), lambda j, info: (0, jnp.minimum(j, half - 1))),
                pl.BlockSpec((width, size), lambda j, info: (0, ffn_chunk(j, info, chunks))),
                whole(dh), whole(unit), whole(inv), whole(first),
            ] + [ANY] * len(deps),
            out_specs=[flat, flat, flat, pl.BlockSpec((8, width), lambda j, info: (0, 0))],
            scratch_shapes=[pltpu.VMEM((count, width), F32)],
        ),
        out_shape=[
            shaped(count, width), shaped(count, width, dtype=BF), shaped(count, width), shaped(8, width)
        ],
        compiler_params=pltpu.CompilerParams(vmem_limit_bytes=ROOM),
        cost_estimate=cost(3),
        name="ffn_back",
    )(info, here, send, up, dh, unit, inv, first, *deps)


def tag_of(ref, k, spare):
    return ref[0, k, spare : spare + 1, 0:1]


def ordered(info_ref, mine, theirs):
    one = info_ref[1] == 1

    def chip(at, k):
        here = one if at else jnp.logical_not(one)
        return jnp.where(here, mine[0, k], theirs[0, k])

    return [[chip(at, k) for k in (0, 1)] for at in (0, 1)]


def join_plane(info, mine, theirs, spare, deps=()):
    rows, _, n, m = mine.shape

    def kernel(info_ref, mine_r, theirs_r, up_o, down_o):
        (lead0, tail0), (lead1, tail1) = ordered(info_ref, mine_r, theirs_r)

        def tag(part):
            return part[spare : spare + 1, 0:1]

        is_sum = lax.broadcasted_iota(jnp.int32, (n, m), 0) < spare
        up_o[0] = tail1 + jnp.where(is_sum & (tag(tail0) == tag(tail1)), tail0, 0.0)
        down_o[0] = lead0 + jnp.where(is_sum & (tag(lead1) == tag(lead0)), lead1, 0.0)

    outs = [shaped(rows, n, m), shaped(rows, n, m)]
    return row_call(kernel, "join_plane", info, [mine, theirs], [per_row(mine)] * 2, outs, deps)


def split_plane(info, mine, theirs, ups, downs, spare):
    rows, _, n, m = mine.shape
    steps = len(ups)

    def kernel(info_ref, mine_r, theirs_r, *refs):
        give_o, own_o = refs[2 * steps :]
        (lead0, tail0), (lead1, tail1) = ordered(info_ref, mine_r, theirs_r)

        def tag(part):
            return part[spare : spare + 1, 0:1]

        before = jnp.zeros((n, m), F32)
        behind = jnp.zeros((n, m), F32)
        for k in range(steps):
            up, down = refs[k][0], refs[steps + k][0]
            before = before + jnp.where(tag(up) == tag(lead0), up, 0.0)
            behind = behind + jnp.where(tag(down) == tag(tail1), down, 0.0)
        behind0 = jnp.where(tag(tail0) == tag(lead1), lead1, 0.0) + jnp.where(
            tag(tail0) == tag(tail1), behind, 0.0
        )
        before1 = jnp.where(tag(lead1) == tag(tail0), tail0, 0.0) + jnp.where(
            tag(lead1) == tag(lead0), before, 0.0
        )
        one = info_ref[1] == 1
        give_o[0, 0] = jnp.where(one, before, before1)
        give_o[0, 1] = jnp.where(one, behind0, behind)
        own_o[0, 0] = jnp.where(one, before1, before)
        own_o[0, 1] = jnp.where(one, behind, behind0)

    inputs = [mine, theirs, *ups, *downs]
    outs = [shaped(rows, 2, n, m), shaped(rows, 2, n, m)]
    return row_call(kernel, "split_plane", info, inputs, [per_row(v) for v in inputs], outs)


def exchange(net, info, keep, send, ids_row, chip_len, spare, late=()):
    if not net.fast:
        first, last = jnp.min(ids_row, 2), jnp.max(ids_row, 2)
        pay = jnp.stack([keep, send], 1)
        up, down = pay[:, :, 1], pay[:, :, 0]
        before = jnp.zeros_like(up)
        behind = jnp.zeros_like(up)
        for _ in range(min(net.n_seq // 2 - 1, -(-SEG_MOST // chip_len))):
            up, down = net.shift(up, 1), net.shift(down, -1)
            reached = up[:, 0, spare, 0:1] == first
            before = before + jnp.where(reached[:, :, None, None], up, 0.0)
            reached = down[:, 0, spare, 0:1] == last
            behind = behind + jnp.where(reached[:, :, None, None], down, 0.0)
        return jnp.stack([before[:, 0], behind[:, 0]], 1), jnp.stack([before[:, 1], behind[:, 1]], 1)
    theirs = net.over_x(send)
    up, down = join_plane(info, keep, theirs, spare, late[0] if late else ())
    ups, downs = [], []
    for _ in range(min(net.nz - 1, -(-SEG_MOST // (2 * chip_len)))):
        up, down = net.z_up(up), net.z_down(down)
        ups.append(up)
        downs.append(down)
    if late:
        late[1].extend([ups[0], downs[0]])
    give, own = split_plane(info, keep, theirs, ups, downs, spare)
    if late:
        late[2].append(own)
    return own, net.over_x(give)


def body(
    tokens,
    segment_ids,
    features,
    query_weight,
    key_weight,
    value_weight,
    out_weight,
    up_weight,
    down_weight,
    first_gain,
    first_bias,
    second_gain,
    second_bias,
    cotangent,
):
    net = Net(lax.axis_size("dp"), lax.axis_size("seq"))
    rows, length, width = tokens.shape
    heads_all, head_dim, _ = features.shape
    heads = heads_all // 2
    mine = width // 2
    ff = up_weight.shape[1]
    ff_half = ff // 2
    core = net.core
    fast = net.fast
    chip_len = 2 * length
    count = rows * length
    spare = heads // 2 * head_dim + heads // 2
    side = net.x if fast else jnp.zeros_like(core)
    info = jnp.stack([core, side]).astype(jnp.int32)

    tokens_got = net.over_core(tokens.astype(F32))
    ids = segment_ids.astype(F32)
    ids_chip = jnp.concatenate([ids, net.over_core(ids)], 1)
    idr, idc = ids_chip[:, None, :], ids_chip[:, :, None]

    keys, values, fk, keep, send = keys_kernel(
        info, tokens, tokens_got, key_weight, value_weight, features, idc, idr
    )
    queries, fq, num, den = queries_kernel(
        info, tokens, tokens_got, query_weight, features, fk, values, idc, idr
    )
    own, got = exchange(net, info, keep, send, idr, chip_len, spare)
    att, den, att_here, att_send = attend_kernel(info, fq, num, den, own, got, idc, idr)
    att_got = net.over_core(att_send).reshape(count, mine)

    flat = tokens.reshape(count, width)
    first = jnp.stack([first_gain, first_bias])
    second = jnp.stack([second_gain, second_bias])
    (
        y1, y1_send, act, act_send, slope, result, dz, dz_send, dh2, unit, inv, sums_two
    ) = ffn_forward(
        info, flat, att_here.reshape(count, mine), att_got, out_weight, first,
        up_weight, down_weight, second, cotangent.reshape(count, width),
    )
    y1_got = net.over_core(y1_send)
    act_got = net.over_core(act_send)
    dz_got = net.over_core(dz_send)
    df, df_send = ffn_inner(info, dz, down_weight, slope)
    df_got = net.over_core(df_send)

    one = jnp.where(net.seq < 0, 0.5, 1.0).astype(F32)

    def rounded(wide):
        return (wide * one).astype(BF)

    def both(a, b):
        return jnp.concatenate([a, rounded(b)], 0)

    deps = ()
    if fast:
        bits_mine, bits_other = stage_bits(net, 0), stage_bits(net, 0, 1 - core)
        down_parts = (act, act_got, dz, dz_got)
        up_parts = (y1, y1_got, df, df_got)
        f_sends = down_products(1 - bits_mine, *down_parts, deps=[df])
        f_sends = up_products(1 - bits_mine, *up_parts, f_sends, 6)
        deps = f_sends[1:]
    else:
        grad_up = total(net, mm_tn(both(y1, y1_got), both(df, df_got)), 1)
        grad_down = total(net, mm_tn(both(act, act_got), both(dz, dz_got)), 0)

    dh1, go, go_send, sums_one = ffn_back(
        info, df, df_send, up_weight, dh2, unit, inv, first, deps
    )
    go_got = net.over_core(go_send)
    dn, dd, keep_d, send_d = grads_one_kernel(
        info, go.reshape(rows, length, width), go_got.reshape(rows, length, width), out_weight,
        att, den, fq, idc, idr,
    )
    late = []
    if fast:
        f_gots = moves(net, f_sends, 0)
        f_keeps = down_products(bits_mine, *down_parts, deps=[go])
        f_keeps = up_products(bits_mine, *up_parts, f_keeps, 1)
        f_sends, f_keeps = add_stage(net, f_keeps, f_gots, 1, [send_d])
        late = [[f_sends[1]], [], []]
    own_d, got_d = exchange(net, info, keep_d, send_d, idr, chip_len, spare, late)
    dq, dfk, dv = grads_two_kernel(
        info, fq, fk, queries, values, dn, dd, features, own, got, idc, idr, deps=late[2] if fast else ()
    )
    if fast:
        f_gots = [
            stage_move(net, f_sends[0], 0, 1), stage_move(net, tie(f_sends[1], *late[1]), 1, 1)
        ]
        f_sends, f_keeps = add_stage(net, f_keeps, f_gots, 2, [dq])
        f_gots = moves(net, f_sends, 2)
    dk, dv = grads_three_kernel(
        info, fk, keys, values, dfk, dv, features, own_d, got_d, idc, idr, deps=f_sends[1:] if fast else ()
    )

    chip_flat = (rows * chip_len, mine)
    if fast:
        sums = jnp.concatenate([sums_one[:2], sums_two[:2]])
        small = (sums + net.over_core(sums)).reshape(8, mine)
        attn_parts = (
            flat, tokens_got.reshape(count, width),
            dq.reshape(chip_flat), dk.reshape(chip_flat), dv.reshape(chip_flat),
            att.reshape(chip_flat), go, go_got, small,
        )

        def over_core(parts):
            return [net.over_core(part) for part in parts]

        a_sends = attn_products(1 - bits_mine, *attn_parts)
        a_gots = moves(net, a_sends, 0)
        a_keeps = attn_products(bits_mine, *attn_parts, deps=a_sends[1:])
        f_sends, f_keeps = add_stage(net, f_keeps, f_gots, 3, a_keeps[1:])
        f_gots = moves(net, f_sends, 3)
        f_own = last_add(f_keeps, f_gots)
        f_gots = moves(net, f_own, 3)
        a_sends, a_keeps = add_stage(net, a_keeps, a_gots, 1, f_own[1:])
        a_gots = moves(net, a_sends, 1)
        f_own = join_stage(net, f_own, f_gots, 3, a_sends[1:])
        f_gots = moves(net, f_own, 2)
        a_sends, a_keeps = add_stage(net, a_keeps, a_gots, 2, f_own[1:])
        a_gots = moves(net, a_sends, 2)
        f_one = join_stage(net, f_own, f_gots, 2, a_sends[1:])
        f_two = moves(net, f_one, 1)
        f_one_core = over_core(f_one)
        a_sends, a_keeps = add_stage(net, a_keeps, a_gots, 3, f_one[1:])
        a_gots = moves(net, a_sends, 3)
        a_own = last_add(a_keeps, a_gots)
        a_gots = moves(net, a_own, 3)
        shapes = [shaped(*w.shape) for w in (up_weight, down_weight)]
        copies = ffn_copies(width, ff_half)
        outs, done = place_pieces(
            net, [(f_one, 0, 0, 0), (f_one_core, 1, 0, 0)], shapes, copies, a_own[1:]
        )
        f_three = moves(net, [tie(part, a_own[1]) for part in f_one], 0)
        a_own = join_stage(net, a_own, a_gots, 3, done)
        a_gots = moves(net, a_own, 2)
        f_two_core = over_core(f_two)
        outs, done = place_pieces(
            net, [(f_two, 0, 0, 1), (f_two_core, 1, 0, 1)], outs, copies, a_own[1:]
        )
        f_four = moves(net, f_two, 0)
        a_one = join_stage(net, a_own, a_gots, 2, done)
        a_two = moves(net, a_one, 1)
        a_three = moves(net, a_one, 0)
        f_three_core = over_core(f_three)
        outs, done = place_pieces(
            net, [(f_three, 0, 1, 0), (f_three_core, 1, 1, 0)], outs, copies, a_one[1:]
        )
        here, share_send = shares_kernel(
            info, dq, dk, dv, query_weight, key_weight, value_weight, deps=done
        )
        a_four = moves(net, a_two, 0)
        f_four_core = over_core(f_four)
        a_one_core = over_core(a_one)
        (grad_up, grad_down), done = place_pieces(
            net, [(f_four, 0, 1, 1), (f_four_core, 1, 1, 1)], outs, copies, [share_send]
        )
        shapes = [shaped(width, width)] * 4
        copies = attn_copies(mine)
        a_two_core = over_core(a_two)
        outs, done = place_pieces(
            net,
            [(a_one, 0, 0, 0), (a_one_core, 1, 0, 0), (a_two, 0, 0, 1), (a_two_core, 1, 0, 1)],
            shapes, copies, done,
        )
        a_three_core = over_core(a_three)
        a_four = [tie(part, *done) for part in a_four]
        outs, done = place_pieces(
            net, [(a_three, 0, 1, 0), (a_three_core, 1, 1, 0), (a_four, 0, 1, 1)], outs, copies
        )
        (grad_query, grad_key, grad_value, grad_out), _ = place_pieces(
            net, [(over_core(a_four), 1, 1, 1)], outs, copies
        )
        rest_rows = mine // 3
        at = rest_rows - (rest_rows + SPARE_ROWS) // 2
        one, two = a_one[1][at : at + 8], a_two[1][at : at + 8]
        small = jnp.where(stage_bit(net, 1, 1, core) == 1, one, two).reshape(4, width)
    else:
        x_chip = jnp.concatenate([tokens, rounded(tokens_got)], 1).reshape(rows * chip_len, width)
        go_chip = jnp.concatenate(
            [go.reshape(rows, length, width), rounded(go_got).reshape(rows, length, width)], 1
        ).reshape(rows * chip_len, width)
        grad_query = total(net, mm_tn(x_chip, dq.reshape(chip_flat)), 1)
        grad_key = total(net, mm_tn(x_chip, dk.reshape(chip_flat)), 1)
        grad_value = total(net, mm_tn(x_chip, dv.reshape(chip_flat)), 1)
        grad_out = total(net, mm_tn(att.astype(BF).reshape(chip_flat), go_chip), 0)

        here, share_send = shares_kernel(info, dq, dk, dv, query_weight, key_weight, value_weight)
        small = lax.psum(jnp.concatenate([sums_one[:2], sums_two[:2]]), AXES)

    grad_input = dh1.reshape(rows, length, width) + here + net.over_core(share_send)
    return (
        result.reshape(rows, length, width),
        grad_input.astype(BF),
        grad_query,
        grad_key,
        grad_value,
        grad_out,
        grad_up,
        grad_down,
        small[0],
        small[1],
        small[2],
        small[3],
    )


def solution(mesh):
    split = P("dp", "seq", None)
    placed = (split, P("dp", "seq")) + (P(),) * 11 + (split,)
    return jax.shard_map(
        body,
        mesh=mesh,
        in_specs=placed,
        out_specs=(split, split) + (P(),) * 10,
        check_vma=False,
    )
```

profile of v0, /device:TPU:0, one launch (start us, length us, event | category | flops | bytes accessed | tf_op | source)
XLA Modules:
  0.0 419.3 jit_solution(2167364467493290471)
XLA Ops:
  9.2 6.4 %keys.1 = (bf16[1,512,384]{2,1,0:T(8,128)(2,1)S(1)}, bf16[1,512,384]{2,1,0:T(8,128)(2,1)S(1)}, bf16[1,6,512,256]{3,2,1,0:T(8,128)(2,1)S(1)}, f32[1,2,200,256]{3,2,1,0:T(8,128)S(1)}, f32[1,2,200,256]{3,2,1,0:T(8,128)S(1)}) custom-call(s32[2]{0:T(128)S(1)} %pad_add_fusion.info_ref, bf16[1,256,768]{2,1,0:T(8,128)(2,1)S(1)} %copy-done.2, ...), custom_call_target="tpu_custom_call" | custom-call | flops 10000000000 | bytes 1 | tf_op jit(solution)/shard_map/keys/pallas_call | solution.py:511
  18.5 9.8 %collective-permute-done.2.refs_1_ = f32[1,2,200,256]{3,2,1,0:T(8,128)S(1)} collective-permute-done((f32[1,2,200,256]{3,2,1,0:T(8,128)S(1)}, f32[1,2,200,256]{3,2,1,0:T(8,128)S(1)}, u32[]{:S(2)}, u32[]{:S(2)}) %collective-permute-start.2) | collective-permute-done | bytes 409632 | tf_op jit(solution)/shard_map/ppermute | solution.py:71
  36.5 4.4 %collective-permute-start.4 = (f32[1,200,256]{2,1,0:T(8,128)S(1)}, f32[1,200,256]{2,1,0:T(8,128)S(1)}, u32[]{:S(2)}, u32[]{:S(2)}) collective-permute-start(f32[1,200,256]{2,1,0:T(8,128)S(1)} %collective-permute-done.3.refs_2_), channel_id=1, source_target_pairs={{0,4},{1,5},{2,6},{3,7},{4,8},{5,9},{6,10},{7,11},{8,12},{9,13},{1... | collective-permute-start | bytes 614408 | tf_op jit(solution)/shard_map/ppermute | solution.py:71
  44.2 4.4 %collective-permute-done.6.refs_5_ = f32[1,200,256]{2,1,0:T(8,128)S(1)} collective-permute-done((f32[1,200,256]{2,1,0:T(8,128)S(1)}, f32[1,200,256]{2,1,0:T(8,128)S(1)}, u32[]{:S(2)}, u32[]{:S(2)}) %collective-permute-start.6) | collective-permute-done | bytes 204832 | tf_op jit(solution)/shard_map/ppermute | solution.py:71
  51.0 5.0 %queries.1 = (bf16[1,512,384]{2,1,0:T(8,128)(2,1)S(1)}, bf16[1,6,512,256]{3,2,1,0:T(8,128)(2,1)S(1)}, f32[1,512,384]{2,1,0:T(8,128)S(1)}, f32[1,512,128]{2,1,0:T(8,128)S(1)}) custom-call(s32[2]{0:T(128)S(1)} %pad_add_fusion.info_ref, bf16[1,256,768]{2,1,0:T(8,128)(2,1)S(1)} %copy-done.3, f32[1,256,768]{2,1,0:T(8,128)S(1)} %collective-permute-done.refs_1_, ...), custom_call_target="tpu_custom_call" | custom-call | flops 8000000000 | bytes 1 | tf_op jit(solution)/shard_map/queries/pallas_call | solution.py:511
  64.1 8.5 %ffn_forward.1 = (bf16[256,768]{1,0:T(8,128)(2,1)S(1)}, f32[256,768]{1,0:T(8,128)S(1)}, bf16[256,1536]{1,0:T(8,128)(2,1)S(1)}, f32[256,1536]{1,0:T(8,128)}, f32[...) custom-call(s32[2]{0:T(128)S(1)} %pad_add_fusion.info_ref, ...), custom_call_target="tpu_custom_call" | custom-call | flops 15000000512 | bytes 1 | tf_op jit(solution)/shard_map/ffn_forward/pallas_call | solution.py:967
  79.8 4.4 %down_products.2 = (f32[1152,768]{1,0:T(8,128)}, f32[384,768]{1,0:T(8,128)S(1)}) custom-call(s32[2]{0:T(128)S(1)} %get-tuple-element.258.bits_ref, bf16[256,1536]{1,0:T(8,128)(2,1)S(1)} %copy-done.89, f32[256,1536]{1,0:T(8,128)} %collective-permute-done.11.a0o.a1o, bf16[256,1536]{1,0:T(8,128)(2,1)S(1)} %copy-done.89, ...), custom_call_target="tpu_custom_call" | custom-call | flops 12000000000 | bytes 1 | tf_op jit(solution)/shard_map/down_products/pallas_call | solution.py:269
  111.1 6.4 %grads_one.1 = (bf16[1,512,384]{2,1,0:T(8,128)(2,1)S(1)}, f32[1,512,128]{2,1,0:T(8,128)S(1)}, f32[1,2,200,256]{3,2,1,0:T(8,128)S(1)}, f32[1,2,200,256]{3,2,1,0:T(8,128)S(1)}) custom-call(s32[2]{0:T(128)S(1)} %copy-done.46, bf16[1,256,768]{2,1,0:T(8,128)(2,1)S(1)} %bitcast.103, f32[1,256,768]{2,1,0:T(8,128)S(1)} %bitcast.84, bf16[768,768]{1,0:T(8,128)(2,1)S(1)} %copy-done.13, ...), custom_call_target="tpu_custom_call" | custom-call | flops 3000000000 | bytes 1 | tf_op jit(solution)/shard_map/grads_one/pallas_call | solution.py:511
  120.1 14.5 %collective-permute-done.15.refs_1_.refs_5_ = f32[1152,768]{1,0:T(8,128)} collective-permute-done((f32[1152,768]{1,0:T(8,128)}, f32[1152,768]{1,0:T(8,128)}, u32[]{:S(2)}, u32[]{:S(2)}) %collective-permute-start.15) | collective-permute-done | bytes 3538976 | tf_op jit(solution)/shard_map/ppermute | solution.py:71
  146.9 4.4 %collective-permute-start.18 = (f32[1,200,256]{2,1,0:T(8,128)S(1)}, f32[1,200,256]{2,1,0:T(8,128)S(1)}, u32[]{:S(2)}, u32[]{:S(2)}) collective-permute-start(f32[1,200,256]{2,1,0:T(8,128)S(1)} %collective-permute-done.17.refs_2_.refs_1_), channel_id=1, source_target_pairs={{0,4},{1,5},{2,6},{3,7},{4,8},{5,9},{6,10},{7,11},{8,12},{9,13},{1... | collective-permute-start | bytes 614408 | tf_op jit(solution)/shard_map/ppermute | solution.py:71
  156.9 4.3 %collective-permute-done.20.refs_5_ = f32[1,200,256]{2,1,0:T(8,128)} collective-permute-done((f32[1,200,256]{2,1,0:T(8,128)S(1)}, f32[1,200,256]{2,1,0:T(8,128)}, u32[]{:S(2)}, u32[]{:S(2)}) %collective-permute-start.20) | collective-permute-done | bytes 204832 | tf_op jit(solution)/shard_map/ppermute | solution.py:71
  165.6 8.4 %grads_two.1 = (bf16[1,512,384]{2,1,0:T(8,128)(2,1)S(1)}, f32[1,6,512,256]{3,2,1,0:T(8,128)S(1)}, f32[1,512,384]{2,1,0:T(8,128)S(1)}) custom-call(s32[2]{0:T(128)S(1)} %copy-done.47, bf16[1,6,512,256]{3,2,1,0:T(8,128)(2,1)S(1)} %copy-done.60, bf16[1,6,512,256]{3,2,1,0:T(8,128)(2,1)S(1)} %copy-done.72, bf16[1,512,384]{2,1,0:T(8,128)(2,1)S(1)} %copy-done.87, ...), custom_call_target="tpu_custom_call" | custom-call | flops 12000000000 | bytes 1 | tf_op jit(solution)/shard_map/grads_two/pallas_call | solution.py:511
  186.8 11.1 %collective-permute-done.24.refs_1_.refs_5_ = f32[288,768]{1,0:T(8,128)S(1)} collective-permute-done((f32[288,768]{1,0:T(8,128)S(1)}, f32[288,768]{1,0:T(8,128)S(1)}, u32[]{:S(2)}, u32[]{:S(2)}) %collective-permute-start.24) | collective-permute-done | bytes 884768 | tf_op jit(solution)/shard_map/ppermute | solution.py:71
  203.7 4.8 %collective-permute-done.28.refs_3_ = f32[48,768]{1,0:T(8,128)S(1)} collective-permute-done((f32[48,768]{1,0:T(8,128)S(1)}, f32[48,768]{1,0:T(8,128)S(1)}, u32[]{:S(2)}, u32[]{:S(2)}) %collective-permute-start.28) | collective-permute-done | bytes 147488 | tf_op jit(solution)/shard_map/ppermute | solution.py:71
  208.4 9.1 %collective-permute-done.27.refs_2_ = f32[144,768]{1,0:T(8,128)S(1)} collective-permute-done((f32[144,768]{1,0:T(8,128)S(1)}, f32[144,768]{1,0:T(8,128)S(1)}, u32[]{:S(2)}, u32[]{:S(2)}) %collective-permute-start.27) | collective-permute-done | bytes 442400 | tf_op jit(solution)/shard_map/ppermute | solution.py:71
  223.6 12.2 %collective-permute-done.30.refs_3_ = f32[48,768]{1,0:T(8,128)S(1)} collective-permute-done((f32[48,768]{1,0:T(8,128)S(1)}, f32[48,768]{1,0:T(8,128)S(1)}, u32[]{:S(2)}, u32[]{:S(2)}) %collective-permute-start.30) | collective-permute-done | bytes 147488 | tf_op jit(solution)/shard_map/ppermute | solution.py:71
  235.9 15.6 %collective-permute-done.29.refs_1_ = f32[144,768]{1,0:T(8,128)S(1)} collective-permute-done((f32[144,768]{1,0:T(8,128)S(1)}, f32[144,768]{1,0:T(8,128)S(1)}, u32[]{:S(2)}, u32[]{:S(2)}) %collective-permute-start.29) | collective-permute-done | bytes 442400 | tf_op jit(solution)/shard_map/ppermute | solution.py:71
  259.0 15.1 %collective-permute-done.33.refs_1_ = f32[288,768]{1,0:T(8,128)S(1)} collective-permute-done((f32[288,768]{1,0:T(8,128)S(1)}, f32[288,768]{1,0:T(8,128)S(1)}, u32[]{:S(2)}, u32[]{:S(2)}) %collective-permute-start.33) | collective-permute-done | bytes 884768 | tf_op jit(solution)/shard_map/ppermute | solution.py:71
  283.6 14.9 %collective-permute-done.40.refs_3_ = f32[24,384]{1,0:T(8,128)} collective-permute-done((f32[24,384]{1,0:T(8,128)S(1)}, f32[24,384]{1,0:T(8,128)}, u32[]{:S(2)}, u32[]{:S(2)}) %collective-permute-start.40) | collective-permute-done | bytes 36896 | tf_op jit(solution)/shard_map/ppermute | solution.py:71
  301.2 5.0 %place_pieces.7 = (f32[768,3072]{1,0:T(8,128)}, f32[3072,768]{1,0:T(8,128)}, f32[8,128]{1,0:T(8,128)S(1)}) custom-call(s32[10]{0:T(128)S(1)} %stack.109.where_ref, f32[576,768]{1,0:T(8,128)S(1)} %bitcast.52, f32[192,768]{1,0:T(8,128)S(1)} %bitcast.56, f32[576,768]{1,0:T(8,128)} %collective-permute-done.49.refs_2_, ...), custom_call_target="tpu_custom_call" | custom-call | flops 13500000256 | bytes 1 | tf_op jit(solution)/shard_map/place_pieces/pallas_call | solution.py:412
  312.0 12.7 %collective-permute-done.46.refs_1_ = f32[192,768]{1,0:T(8,128)S(1)} collective-permute-done((f32[192,768]{1,0:T(8,128)S(1)}, f32[192,768]{1,0:T(8,128)S(1)}, u32[]{:S(2)}, u32[]{:S(2)}) %collective-permute-start.46) | collective-permute-done | bytes 589856 | tf_op jit(solution)/shard_map/ppermute | solution.py:71
  324.7 5.3 %collective-permute-done.51.refs_1_ = f32[176,384]{1,0:T(8,128)S(1)} collective-permute-done((f32[176,384]{1,0:T(8,128)S(1)}, f32[176,384]{1,0:T(8,128)S(1)}, u32[]{:S(2)}, u32[]{:S(2)}) %collective-permute-start.51) | collective-permute-done | bytes 270368 | tf_op jit(solution)/shard_map/ppermute | solution.py:71
  335.2 4.4 %place_pieces.8 = (f32[768,3072]{1,0:T(8,128)}, f32[3072,768]{1,0:T(8,128)}, f32[8,128]{1,0:T(8,128)S(1)}) custom-call(s32[10]{0:T(128)S(1)} %stack.108.where_ref, f32[576,768]{1,0:T(8,128)} %collective-permute-done.45.refs_0_, f32[192,768]{1,0:T(8,128)S(1)} %collective-permute-done.46.refs_1_, ...), custom_call_target="tpu_custom_call", output_to_operand_aliasing={{0}: (5, {}), {1}: (6, {})} | custom-call | flops 13500000256 | bytes 1 | tf_op jit(solution)/shard_map/place_pieces/pallas_call | solution.py:412
  340.0 10.1 %collective-permute-done.53.refs_1_ = f32[352,384]{1,0:T(8,128)S(1)} collective-permute-done((f32[352,384]{1,0:T(8,128)S(1)}, f32[352,384]{1,0:T(8,128)S(1)}, u32[]{:S(2)}, u32[]{:S(2)}) %collective-permute-start.53) | collective-permute-done | bytes 540704 | tf_op jit(solution)/shard_map/ppermute | solution.py:71
  352.2 11.4 %collective-permute-done.42.refs_1_ = f32[192,768]{1,0:T(8,128)} collective-permute-done((f32[192,768]{1,0:T(8,128)S(1)}, f32[192,768]{1,0:T(8,128)}, u32[]{:S(2)}, u32[]{:S(2)}) %collective-permute-start.42) | collective-permute-done | bytes 589856 | tf_op jit(solution)/shard_map/ppermute | solution.py:71
  363.6 8.8 %collective-permute-start.44 = (f32[192,768]{1,0:T(8,128)}, f32[192,768]{1,0:T(8,128)}, u32[]{:S(2)}, u32[]{:S(2)}) collective-permute-start(f32[192,768]{1,0:T(8,128)} %collective-permute-done.42.refs_1_), channel_id=1, source_target_pairs={{0,1},{1,0},{2,3},{3,2},{4,5},{5,4},{6,7},{7,6},{8,9},{9,8},{10,11... | collective-permute-start | bytes 1769480 | tf_op jit(solution)/shard_map/ppermute | solution.py:71
  377.7 4.7 %place_pieces.9 = (f32[768,3072]{1,0:T(8,128)}, f32[3072,768]{1,0:T(8,128)}, f32[8,128]{1,0:T(8,128)S(1)}) custom-call(s32[10]{0:T(128)S(1)} %stack.99.where_ref, f32[576,768]{1,0:T(8,128)} %collective-permute-done.41.refs_0_, f32[192,768]{1,0:T(8,128)} %collective-permute-done.42.refs_1_, ...), custom_call_target="tpu_custom_call", output_to_operand_aliasing={{0}: (5, {}), {1}: (6, {})} | custom-call | flops 13500000256 | bytes 1 | tf_op jit(solution)/shard_map/place_pieces/pallas_call | solution.py:412
  389.1 4.4 %place_pieces.10 = (f32[768,3072]{1,0:T(8,128)}, f32[3072,768]{1,0:T(8,128)}, f32[8,128]{1,0:T(8,128)S(1)}) custom-call(s32[10]{0:T(128)S(1)} %stack.112.where_ref, f32[576,768]{1,0:T(8,128)} %collective-permute-done.63.refs_0_, f32[192,768]{1,0:T(8,128)} %collective-permute-done.64.refs_1_, ...), custom_call_target="tpu_custom_call", output_to_operand_aliasing={{0}: (5, {}), {1}: (6, {})} | custom-call | flops 13500000256 | bytes 1 | tf_op jit(solution)/shard_map/place_pieces/pallas_call | solution.py:412
  395.2 4.5 %collective-permute-done.70.refs_0_ = f32[704,384]{1,0:T(8,128)S(1)} collective-permute-done((f32[704,384]{1,0:T(8,128)S(1)}, f32[704,384]{1,0:T(8,128)S(1)}, u32[]{:S(2)}, u32[]{:S(2)}) %collective-permute-start.70) | collective-permute-done | bytes 1081376 | tf_op jit(solution)/shard_map/ppermute | solution.py:71
  400.3 4.4 %place_pieces.11 = (f32[768,768]{1,0:T(8,128)}, f32[768,768]{1,0:T(8,128)}, f32[768,768]{1,0:T(8,128)}, f32[768,768]{1,0:T(8,128)}, f32[8,128]{1,0:T(8,128)S(1)}) custom-call(s32[20]{0:T(128)S(1)} %stack.111.where_ref, f32[704,384]{1,0:T(8,128)S(1)} %bitcast.77, f32[96,384]{1,0:T(8,128)S(1)} %bitcast.69, f32[704,384]{1,0:T(8,128)S(1)} %collective-permute-done.58.refs_2_, ...), custom_call_target="tpu_custom_call" | custom-call | flops 13500000256 | bytes 1 | tf_op jit(solution)/shard_map/place_pieces/pallas_call | solution.py:412
  404.9 6.5 %collective-permute-done.57.refs_0_ = f32[704,384]{1,0:T(8,128)S(1)} collective-permute-done((f32[704,384]{1,0:T(8,128)S(1)}, f32[704,384]{1,0:T(8,128)S(1)}, u32[]{:S(2)}, u32[]{:S(2)}) %collective-permute-start.57) | collective-permute-done | bytes 1081376 | tf_op jit(solution)/shard_map/ppermute | solution.py:71
  411.4 4.2 %place_pieces.12 = (f32[768,768]{1,0:T(8,128)}, f32[768,768]{1,0:T(8,128)}, f32[768,768]{1,0:T(8,128)}, f32[768,768]{1,0:T(8,128)}, f32[8,128]{1,0:T(8,128)}) custom-call(s32[15]{0:T(128)S(1)} %stack.113.where_ref, f32[704,384]{1,0:T(8,128)S(1)} %collective-permute-done.70.refs_0_, ...), custom_call_target="tpu_custom_call", output_to_operand_aliasing={{0}: (7, {}), {1}: (8, {}), {2}: (9, {}), {3}: (10, {})} | custom-call | flops 13500000256 | bytes 1 | tf_op jit(solution)/shard_map/place_pieces/pallas_call | solution.py:412
  (397 shorter events, 166.4 us)
Async XLA Ops:
  88.5 46.2 %collective-permute-start.15 = (f32[1152,768]{1,0:T(8,128)}, f32[1152,768]{1,0:T(8,128)}, u32[]{:S(2)}, u32[]{:S(2)}) collective-permute-start(f32[1152,768]{1,0:T(8,128)} %get-tuple-element.177), channel_id=1, source_target_pairs={{0,2},{1,17},{2,0},{3,19},{4,6},{5,21},{6,4},{7,23},{8,10},{9,25},... | collective-permute-start | bytes 10616840 | tf_op jit(solution)/shard_map/ppermute | solution.py:71
  91.4 28.7 %collective-permute-start.16 = (f32[384,768]{1,0:T(8,128)}, f32[384,768]{1,0:T(8,128)S(1)}, u32[]{:S(2)}, u32[]{:S(2)}) collective-permute-start(f32[384,768]{1,0:T(8,128)} %copy-done.20), channel_id=1, source_target_pairs={{0,4},{1,9},{2,6},{3,11},{4,0},{5,13},{6,2},{7,15},{8,12},{9,1},{1... | collective-permute-start | bytes 3538952 | tf_op jit(solution)/shard_map/ppermute | solution.py:71
  117.5 21.8 %collective-permute-start.14 = (f32[1,2,200,256]{3,2,1,0:T(8,128)S(1)}, f32[1,2,200,256]{3,2,1,0:T(8,128)S(1)}, u32[]{:S(2)}, u32[]{:S(2)}) collective-permute-start(f32[1,2,200,256]{3,2,1,0:T(8,128)S(1)} %get-tuple-element.173.refs_8_), channel_id=1, source_target_pairs={{0,2},{1,3},{2,0},{3,1},{4,6},{5,7},{6,4},{7,5},{8,10},{9,11},{10,... | collective-permute-start | bytes 1228808 | tf_op jit(solution)/shard_map/ppermute | solution.py:71
  144.9 29.1 %collective-permute-start.22 = (f32[576,768]{1,0:T(8,128)S(1)}, f32[576,768]{1,0:T(8,128)}, u32[]{:S(2)}, u32[]{:S(2)}) collective-permute-start(f32[576,768]{1,0:T(8,128)S(1)} %get-tuple-element.189), channel_id=1, source_target_pairs={{0,16},{1,3},{2,18},{3,1},{4,20},{5,7},{6,22},{7,5},{8,24},{9,11},... | collective-permute-start | bytes 5308424 | tf_op jit(solution)/shard_map/ppermute | solution.py:71
  153.2 20.9 %collective-permute-start.23 = (f32[192,768]{1,0:T(8,128)S(1)}, f32[192,768]{1,0:T(8,128)S(1)}, u32[]{:S(2)}, u32[]{:S(2)}) collective-permute-start(f32[192,768]{1,0:T(8,128)S(1)} %tie.5), channel_id=1, source_target_pairs={{0,8},{1,5},{2,10},{3,7},{4,12},{5,1},{6,14},{7,3},{8,0},{9,13},{1... | collective-permute-start | bytes 1769480 | tf_op jit(solution)/shard_map/ppermute | solution.py:71
  176.4 21.5 %collective-permute-start.24 = (f32[288,768]{1,0:T(8,128)S(1)}, f32[288,768]{1,0:T(8,128)S(1)}, u32[]{:S(2)}, u32[]{:S(2)}) collective-permute-start(f32[288,768]{1,0:T(8,128)S(1)} %get-tuple-element.195), channel_id=1, source_target_pairs={{0,4},{1,9},{2,6},{3,11},{4,0},{5,13},{6,2},{7,15},{8,12},{9,1},{1... | collective-permute-start | bytes 2654216 | tf_op jit(solution)/shard_map/ppermute | solution.py:71
  184.1 33.6 %collective-permute-start.31 = (f32[1408,384]{1,0:T(8,128)S(1)}, f32[1408,384]{1,0:T(8,128)S(1)}, u32[]{:S(2)}, u32[]{:S(2)}) collective-permute-start(f32[1408,384]{1,0:T(8,128)S(1)} %get-tuple-element.208), channel_id=1, source_target_pairs={{0,2},{1,17},{2,0},{3,19},{4,6},{5,21},{6,4},{7,23},{8,10},{9,25},... | collective-permute-start | bytes 6488072 | tf_op jit(solution)/shard_map/ppermute | solution.py:71
  198.6 19.0 %collective-permute-start.27 = (f32[144,768]{1,0:T(8,128)S(1)}, f32[144,768]{1,0:T(8,128)S(1)}, u32[]{:S(2)}, u32[]{:S(2)}) collective-permute-start(f32[144,768]{1,0:T(8,128)S(1)} %get-tuple-element.203), channel_id=1, source_target_pairs={{0,8},{1,5},{2,10},{3,7},{4,12},{5,1},{6,14},{7,3},{8,0},{9,13},{1... | collective-permute-start | bytes 1327112 | tf_op jit(solution)/shard_map/ppermute | solution.py:71
  217.6 33.8 %collective-permute-start.29 = (f32[144,768]{1,0:T(8,128)S(1)}, f32[144,768]{1,0:T(8,128)S(1)}, u32[]{:S(2)}, u32[]{:S(2)}) collective-permute-start(f32[144,768]{1,0:T(8,128)S(1)} %get-tuple-element.205.refs_0_), channel_id=1, source_target_pairs={{0,8},{1,5},{2,10},{3,7},{4,12},{5,1},{6,14},{7,3},{8,0},{9,13},{1... | collective-permute-start | bytes 1327112 | tf_op jit(solution)/shard_map/ppermute | solution.py:71
  219.1 35.6 %collective-permute-start.35 = (f32[704,384]{1,0:T(8,128)S(1)}, f32[704,384]{1,0:T(8,128)S(1)}, u32[]{:S(2)}, u32[]{:S(2)}) collective-permute-start(f32[704,384]{1,0:T(8,128)S(1)} %get-tuple-element.213), channel_id=1, source_target_pairs={{0,16},{1,3},{2,18},{3,1},{4,20},{5,7},{6,22},{7,5},{8,24},{9,11},... | collective-permute-start | bytes 3244040 | tf_op jit(solution)/shard_map/ppermute | solution.py:71
  221.2 33.5 %collective-permute-start.36 = (f32[96,384]{1,0:T(8,128)S(1)}, f32[96,384]{1,0:T(8,128)S(1)}, u32[]{:S(2)}, u32[]{:S(2)}) collective-permute-start(f32[96,384]{1,0:T(8,128)S(1)} %get-tuple-element.209.refs_4_), channel_id=1, source_target_pairs={{0,8},{1,5},{2,10},{3,7},{4,12},{5,1},{6,14},{7,3},{8,0},{9,13},{1... | collective-permute-start | bytes 442376 | tf_op jit(solution)/shard_map/ppermute | solution.py:71
  252.1 22.0 %collective-permute-start.33 = (f32[288,768]{1,0:T(8,128)S(1)}, f32[288,768]{1,0:T(8,128)S(1)}, u32[]{:S(2)}, u32[]{:S(2)}) collective-permute-start(f32[288,768]{1,0:T(8,128)S(1)} %bitcast.78), channel_id=1, source_target_pairs={{0,4},{1,9},{2,6},{3,11},{4,0},{5,13},{6,2},{7,15},{8,12},{9,1},{1... | collective-permute-start | bytes 2654216 | tf_op jit(solution)/shard_map/ppermute | solution.py:71
  255.4 24.5 %collective-permute-start.37 = (f32[352,384]{1,0:T(8,128)S(1)}, f32[352,384]{1,0:T(8,128)S(1)}, u32[]{:S(2)}, u32[]{:S(2)}) collective-permute-start(f32[352,384]{1,0:T(8,128)S(1)} %get-tuple-element.218), channel_id=1, source_target_pairs={{0,4},{1,9},{2,6},{3,11},{4,0},{5,13},{6,2},{7,15},{8,12},{9,1},{1... | collective-permute-start | bytes 1622024 | tf_op jit(solution)/shard_map/ppermute | solution.py:71
  256.1 20.6 %collective-permute-start.38 = (f32[48,384]{1,0:T(8,128)S(1)}, f32[48,384]{1,0:T(8,128)S(1)}, u32[]{:S(2)}, u32[]{:S(2)}) collective-permute-start(f32[48,384]{1,0:T(8,128)S(1)} %get-tuple-element.215.refs_4_), channel_id=1, source_target_pairs={{0,2},{1,3},{2,0},{3,1},{4,6},{5,7},{6,4},{7,5},{8,10},{9,11},{10,... | collective-permute-start | bytes 221192 | tf_op jit(solution)/shard_map/ppermute | solution.py:71
  275.0 26.2 %collective-permute-start.49 = (f32[576,768]{1,0:T(8,128)S(1)}, f32[576,768]{1,0:T(8,128)}, u32[]{:S(2)}, u32[]{:S(2)}) collective-permute-start(f32[576,768]{1,0:T(8,128)S(1)} %bitcast.50), channel_id=1, source_target_pairs={{0,1},{1,0},{2,3},{3,2},{4,5},{5,4},{6,7},{7,6},{8,9},{9,8},{10,11... | collective-permute-start | bytes 5308424 | tf_op jit(solution)/shard_map/ppermute | solution.py:71
  275.1 26.0 %collective-permute-start.45 = (f32[576,768]{1,0:T(8,128)S(1)}, f32[576,768]{1,0:T(8,128)}, u32[]{:S(2)}, u32[]{:S(2)}) collective-permute-start(f32[576,768]{1,0:T(8,128)S(1)} %bitcast.51), channel_id=1, source_target_pairs={{0,16},{1,3},{2,18},{3,1},{4,20},{5,7},{6,22},{7,5},{8,24},{9,11},... | collective-permute-start | bytes 5308424 | tf_op jit(solution)/shard_map/ppermute | solution.py:71
  281.8 16.8 %collective-permute-start.39 = (f32[176,384]{1,0:T(8,128)S(1)}, f32[176,384]{1,0:T(8,128)S(1)}, u32[]{:S(2)}, u32[]{:S(2)}) collective-permute-start(f32[176,384]{1,0:T(8,128)S(1)} %get-tuple-element.223), channel_id=1, source_target_pairs={{0,8},{1,5},{2,10},{3,7},{4,12},{5,1},{6,14},{7,3},{8,0},{9,13},{1... | collective-permute-start | bytes 811016 | tf_op jit(solution)/shard_map/ppermute | solution.py:71
  281.8 19.3 %collective-permute-start.50 = (f32[192,768]{1,0:T(8,128)S(1)}, f32[192,768]{1,0:T(8,128)S(1)}, u32[]{:S(2)}, u32[]{:S(2)}) collective-permute-start(f32[192,768]{1,0:T(8,128)S(1)} %bitcast.55), channel_id=1, source_target_pairs={{0,1},{1,0},{2,3},{3,2},{4,5},{5,4},{6,7},{7,6},{8,9},{9,8},{10,11... | collective-permute-start | bytes 1769480 | tf_op jit(solution)/shard_map/ppermute | solution.py:71
  281.8 16.7 %collective-permute-start.40 = (f32[24,384]{1,0:T(8,128)S(1)}, f32[24,384]{1,0:T(8,128)}, u32[]{:S(2)}, u32[]{:S(2)}) collective-permute-start(f32[24,384]{1,0:T(8,128)S(1)} %get-tuple-element.224), channel_id=1, source_target_pairs={{0,16},{1,17},{2,18},{3,19},{4,20},{5,21},{6,22},{7,23},{8,24},{9,... | collective-permute-start | bytes 110600 | tf_op jit(solution)/shard_map/ppermute | solution.py:71
  301.1 31.1 %collective-permute-start.47 = (f32[576,768]{1,0:T(8,128)}, f32[576,768]{1,0:T(8,128)}, u32[]{:S(2)}, u32[]{:S(2)}) collective-permute-start(f32[576,768]{1,0:T(8,128)} %collective-permute-done.45.refs_0_), channel_id=1, source_target_pairs={{0,1},{1,0},{2,3},{3,2},{4,5},{5,4},{6,7},{7,6},{8,9},{9,8},{10,11... | collective-permute-start | bytes 5308424 | tf_op jit(solution)/shard_map/ppermute | solution.py:71
  306.2 27.4 %collective-permute-start.41 = (f32[576,768]{1,0:T(8,128)S(1)}, f32[576,768]{1,0:T(8,128)}, u32[]{:S(2)}, u32[]{:S(2)}) collective-permute-start(f32[576,768]{1,0:T(8,128)S(1)} %tie.6), channel_id=1, source_target_pairs={{0,2},{1,17},{2,0},{3,19},{4,6},{5,21},{6,4},{7,23},{8,10},{9,25},... | collective-permute-start | bytes 5308424 | tf_op jit(solution)/shard_map/ppermute | solution.py:71
  307.6 17.1 %collective-permute-start.46 = (f32[192,768]{1,0:T(8,128)S(1)}, f32[192,768]{1,0:T(8,128)S(1)}, u32[]{:S(2)}, u32[]{:S(2)}) collective-permute-start(f32[192,768]{1,0:T(8,128)S(1)} %bitcast.57), channel_id=1, source_target_pairs={{0,8},{1,5},{2,10},{3,7},{4,12},{5,1},{6,14},{7,3},{8,0},{9,13},{1... | collective-permute-start | bytes 1769480 | tf_op jit(solution)/shard_map/ppermute | solution.py:71
  307.6 22.4 %collective-permute-start.51 = (f32[176,384]{1,0:T(8,128)S(1)}, f32[176,384]{1,0:T(8,128)S(1)}, u32[]{:S(2)}, u32[]{:S(2)}) collective-permute-start(f32[176,384]{1,0:T(8,128)S(1)} %get-tuple-element.228.refs_0_), channel_id=1, source_target_pairs={{0,8},{1,5},{2,10},{3,7},{4,12},{5,1},{6,14},{7,3},{8,0},{9,13},{1... | collective-permute-start | bytes 811016 | tf_op jit(solution)/shard_map/ppermute | solution.py:71
  324.7 48.2 %collective-permute-start.64 = (f32[192,768]{1,0:T(8,128)S(1)}, f32[192,768]{1,0:T(8,128)}, u32[]{:S(2)}, u32[]{:S(2)}) collective-permute-start(f32[192,768]{1,0:T(8,128)S(1)} %collective-permute-done.46.refs_1_), channel_id=1, source_target_pairs={{0,4},{1,9},{2,6},{3,11},{4,0},{5,13},{6,2},{7,15},{8,12},{9,1},{1... | collective-permute-start | bytes 1769480 | tf_op jit(solution)/shard_map/ppermute | solution.py:71
  331.4 18.8 %collective-permute-start.53 = (f32[352,384]{1,0:T(8,128)S(1)}, f32[352,384]{1,0:T(8,128)S(1)}, u32[]{:S(2)}, u32[]{:S(2)}) collective-permute-start(f32[352,384]{1,0:T(8,128)S(1)} %bitcast.85), channel_id=1, source_target_pairs={{0,4},{1,9},{2,6},{3,11},{4,0},{5,13},{6,2},{7,15},{8,12},{9,1},{1... | collective-permute-start | bytes 1622024 | tf_op jit(solution)/shard_map/ppermute | solution.py:71
  332.2 44.9 %collective-permute-start.63 = (f32[576,768]{1,0:T(8,128)}, f32[576,768]{1,0:T(8,128)}, u32[]{:S(2)}, u32[]{:S(2)}) collective-permute-start(f32[576,768]{1,0:T(8,128)} %collective-permute-done.45.refs_0_), channel_id=1, source_target_pairs={{0,2},{1,17},{2,0},{3,19},{4,6},{5,21},{6,4},{7,23},{8,10},{9,25},... | collective-permute-start | bytes 5308424 | tf_op jit(solution)/shard_map/ppermute | solution.py:71
  333.6 44.0 %collective-permute-start.43 = (f32[576,768]{1,0:T(8,128)}, f32[576,768]{1,0:T(8,128)}, u32[]{:S(2)}, u32[]{:S(2)}) collective-permute-start(f32[576,768]{1,0:T(8,128)} %collective-permute-done.41.refs_0_), channel_id=1, source_target_pairs={{0,1},{1,0},{2,3},{3,2},{4,5},{5,4},{6,7},{7,6},{8,9},{9,8},{10,11... | collective-permute-start | bytes 5308424 | tf_op jit(solution)/shard_map/ppermute | solution.py:71
  339.7 23.9 %collective-permute-start.42 = (f32[192,768]{1,0:T(8,128)S(1)}, f32[192,768]{1,0:T(8,128)}, u32[]{:S(2)}, u32[]{:S(2)}) collective-permute-start(f32[192,768]{1,0:T(8,128)S(1)} %tie.7), channel_id=1, source_target_pairs={{0,4},{1,9},{2,6},{3,11},{4,0},{5,13},{6,2},{7,15},{8,12},{9,1},{1... | collective-permute-start | bytes 1769480 | tf_op jit(solution)/shard_map/ppermute | solution.py:71
  350.9 22.0 %collective-permute-start.60 = (f32[96,384]{1,0:T(8,128)S(1)}, f32[96,384]{1,0:T(8,128)S(1)}, u32[]{:S(2)}, u32[]{:S(2)}) collective-permute-start(f32[96,384]{1,0:T(8,128)S(1)} %bitcast.64), channel_id=1, source_target_pairs={{0,8},{1,5},{2,10},{3,7},{4,12},{5,1},{6,14},{7,3},{8,0},{9,13},{1... | collective-permute-start | bytes 442376 | tf_op jit(solution)/shard_map/ppermute | solution.py:71
  377.1 16.7 %collective-permute-start.58 = (f32[704,384]{1,0:T(8,128)S(1)}, f32[704,384]{1,0:T(8,128)S(1)}, u32[]{:S(2)}, u32[]{:S(2)}) collective-permute-start(f32[704,384]{1,0:T(8,128)S(1)} %bitcast.75), channel_id=1, source_target_pairs={{0,1},{1,0},{2,3},{3,2},{4,5},{5,4},{6,7},{7,6},{8,9},{9,8},{10,11... | collective-permute-start | bytes 3244040 | tf_op jit(solution)/shard_map/ppermute | solution.py:71
  393.7 17.8 %collective-permute-start.73 = (f32[96,384]{1,0:T(8,128)S(1)}, f32[96,384]{1,0:T(8,128)S(1)}, u32[]{:S(2)}, u32[]{:S(2)}) collective-permute-start(f32[96,384]{1,0:T(8,128)S(1)} %collective-permute-done.71.refs_1_), channel_id=1, source_target_pairs={{0,1},{1,0},{2,3},{3,2},{4,5},{5,4},{6,7},{7,6},{8,9},{9,8},{10,11... | collective-permute-start | bytes 442376 | tf_op jit(solution)/shard_map/ppermute | solution.py:71
  393.7 17.6 %collective-permute-start.57 = (f32[704,384]{1,0:T(8,128)S(1)}, f32[704,384]{1,0:T(8,128)S(1)}, u32[]{:S(2)}, u32[]{:S(2)}) collective-permute-start(f32[704,384]{1,0:T(8,128)S(1)} %collective-permute-done.56.refs_4_), channel_id=1, source_target_pairs={{0,2},{1,17},{2,0},{3,19},{4,6},{5,21},{6,4},{7,23},{8,10},{9,25},... | collective-permute-start | bytes 3244040 | tf_op jit(solution)/shard_map/ppermute | solution.py:71
  (143 other events, 1245.5 us)
where the time goes:
time: 425 us; the launch traced here: 419 us
  waiting for transfers between devices  185 us (44%)
  Pallas kernels  115 us (27%)
  starting transfers between devices  85.9 us (20%)
  local copies, waits for them, and re-layouts  27.1 us (6%)
    ppermute x74, waiting for transfers between devices, send(): return lax.ppermute(value, AXES, self.perm(move))  185 us
    ppermute x74, starting transfers between devices, send(): return lax.ppermute(value, AXES, self.perm(move))  85.9 us
    pallas_call x11, Pallas kernels, row_call(): pl.pallas_call(run, grid_spec=pltpu.PrefetchScalarGridSpec(num_scalar_pre...  39 us
    pallas_call x7, Pallas kernels, place_pieces(): pl.pallas_call(kernel, grid_spec=pltpu.PrefetchScalarGridSpec(num_scalar_...  29.7 us
    unnamed x202, local copies, waits for them, and re-layouts  23.2 us
    pallas_call x6, Pallas kernels, add_stage(): pl.pallas_call(kernel, grid_spec=pltpu.PrefetchScalarGridSpec(num_scalar_...  8.62 us
  transfers between devices with their start and end apart: 74, of which 28 were waited for; matrix products, arithmetic and copies ran while one was open for 2% of the time, Pallas kernels for 21%

commit v1 on v0

--- a/solution.py
+++ b/solution.py
@@ -6,7 +6,7 @@
 from jax.sharding import PartitionSpec as P
 
 SEG_MOST = 2048
-SPARE_ROWS = 64
+SPARE_ROWS = 128
 EPSILON = 1e-06
 AXES = ("dp", "seq")
 BF = jnp.bfloat16
@@ -17,10 +17,18 @@
 SMALL = 14 << 20
 
 
-SCALE = 3
-
-
-def cost(us):
+COSTS = {
+    "tie": 0.1, "add_stage": 12, "last_add": 4.5, "join_stage": 9, "down_products": 12, "up_products 1": 6,
+    "up_products 2": 1, "attn_products": 12, "place_pieces": 13.5, "ffn_forward": 15, "ffn_inner": 8,
+    "ffn_back": 3, "keys": 10, "queries": 8, "attend": 6, "grads_one": 3, "grads_two": 12, "grads_three": 8,
+    "shares": 9, "join_plane": 3, "split_plane": 3,
+}
+CALLS = {}
+
+
+def cost(name):
+    CALLS[name] = CALLS.get(name, 0) + 1
+    us = COSTS.get(f"{name} {CALLS[name]}", COSTS.get(name))
     return pl.CostEstimate(flops=int(us * 1e9), bytes_accessed=1, transcendentals=0)
 
 
@@ -126,7 +134,7 @@
         out_shape=jax.ShapeDtypeStruct(value.shape, value.dtype),
         input_output_aliases={0: 0},
         compiler_params=pltpu.CompilerParams(vmem_limit_bytes=SMALL),
-        cost_estimate=cost(0.1),
+        cost_estimate=cost("tie"),
         name="tie",
     )(value, *deps)
 
@@ -135,17 +143,17 @@
     return [stage_move(net, part, i, stage) for i, part in enumerate(parts)]
 
 
-def stage_bits(net, stage, core=None):
-    core = net.core if core is None else core
-    return jnp.stack([stage_bit(net, i, stage, core) for i in range(2)]).astype(jnp.int32)
+def stage_bits(net, stage, count=2):
+    return jnp.stack([stage_bit(net, i, stage, net.core) for i in range(count)]).astype(jnp.int32)
 
 
 def add_stage(net, keeps, gots, stage, deps=()):
-    steps = max(1, keeps[0].shape[0] // 288)
+    rows, count = keeps[0].shape[0], len(keeps)
+    steps = 4 if rows >= 1152 else 2 if rows >= 512 else 1
 
     def kernel(bits_ref, *refs):
-        outs = refs[8 + len(deps) :]
-        for i in range(4):
+        outs = refs[4 * count + len(deps) :]
+        for i in range(2 * count):
             outs[i][...] = refs[2 * i][...] + refs[2 * i + 1][...]
 
     in_specs, inputs, out_specs, shapes = [], [], [], []
@@ -172,36 +180,39 @@
         ),
         out_shape=shapes,
         compiler_params=pltpu.CompilerParams(vmem_limit_bytes=SMALL),
-        cost_estimate=cost(4 * SCALE),
+        cost_estimate=cost("add_stage"),
         name="add_stage",
-    )(stage_bits(net, stage), *inputs, *deps)
-    return outs[:2], outs[2:]
+    )(stage_bits(net, stage, count), *inputs, *deps)
+    return outs[:count], outs[count:]
 
 
 def last_add(keeps, gots, deps=()):
+    count = len(keeps)
+
     def kernel(*refs):
-        outs = refs[4 + len(deps) :]
-        for i in range(2):
-            outs[i][...] = refs[i][...] + refs[2 + i][...]
+        outs = refs[2 * count + len(deps) :]
+        for i in range(count):
+            outs[i][...] = refs[i][...] + refs[count + i][...]
 
     whole = pl.BlockSpec(memory_space=pltpu.VMEM)
     return pl.pallas_call(
         kernel,
-        in_specs=[whole] * 4 + [ANY] * len(deps),
-        out_specs=[whole] * 2,
+        in_specs=[whole] * (2 * count) + [ANY] * len(deps),
+        out_specs=[whole] * count,
         out_shape=[shaped(*k.shape) for k in keeps],
         compiler_params=pltpu.CompilerParams(vmem_limit_bytes=SMALL),
-        cost_estimate=cost(1.5 * SCALE),
+        cost_estimate=cost("last_add"),
         name="last_add",
     )(*keeps, *gots, *deps)
 
 
 def join_stage(net, parts, gots, stage, deps=()):
     steps = max(1, parts[0].shape[0] // 144)
+    count = len(parts)
 
     def kernel(bits_ref, *refs):
-        outs = refs[4 + len(deps) :]
-        for i in range(2):
+        outs = refs[2 * count + len(deps) :]
+        for i in range(count):
             bit = bits_ref[i]
             outs[i][pl.ds(bit, 1)] = refs[2 * i][...][None]
             outs[i][pl.ds(1 - bit, 1)] = refs[2 * i + 1][...][None]
@@ -223,9 +234,9 @@
         ),
         out_shape=shapes,
         compiler_params=pltpu.CompilerParams(vmem_limit_bytes=SMALL),
-        cost_estimate=cost(3 * SCALE),
+        cost_estimate=cost("join_stage"),
         name="join_stage",
-    )(stage_bits(net, stage), *[v for pair in zip(parts, gots) for v in pair], *deps)
+    )(stage_bits(net, stage, count), *[v for pair in zip(parts, gots) for v in pair], *deps)
     return [out.reshape(2 * out.shape[1], out.shape[2]) for out in outs]
 
 
@@ -281,12 +292,12 @@
         ),
         out_shape=[shaped(2 * up_rows + sizes[0], width), shaped(up_rows + sizes[1], width)],
         compiler_params=pltpu.CompilerParams(vmem_limit_bytes=ROOM),
-        cost_estimate=cost(4 * SCALE),
+        cost_estimate=cost("down_products"),
         name="down_products",
     )(bits, act, act_other, act, act_other, gz, gz_other, *deps)
 
 
-def up_products(bits, y1, y1_other, gi, gi_other, outs, big):
+def up_products(bits, y1, y1_other, gi, gi_other, outs):
     count, width = y1.shape
     u = width // 6
     parts = gi.shape[1] // width
@@ -320,7 +331,7 @@
         out_shape=[shaped(*o.shape) for o in outs],
         input_output_aliases={5: 0, 6: 1},
         compiler_params=pltpu.CompilerParams(vmem_limit_bytes=ROOM),
-        cost_estimate=cost(big),
+        cost_estimate=cost("up_products"),
         name="up_products",
     )(bits, y1, y1_other, gi, gi_other, *outs)
 
@@ -328,73 +339,67 @@
 def attn_products(bits, x, x_other, dq, dk, dv, attn, go, go_other, small, deps=()):
     count, width = x.shape
     mine = attn.shape[1]
-    cut = 2 * mine // 3
-
-    def kernel(
-        bits_ref, x0, x0o, x1, x1o, dq_r, dk_r, dv_r, attn_r, go_r, goo_r, small_r, *rest
-    ):
-        one, two = rest[len(deps) :]
-        x, xo = x0[...], x0o[...].astype(BF)
-        one[:mine, :] = tn(x, xo, dq_r[:count], dq_r[count:])
-        one[mine : 2 * mine, :] = tn(x, xo, dk_r[:count], dk_r[count:])
+
+    def kernel(bits_ref, x_r, xo_r, dq_r, dk_r, dv_r, attn_r, go_r, goo_r, small_r, *rest):
+        (out,) = rest[len(deps) :]
+        x, xo = x_r[...], xo_r[...].astype(BF)
+        for k, grad in enumerate((dq_r, dk_r, dv_r)):
+            out[k * mine : (k + 1) * mine, :] = tn(x, xo, grad[:count], grad[count:])
         part = attn_r[...].astype(BF)
-        one[2 * mine : 3 * mine, :] = tn(part[:count], part[count:], go_r[...], goo_r[...])
-        one[3 * mine :, :] = tn(x[:, :cut], xo[:, :cut], dv_r[:count], dv_r[count:])
-        rest_rows = mine - cut
-        two[:rest_rows, :] = tn(x1[:, cut:], x1o[:, cut:], dv_r[:count], dv_r[count:])
-        two[rest_rows:, :] = jnp.zeros((SPARE_ROWS, mine), F32)
-        two[rest_rows : rest_rows + 8, :] = small_r[...]
-
-    first = picked_columns(count, mine, lambda bits: bits[0])
-    second = picked_columns(count, mine, lambda bits: bits[1])
-    return pl.pallas_call(
+        out[3 * mine : 4 * mine, :] = tn(part[:count], part[count:], go_r[...], goo_r[...])
+        out[4 * mine :, :] = jnp.zeros((SPARE_ROWS, mine), F32)
+        out[4 * mine : 4 * mine + 8, :] = small_r[...]
+
+    half = picked_columns(count, mine, lambda bits: bits[0])
+    rows = 4 * mine + SPARE_ROWS
+    out = pl.pallas_call(
         kernel,
         grid_spec=pltpu.PrefetchScalarGridSpec(
             num_scalar_prefetch=1,
             grid=(1,),
-            in_specs=[first, first, second, second]
+            in_specs=[half, half]
             + [whole_of(v) for v in (dq, dk, dv, attn)]
-            + [first, first, whole_of(small)]
+            + [half, half, whole_of(small)]
             + [ANY] * len(deps),
-            out_specs=[
-                pl.BlockSpec((3 * mine + cut, mine), lambda g, bits: (0, 0)),
-                pl.BlockSpec((mine - cut + SPARE_ROWS, mine), lambda g, bits: (0, 0)),
-            ],
+            out_specs=pl.BlockSpec((rows, mine), lambda g, bits: (0, 0)),
         ),
-        out_shape=[shaped(3 * mine + cut, mine), shaped(mine - cut + SPARE_ROWS, mine)],
+        out_shape=shaped(rows, mine),
         compiler_params=pltpu.CompilerParams(vmem_limit_bytes=ROOM),
-        cost_estimate=cost(4 * SCALE),
+        cost_estimate=cost("attn_products"),
         name="attn_products",
-    )(bits, x, x_other, x, x_other, dq, dk, dv, attn, go, go_other, small, *deps)
+    )(bits, x, x_other, dq, dk, dv, attn, go, go_other, small, *deps)
+    return [out]
 
 
 def place_pieces(net, pieces, outs, copies, deps=()):
     fresh = isinstance(outs[0], jax.ShapeDtypeStruct)
-    n_out, n = len(outs), len(pieces)
+    n_out, m = len(outs), len(pieces[0][0])
     inputs = [part for piece in pieces for part in piece[0]]
+    n = len(inputs)
     scalars = []
     for _, other_core, other_first, other_second in pieces:
         core = 1 - net.core if other_core else net.core
         scalars.append(core)
-        for i in range(2):
+        for i in range(m):
             for stage, flip in ((0, other_first), (1, other_second)):
                 bit = stage_bit(net, i, stage, core)
                 scalars.append(1 - bit if flip else bit)
     where = jnp.stack(scalars).astype(jnp.int32)
 
     def kernel(where_ref, *refs):
-        srcs = refs[: 2 * n]
-        dests = refs[-(2 * n + 3 + n_out) : -(2 * n + 3)]
-        refs[-(2 * n + 3)][...] = jnp.zeros((8, 128), F32)
-        held, (arrive, sems) = refs[-(2 * n + 2) : -2], refs[-2:]
-        loads = [pltpu.make_async_copy(srcs[j], held[j], arrive.at[j]) for j in range(2 * n)]
+        srcs = refs[: n]
+        dests = refs[-(n + 3 + n_out) : -(n + 3)]
+        refs[-(n + 3)][...] = jnp.zeros((8, 128), F32)
+        held, (arrive, sems) = refs[-(n + 2) : -2], refs[-2:]
+        loads = [pltpu.make_async_copy(srcs[j], held[j], arrive.at[j]) for j in range(n)]
         for load in loads:
             load.start()
 
         def each(j, act):
-            piece, i = j // 2, j % 2
-            core = where_ref[5 * piece]
-            first, second = where_ref[5 * piece + 1 + 2 * i], where_ref[5 * piece + 2 + 2 * i]
+            piece, i = j // m, j % m
+            core = where_ref[(1 + 2 * m) * piece]
+            at = (1 + 2 * m) * piece + 1 + 2 * i
+            first, second = where_ref[at], where_ref[at + 1]
             for quarter in (0, 1):
 
                 @pl.when(second == quarter)
@@ -402,10 +407,10 @@
                     for k, (src, dest) in enumerate(copies(i, quarter, core, first, held[j], dests)):
                         act(pltpu.make_async_copy(src, dest, sems.at[j, k]))
 
-        for j in range(2 * n):
+        for j in range(n):
             loads[j].wait()
             each(j, lambda copy: copy.start())
-        for j in range(2 * n):
+        for j in range(n):
             each(j, lambda copy: copy.wait())
 
     operands = inputs + ([] if fresh else list(outs)) + list(deps)
@@ -417,14 +422,14 @@
             in_specs=[ANY] * len(inputs) + [HBM] * (0 if fresh else n_out) + [ANY] * len(deps),
             out_specs=[HBM] * n_out + [pl.BlockSpec((8, 128), lambda g, where: (0, 0))],
             scratch_shapes=[pltpu.VMEM(part.shape, F32) for part in inputs] + [
-                pltpu.SemaphoreType.DMA((2 * n,)),
-                pltpu.SemaphoreType.DMA((2 * n, 6)),
+                pltpu.SemaphoreType.DMA((n,)),
+                pltpu.SemaphoreType.DMA((n, 6)),
             ],
         ),
         out_shape=[shaped(*o.shape) for o in outs] + [shaped(8, 128)],
-        input_output_aliases={} if fresh else {1 + 2 * n + i: i for i in range(n_out)},
+        input_output_aliases={} if fresh else {1 + n + i: i for i in range(n_out)},
         compiler_params=pltpu.CompilerParams(vmem_limit_bytes=ROOM),
-        cost_estimate=cost(4.5 * SCALE),
+        cost_estimate=cost("place_pieces"),
         name="place_pieces",
     )(where, *operands)
     return outs, [done]
@@ -470,14 +475,10 @@
     def copies(i, quarter, c, b, src, dests):
         own = pl.ds(pl.multiple_of(c * mine, 128), mine)
         half = pl.ds(pl.multiple_of(b * mine, 128), mine)
-        cut = 2 * mine // 3
-        sizes = [mine - cut] if i else [mine] * 3 + [cut]
         length = src.shape[0]
-        for k, row, at, n in spans(sizes, quarter * length, length):
-            if i:
-                dest = rows_at(dests[2], b * mine + cut + row, n, 8, own)
-            elif k != 2:
-                dest = rows_at(dests[min(k, 2)], b * mine + row, n, 8, own)
+        for k, row, at, n in spans([mine] * 4, quarter * length, length):
+            if k < 3:
+                dest = rows_at(dests[k], b * mine + row, n, 8, own)
             else:
                 dest = rows_at(dests[3], c * mine + row, n, 8, half)
             yield src.at[at : at + n], dest
@@ -495,9 +496,6 @@
 def per_row(array):
     rest = array.shape[1:]
     return pl.BlockSpec((1, *rest), lambda r, info: (r, *(0 for _ in rest)))
-
-
-COSTS = {"keys": 10, "queries": 8, "attend": 6, "grads_one": 3, "grads_two": 12, "grads_three": 8, "shares": 3 * SCALE, "join_plane": 3, "split_plane": 3}
 
 
 def row_call(kernel, name, info, inputs, in_specs, outs, deps=(), flops=0):
@@ -518,7 +516,7 @@
         ),
         out_shape=outs,
         compiler_params=pltpu.CompilerParams(vmem_limit_bytes=ROOM),
-        cost_estimate=cost(COSTS[name]),
+        cost_estimate=cost(name),
         name=name,
     )(info, *inputs, *deps)
 
@@ -983,7 +981,7 @@
         ),
         out_shape=[shape for shape, _ in outs],
         compiler_params=pltpu.CompilerParams(vmem_limit_bytes=ROOM),
-        cost_estimate=cost(15),
+        cost_estimate=cost("ffn_forward"),
         name="ffn_forward",
     )(info, x, att, att_got, out_weight, out_weight, first, up, down, second, cot)
 
@@ -1023,7 +1021,7 @@
         ),
         out_shape=[shaped(count, ff // 2, dtype=BF), shaped(count, ff // 2)],
         compiler_params=pltpu.CompilerParams(vmem_limit_bytes=ROOM),
-        cost_estimate=cost(8),
+        cost_estimate=cost("ffn_inner"),
         name="ffn_inner",
     )(info, dz, down, slope)
 
@@ -1081,7 +1079,7 @@
             shaped(count, width), shaped(count, width, dtype=BF), shaped(count, width), shaped(8, width)
         ],
         compiler_params=pltpu.CompilerParams(vmem_limit_bytes=ROOM),
-        cost_estimate=cost(3),
+        cost_estimate=cost("ffn_back"),
         name="ffn_back",
     )(info, here, send, up, dh, unit, inv, first, *deps)
 
@@ -1196,6 +1194,7 @@
     second_bias,
     cotangent,
 ):
+    CALLS.clear()
     net = Net(lax.axis_size("dp"), lax.axis_size("seq"))
     rows, length, width = tokens.shape
     heads_all, head_dim, _ = features.shape
@@ -1251,11 +1250,11 @@
 
     deps = ()
     if fast:
-        bits_mine, bits_other = stage_bits(net, 0), stage_bits(net, 0, 1 - core)
+        bits_mine = stage_bits(net, 0)
         down_parts = (act, act_got, dz, dz_got)
         up_parts = (y1, y1_got, df, df_got)
         f_sends = down_products(1 - bits_mine, *down_parts, deps=[df])
-        f_sends = up_products(1 - bits_mine, *up_parts, f_sends, 6)
+        f_sends = up_products(1 - bits_mine, *up_parts, f_sends)
         deps = f_sends[1:]
     else:
         grad_up = total(net, mm_tn(both(y1, y1_got), both(df, df_got)), 1)
@@ -1273,7 +1272,7 @@
     if fast:
         f_gots = moves(net, f_sends, 0)
         f_keeps = down_products(bits_mine, *down_parts, deps=[go])
-        f_keeps = up_products(bits_mine, *up_parts, f_keeps, 1)
+        f_keeps = up_products(bits_mine, *up_parts, f_keeps)
         f_sends, f_keeps = add_stage(net, f_keeps, f_gots, 1, [send_d])
         late = [[f_sends[1]], [], []]
     own_d, got_d = exchange(net, info, keep_d, send_d, idr, chip_len, spare, late)
@@ -1305,35 +1304,36 @@
 
         a_sends = attn_products(1 - bits_mine, *attn_parts)
         a_gots = moves(net, a_sends, 0)
-        a_keeps = attn_products(bits_mine, *attn_parts, deps=a_sends[1:])
-        f_sends, f_keeps = add_stage(net, f_keeps, f_gots, 3, a_keeps[1:])
+        a_keeps = attn_products(bits_mine, *attn_parts, deps=a_sends)
+        f_sends, f_keeps = add_stage(net, f_keeps, f_gots, 3, a_keeps)
         f_gots = moves(net, f_sends, 3)
         f_own = last_add(f_keeps, f_gots)
         f_gots = moves(net, f_own, 3)
+        f_own = join_stage(net, f_own, f_gots, 3)
+        f_gots = moves(net, f_own, 2)
         a_sends, a_keeps = add_stage(net, a_keeps, a_gots, 1, f_own[1:])
         a_gots = moves(net, a_sends, 1)
-        f_own = join_stage(net, f_own, f_gots, 3, a_sends[1:])
-        f_gots = moves(net, f_own, 2)
-        a_sends, a_keeps = add_stage(net, a_keeps, a_gots, 2, f_own[1:])
+        a_sends, a_keeps = add_stage(net, a_keeps, a_gots, 2)
         a_gots = moves(net, a_sends, 2)
-        f_one = join_stage(net, f_own, f_gots, 2, a_sends[1:])
+        f_one = join_stage(net, f_own, f_gots, 2, a_sends)
         f_two = moves(net, f_one, 1)
-        f_one_core = over_core(f_one)
         a_sends, a_keeps = add_stage(net, a_keeps, a_gots, 3, f_one[1:])
         a_gots = moves(net, a_sends, 3)
-        a_own = last_add(a_keeps, a_gots)
-        a_gots = moves(net, a_own, 3)
+        f_one_core = over_core([tie(part, *a_sends) for part in f_one])
         shapes = [shaped(*w.shape) for w in (up_weight, down_weight)]
         copies = ffn_copies(width, ff_half)
         outs, done = place_pieces(
-            net, [(f_one, 0, 0, 0), (f_one_core, 1, 0, 0)], shapes, copies, a_own[1:]
+            net, [(f_one, 0, 0, 0), (f_one_core, 1, 0, 0)], shapes, copies, a_sends
         )
-        f_three = moves(net, [tie(part, a_own[1]) for part in f_one], 0)
+        a_keeps = [tie(a_keeps[0], *f_two)]
+        a_own = last_add(a_keeps, a_gots, done)
+        a_gots = moves(net, a_own, 3)
+        f_three = moves(net, f_one, 0)
         a_own = join_stage(net, a_own, a_gots, 3, done)
         a_gots = moves(net, a_own, 2)
         f_two_core = over_core(f_two)
         outs, done = place_pieces(
-            net, [(f_two, 0, 0, 1), (f_two_core, 1, 0, 1)], outs, copies, a_own[1:]
+            net, [(f_two, 0, 0, 1), (f_two_core, 1, 0, 1)], outs, copies, a_own
         )
         f_four = moves(net, f_two, 0)
         a_one = join_stage(net, a_own, a_gots, 2, done)
@@ -1341,7 +1341,7 @@
         a_three = moves(net, a_one, 0)
         f_three_core = over_core(f_three)
         outs, done = place_pieces(
-            net, [(f_three, 0, 1, 0), (f_three_core, 1, 1, 0)], outs, copies, a_one[1:]
+            net, [(f_three, 0, 1, 0), (f_three_core, 1, 1, 0)], outs, copies, a_one
         )
         here, share_send = shares_kernel(
             info, dq, dk, dv, query_weight, key_weight, value_weight, deps=done
@@ -1361,17 +1361,17 @@
             shapes, copies, done,
         )
         a_three_core = over_core(a_three)
+        outs, done = place_pieces(
+            net, [(a_three, 0, 1, 0), (a_three_core, 1, 1, 0)], outs, copies, done
+        )
         a_four = [tie(part, *done) for part in a_four]
-        outs, done = place_pieces(
-            net, [(a_three, 0, 1, 0), (a_three_core, 1, 1, 0), (a_four, 0, 1, 1)], outs, copies
-        )
+        outs, done = place_pieces(net, [(a_four, 0, 1, 1)], outs, copies)
         (grad_query, grad_key, grad_value, grad_out), _ = place_pieces(
             net, [(over_core(a_four), 1, 1, 1)], outs, copies
         )
-        rest_rows = mine // 3
-        at = rest_rows - (rest_rows + SPARE_ROWS) // 2
-        one, two = a_one[1][at : at + 8], a_two[1][at : at + 8]
-        small = jnp.where(stage_bit(net, 1, 1, core) == 1, one, two).reshape(4, width)
+        at = 4 * mine - (4 * mine + SPARE_ROWS) // 2
+        one, two = a_one[0][at : at + 8], a_two[0][at : at + 8]
+        small = jnp.where(stage_bit(net, 0, 1, core) == 1, one, two).reshape(4, width)
     else:
         x_chip = jnp.concatenate([tokens, rounded(tokens_got)], 1).reshape(rows * chip_len, width)
         go_chip = jnp.concatenate(

time: 425 us -> 393 us (0.925)
  waiting for transfers between devices: 185 us -> 165 us
  starting transfers between devices: 85.9 us -> 73 us
    ppermute x74 -> x61, waiting for transfers between devices: 185 us -> 165 us  [send(): return lax.ppermute(value, AXES, self.perm(move))]
    ppermute x74 -> x61, starting transfers between devices: 85.9 us -> 73 us  [send(): return lax.ppermute(value, AXES, self.perm(move))]
    pallas_call x7 -> x8, Pallas kernels: 29.7 us -> 30.8 us  [place_pieces(): pl.pallas_call(kernel, grid_spec=pltpu.PrefetchScalarGridSpec(num_scalar_...]
    unnamed x202 -> x198, local copies, waits for them, and re-layouts: 23.2 us -> 23.7 us
  transfers between devices with their start and end apart: 74 -> 61, of which waited for: 28 -> 25; matrix products, arithmetic and copies ran while one was open for 2% -> 3% of each run, Pallas kernels for 21% -> 23%
where the time goes in v1:
time: 393 us; the launch traced here: 388 us
  waiting for transfers between devices  165 us (42%)
  Pallas kernels  114 us (29%)
  starting transfers between devices  73 us (19%)
  local copies, waits for them, and re-layouts  27.5 us (7%)
  other arithmetic  5.59 us (1%)
    ppermute x61, waiting for transfers between devices, send(): return lax.ppermute(value, AXES, self.perm(move))  165 us
    ppermute x61, starting transfers between devices, send(): return lax.ppermute(value, AXES, self.perm(move))  73 us
    pallas_call x11, Pallas kernels, row_call(): pl.pallas_call(run, grid_spec=pltpu.PrefetchScalarGridSpec(num_scalar_pre...  39.9 us
    pallas_call x8, Pallas kernels, place_pieces(): pl.pallas_call(kernel, grid_spec=pltpu.PrefetchScalarGridSpec(num_scalar_...  30.8 us
    unnamed x198, local copies, waits for them, and re-layouts  23.7 us
    pallas_call x1, Pallas kernels, ffn_forward(): pl.pallas_call(kernel, grid_spec=pltpu.PrefetchScalarGridSpec(num_scalar_...  8.48 us
  transfers between devices with their start and end apart: 61, of which 25 were waited for; matrix products, arithmetic and copies ran while one was open for 3% of the time, Pallas kernels for 23%

profile of v1, /device:TPU:0, one launch (start us, length us, event | category | flops | bytes accessed | tf_op | source)
XLA Modules:
  0.0 388.0 jit_solution(12932260692433498373)
XLA Ops:
  9.2 6.4 %keys.1 = (bf16[1,512,384]{2,1,0:T(8,128)(2,1)S(1)}, bf16[1,512,384]{2,1,0:T(8,128)(2,1)S(1)}, bf16[1,6,512,256]{3,2,1,0:T(8,128)(2,1)S(1)}, f32[1,2,200,256]{3,2,1,0:T(8,128)S(1)}, f32[1,2,200,256]{3,2,1,0:T(8,128)S(1)}) custom-call(s32[2]{0:T(128)S(1)} %pad_add_fusion.info_ref, bf16[1,256,768]{2,1,0:T(8,128)(2,1)S(1)} %copy-done.2, ...), custom_call_target="tpu_custom_call" | custom-call | flops 10000000000 | bytes 1 | tf_op jit(solution)/shard_map/keys/pallas_call | solution.py:509
  18.5 9.8 %collective-permute-done.2.refs_1_ = f32[1,2,200,256]{3,2,1,0:T(8,128)S(1)} collective-permute-done((f32[1,2,200,256]{3,2,1,0:T(8,128)S(1)}, f32[1,2,200,256]{3,2,1,0:T(8,128)S(1)}, u32[]{:S(2)}, u32[]{:S(2)}) %collective-permute-start.2) | collective-permute-done | bytes 409632 | tf_op jit(solution)/shard_map/ppermute | solution.py:79
  36.5 4.4 %collective-permute-start.4 = (f32[1,200,256]{2,1,0:T(8,128)S(1)}, f32[1,200,256]{2,1,0:T(8,128)S(1)}, u32[]{:S(2)}, u32[]{:S(2)}) collective-permute-start(f32[1,200,256]{2,1,0:T(8,128)S(1)} %collective-permute-done.3.refs_2_), channel_id=1, source_target_pairs={{0,4},{1,5},{2,6},{3,7},{4,8},{5,9},{6,10},{7,11},{8,12},{9,13},{1... | collective-permute-start | bytes 614408 | tf_op jit(solution)/shard_map/ppermute | solution.py:79
  44.2 4.4 %collective-permute-done.6.refs_5_ = f32[1,200,256]{2,1,0:T(8,128)S(1)} collective-permute-done((f32[1,200,256]{2,1,0:T(8,128)S(1)}, f32[1,200,256]{2,1,0:T(8,128)S(1)}, u32[]{:S(2)}, u32[]{:S(2)}) %collective-permute-start.6) | collective-permute-done | bytes 204832 | tf_op jit(solution)/shard_map/ppermute | solution.py:79
  51.0 5.0 %queries.1 = (bf16[1,512,384]{2,1,0:T(8,128)(2,1)S(1)}, bf16[1,6,512,256]{3,2,1,0:T(8,128)(2,1)S(1)}, f32[1,512,384]{2,1,0:T(8,128)S(1)}, f32[1,512,128]{2,1,0:T(8,128)S(1)}) custom-call(s32[2]{0:T(128)S(1)} %pad_add_fusion.info_ref, bf16[1,256,768]{2,1,0:T(8,128)(2,1)S(1)} %copy-done.3, f32[1,256,768]{2,1,0:T(8,128)S(1)} %collective-permute-done.refs_1_, ...), custom_call_target="tpu_custom_call" | custom-call | flops 8000000000 | bytes 1 | tf_op jit(solution)/shard_map/queries/pallas_call | solution.py:509
  64.1 8.5 %ffn_forward.1 = (bf16[256,768]{1,0:T(8,128)(2,1)S(1)}, f32[256,768]{1,0:T(8,128)S(1)}, bf16[256,1536]{1,0:T(8,128)(2,1)S(1)}, f32[256,1536]{1,0:T(8,128)}, f32[...) custom-call(s32[2]{0:T(128)S(1)} %pad_add_fusion.info_ref, ...), custom_call_target="tpu_custom_call" | custom-call | flops 15000000512 | bytes 1 | tf_op jit(solution)/shard_map/ffn_forward/pallas_call | solution.py:965
  79.8 4.4 %down_products.2 = (f32[1152,768]{1,0:T(8,128)}, f32[384,768]{1,0:T(8,128)S(1)}) custom-call(s32[2]{0:T(128)S(1)} %get-tuple-element.236.bits_ref, bf16[256,1536]{1,0:T(8,128)(2,1)S(1)} %copy-done.88, f32[256,1536]{1,0:T(8,128)} %collective-permute-done.11.a0o.a1o, bf16[256,1536]{1,0:T(8,128)(2,1)S(1)} %copy-done.88, ...), custom_call_target="tpu_custom_call" | custom-call | flops 12000000000 | bytes 1 | tf_op jit(solution)/shard_map/down_products/pallas_call | solution.py:280
  100.3 4.2 %ffn_back.1 = (f32[256,768]{1,0:T(8,128)S(1)}, bf16[256,768]{1,0:T(8,128)(2,1)S(1)}, f32[256,768]{1,0:T(8,128)S(1)}, f32[8,768]{1,0:T(8,128)S(1)}) custom-call(s32[2]{0:T(128)S(1)} %copy-done.49, bf16[256,1536]{1,0:T(8,128)(2,1)S(1)} %get-tuple-element.140.rest_0_.gi_r.here_r, f32[256,1536]{1,0:T(8,128)} %get-tuple-element.141.send_r, ...), custom_call_target="tpu_custom_call" | custom-call | flops 3000000000 | bytes 1 | tf_op jit(solution)/shard_map/ffn_back/pallas_call | solution.py:1064
  111.1 6.4 %grads_one.1 = (bf16[1,512,384]{2,1,0:T(8,128)(2,1)S(1)}, f32[1,512,128]{2,1,0:T(8,128)S(1)}, f32[1,2,200,256]{3,2,1,0:T(8,128)S(1)}, f32[1,2,200,256]{3,2,1,0:T(8,128)S(1)}) custom-call(s32[2]{0:T(128)S(1)} %copy-done.50, bf16[1,256,768]{2,1,0:T(8,128)(2,1)S(1)} %bitcast.81, f32[1,256,768]{2,1,0:T(8,128)S(1)} %bitcast.64, bf16[768,768]{1,0:T(8,128)(2,1)S(1)} %copy-done.17, ...), custom_call_target="tpu_custom_call" | custom-call | flops 3000000000 | bytes 1 | tf_op jit(solution)/shard_map/grads_one/pallas_call | solution.py:509
  120.1 14.5 %collective-permute-done.15.refs_1_.refs_5_ = f32[1152,768]{1,0:T(8,128)} collective-permute-done((f32[1152,768]{1,0:T(8,128)}, f32[1152,768]{1,0:T(8,128)}, u32[]{:S(2)}, u32[]{:S(2)}) %collective-permute-start.15) | collective-permute-done | bytes 3538976 | tf_op jit(solution)/shard_map/ppermute | solution.py:79
  146.9 4.4 %collective-permute-start.18 = (f32[1,200,256]{2,1,0:T(8,128)S(1)}, f32[1,200,256]{2,1,0:T(8,128)S(1)}, u32[]{:S(2)}, u32[]{:S(2)}) collective-permute-start(f32[1,200,256]{2,1,0:T(8,128)S(1)} %collective-permute-done.17.refs_2_.refs_1_), channel_id=1, source_target_pairs={{0,4},{1,5},{2,6},{3,7},{4,8},{5,9},{6,10},{7,11},{8,12},{9,13},{1... | collective-permute-start | bytes 614408 | tf_op jit(solution)/shard_map/ppermute | solution.py:79
  156.8 4.4 %collective-permute-done.20.refs_5_ = f32[1,200,256]{2,1,0:T(8,128)} collective-permute-done((f32[1,200,256]{2,1,0:T(8,128)S(1)}, f32[1,200,256]{2,1,0:T(8,128)}, u32[]{:S(2)}, u32[]{:S(2)}) %collective-permute-start.20) | collective-permute-done | bytes 204832 | tf_op jit(solution)/shard_map/ppermute | solution.py:79
  165.6 8.5 %grads_two.1 = (bf16[1,512,384]{2,1,0:T(8,128)(2,1)S(1)}, f32[1,6,512,256]{3,2,1,0:T(8,128)S(1)}, f32[1,512,384]{2,1,0:T(8,128)S(1)}) custom-call(s32[2]{0:T(128)S(1)} %copy-done.51, bf16[1,6,512,256]{3,2,1,0:T(8,128)(2,1)S(1)} %copy-done.61, bf16[1,6,512,256]{3,2,1,0:T(8,128)(2,1)S(1)} %copy-done.73, bf16[1,512,384]{2,1,0:T(8,128)(2,1)S(1)} %copy-done.86, ...), custom_call_target="tpu_custom_call" | custom-call | flops 12000000000 | bytes 1 | tf_op jit(solution)/shard_map/grads_two/pallas_call | solution.py:509
  178.3 4.2 %grads_three.1 = (bf16[1,512,384]{2,1,0:T(8,128)(2,1)S(1)}, bf16[1,512,384]{2,1,0:T(8,128)(2,1)S(1)}) custom-call(s32[2]{0:T(128)S(1)} %copy-done.51, bf16[1,6,512,256]{3,2,1,0:T(8,128)(2,1)S(1)} %copy-done.73, bf16[1,512,384]{2,1,0:T(8,128)(2,1)S(1)} %copy-done.82, bf16[1,512,384]{2,1,0:T(8,128)(2,1)S(1)} %copy-done.84, ...), custom_call_target="tpu_custom_call" | custom-call | flops 8000000000 | bytes 1 | tf_op jit(solution)/shard_map/grads_three/pallas_call | solution.py:509
  186.8 11.1 %collective-permute-done.24.refs_1_.refs_5_ = f32[288,768]{1,0:T(8,128)S(1)} collective-permute-done((f32[288,768]{1,0:T(8,128)S(1)}, f32[288,768]{1,0:T(8,128)S(1)}, u32[]{:S(2)}, u32[]{:S(2)}) %collective-permute-start.24) | collective-permute-done | bytes 884768 | tf_op jit(solution)/shard_map/ppermute | solution.py:79
  203.6 4.8 %collective-permute-done.28.refs_3_ = f32[48,768]{1,0:T(8,128)S(1)} collective-permute-done((f32[48,768]{1,0:T(8,128)S(1)}, f32[48,768]{1,0:T(8,128)S(1)}, u32[]{:S(2)}, u32[]{:S(2)}) %collective-permute-start.28) | collective-permute-done | bytes 147488 | tf_op jit(solution)/shard_map/ppermute | solution.py:79
  208.4 4.0 %collective-permute-done.27.refs_2_ = f32[144,768]{1,0:T(8,128)S(1)} collective-permute-done((f32[144,768]{1,0:T(8,128)S(1)}, f32[144,768]{1,0:T(8,128)S(1)}, u32[]{:S(2)}, u32[]{:S(2)}) %collective-permute-start.27) | collective-permute-done | bytes 442400 | tf_op jit(solution)/shard_map/ppermute | solution.py:79
  212.5 4.1 %collective-permute-start.30 = (f32[48,768]{1,0:T(8,128)S(1)}, f32[48,768]{1,0:T(8,128)S(1)}, u32[]{:S(2)}, u32[]{:S(2)}) collective-permute-start(f32[48,768]{1,0:T(8,128)S(1)} %get-tuple-element.193.refs_2_), channel_id=1, source_target_pairs={{0,16},{1,17},{2,18},{3,19},{4,20},{5,21},{6,22},{7,23},{8,24},{9,... | collective-permute-start | bytes 442376 | tf_op jit(solution)/shard_map/ppermute | solution.py:79
  224.9 4.0 %collective-permute-start.34 = (f32[832,384]{1,0:T(8,128)S(1)}, f32[832,384]{1,0:T(8,128)S(1)}, u32[]{:S(2)}, u32[]{:S(2)}) collective-permute-start(f32[832,384]{1,0:T(8,128)S(1)} %get-tuple-element.197), channel_id=1, source_target_pairs={{0,16},{1,3},{2,18},{3,1},{4,20},{5,7},{6,22},{7,5},{8,24},{9,11},... | collective-permute-start | bytes 3833864 | tf_op jit(solution)/shard_map/ppermute | solution.py:79
  228.9 15.2 %collective-permute-done.34.refs_1_.refs_3_ = f32[832,384]{1,0:T(8,128)S(1)} collective-permute-done((f32[832,384]{1,0:T(8,128)S(1)}, f32[832,384]{1,0:T(8,128)S(1)}, u32[]{:S(2)}, u32[]{:S(2)}) %collective-permute-start.34) | collective-permute-done | bytes 1277984 | tf_op jit(solution)/shard_map/ppermute | solution.py:79
  244.4 4.9 %collective-permute-done.31.refs_1_ = f32[288,768]{1,0:T(8,128)S(1)} collective-permute-done((f32[288,768]{1,0:T(8,128)S(1)}, f32[288,768]{1,0:T(8,128)S(1)}, u32[]{:S(2)}, u32[]{:S(2)}) %collective-permute-start.31) | collective-permute-done | bytes 884768 | tf_op jit(solution)/shard_map/ppermute | solution.py:79
  252.8 10.6 %collective-permute-done.43.refs_1_.refs_3_ = f32[416,384]{1,0:T(8,128)S(1)} collective-permute-done((f32[416,384]{1,0:T(8,128)S(1)}, f32[416,384]{1,0:T(8,128)S(1)}, u32[]{:S(2)}, u32[]{:S(2)}) %collective-permute-start.43) | collective-permute-done | bytes 639008 | tf_op jit(solution)/shard_map/ppermute | solution.py:79
  268.7 14.7 %collective-permute-done.40.refs_2_.refs_1_ = f32[192,768]{1,0:T(8,128)} collective-permute-done((f32[192,768]{1,0:T(8,128)S(1)}, f32[192,768]{1,0:T(8,128)}, u32[]{:S(2)}, u32[]{:S(2)}) %collective-permute-start.40) | collective-permute-done | bytes 589856 | tf_op jit(solution)/shard_map/ppermute | solution.py:79
  288.0 4.4 %place_pieces.8 = (f32[768,3072]{1,0:T(8,128)}, f32[3072,768]{1,0:T(8,128)}, f32[8,128]{1,0:T(8,128)S(1)}) custom-call(s32[10]{0:T(128)S(1)} %stack.215.where_ref, f32[576,768]{1,0:T(8,128)} %bitcast.31.refs_0_, f32[192,768]{1,0:T(8,128)S(1)} %bitcast.52, f32[576,768]{1,0:T(8,128)} %collective-permute-done.44.refs_2_, ...), custom_call_target="tpu_custom_call" | custom-call | flops 13500000256 | bytes 1 | tf_op jit(solution)/shard_map/place_pieces/pallas_call | solution.py:417
  292.4 10.3 %collective-permute-done.46.refs_1_ = f32[208,384]{1,0:T(8,128)S(1)} collective-permute-done((f32[208,384]{1,0:T(8,128)S(1)}, f32[208,384]{1,0:T(8,128)S(1)}, u32[]{:S(2)}, u32[]{:S(2)}) %collective-permute-start.46) | collective-permute-done | bytes 319520 | tf_op jit(solution)/shard_map/ppermute | solution.py:79
  308.1 6.5 %collective-permute-done.47.refs_1_ = f32[208,384]{1,0:T(8,128)S(1)} collective-permute-done((f32[208,384]{1,0:T(8,128)S(1)}, f32[208,384]{1,0:T(8,128)S(1)}, u32[]{:S(2)}, u32[]{:S(2)}) %collective-permute-start.47) | collective-permute-done | bytes 319520 | tf_op jit(solution)/shard_map/ppermute | solution.py:79
  314.7 4.4 %place_pieces.9 = (f32[768,3072]{1,0:T(8,128)}, f32[3072,768]{1,0:T(8,128)}, f32[8,128]{1,0:T(8,128)S(1)}) custom-call(s32[10]{0:T(128)S(1)} %stack.214.where_ref, f32[576,768]{1,0:T(8,128)} %collective-permute-done.39.refs_1_.refs_0_, f32[192,768]{1,0:T(8,128)} %collective-permute-done.40.refs_2_.refs_1_, ...), custom_call_target="tpu_custom_call", output_to_operand_aliasing={{0}: (5, {}), {1}: (6, {})} | custom-call | flops 13500000256 | bytes 1 | tf_op jit(solution)/shard_map/place_pieces/pallas_call | solution.py:417
  319.2 12.8 %collective-permute-done.48.refs_1_ = f32[416,384]{1,0:T(8,128)S(1)} collective-permute-done((f32[416,384]{1,0:T(8,128)S(1)}, f32[416,384]{1,0:T(8,128)S(1)}, u32[]{:S(2)}, u32[]{:S(2)}) %collective-permute-start.48) | collective-permute-done | bytes 639008 | tf_op jit(solution)/shard_map/ppermute | solution.py:79
  334.1 4.7 %place_pieces.10 = (f32[768,3072]{1,0:T(8,128)}, f32[3072,768]{1,0:T(8,128)}, f32[8,128]{1,0:T(8,128)S(1)}) custom-call(s32[10]{0:T(128)S(1)} %stack.101.where_ref, f32[576,768]{1,0:T(8,128)} %collective-permute-done.35.refs_0_, f32[192,768]{1,0:T(8,128)} %collective-permute-done.36.refs_1_, ...), custom_call_target="tpu_custom_call", output_to_operand_aliasing={{0}: (5, {}), {1}: (6, {})} | custom-call | flops 13500000256 | bytes 1 | tf_op jit(solution)/shard_map/place_pieces/pallas_call | solution.py:417
  343.5 16.1 %collective-permute-done.57.refs_1_ = f32[192,768]{1,0:T(8,128)} collective-permute-done((f32[192,768]{1,0:T(8,128)}, f32[192,768]{1,0:T(8,128)}, u32[]{:S(2)}, u32[]{:S(2)}) %collective-permute-start.57) | collective-permute-done | bytes 589856 | tf_op jit(solution)/shard_map/ppermute | solution.py:79
  364.3 4.4 %place_pieces.11 = (f32[768,3072]{1,0:T(8,128)}, f32[3072,768]{1,0:T(8,128)}, f32[8,128]{1,0:T(8,128)S(1)}) custom-call(s32[10]{0:T(128)S(1)} %stack.219.where_ref, f32[576,768]{1,0:T(8,128)} %collective-permute-done.56.refs_0_, f32[192,768]{1,0:T(8,128)} %collective-permute-done.57.refs_1_, ...), custom_call_target="tpu_custom_call", output_to_operand_aliasing={{0}: (5, {}), {1}: (6, {})} | custom-call | flops 13500000256 | bytes 1 | tf_op jit(solution)/shard_map/place_pieces/pallas_call | solution.py:417
  368.8 4.3 %place_pieces.12 = (f32[768,768]{1,0:T(8,128)}, f32[768,768]{1,0:T(8,128)}, f32[768,768]{1,0:T(8,128)}, f32[768,768]{1,0:T(8,128)}, f32[8,128]{1,0:T(8,128)S(1)}) custom-call(s32[12]{0:T(128)S(1)} %stack.218.where_ref, f32[832,384]{1,0:T(8,128)} %bitcast.40.refs_6_.refs_0_, f32[832,384]{1,0:T(8,128)S(1)} %collective-permute-done.54.refs_1_, ...), custom_call_target="tpu_custom_call" | custom-call | flops 13500000256 | bytes 1 | tf_op jit(solution)/shard_map/place_pieces/pallas_call | solution.py:417
  (369 shorter events, 154.7 us)
Async XLA Ops:
  15.6 12.7 %collective-permute-start.2 = (f32[1,2,200,256]{3,2,1,0:T(8,128)S(1)}, f32[1,2,200,256]{3,2,1,0:T(8,128)S(1)}, u32[]{:S(2)}, u32[]{:S(2)}) collective-permute-start(f32[1,2,200,256]{3,2,1,0:T(8,128)S(1)} %get-tuple-element.130), channel_id=1, source_target_pairs={{0,2},{1,3},{2,0},{3,1},{4,6},{5,7},{6,4},{7,5},{8,10},{9,11},{10,... | collective-permute-start | bytes 1228808 | tf_op jit(solution)/shard_map/ppermute | solution.py:79
  88.4 46.2 %collective-permute-start.15 = (f32[1152,768]{1,0:T(8,128)}, f32[1152,768]{1,0:T(8,128)}, u32[]{:S(2)}, u32[]{:S(2)}) collective-permute-start(f32[1152,768]{1,0:T(8,128)} %get-tuple-element.166), channel_id=1, source_target_pairs={{0,2},{1,17},{2,0},{3,19},{4,6},{5,21},{6,4},{7,23},{8,10},{9,25},... | collective-permute-start | bytes 10616840 | tf_op jit(solution)/shard_map/ppermute | solution.py:79
  91.3 28.8 %collective-permute-start.16 = (f32[384,768]{1,0:T(8,128)}, f32[384,768]{1,0:T(8,128)S(1)}, u32[]{:S(2)}, u32[]{:S(2)}) collective-permute-start(f32[384,768]{1,0:T(8,128)} %copy-done.24), channel_id=1, source_target_pairs={{0,4},{1,9},{2,6},{3,11},{4,0},{5,13},{6,2},{7,15},{8,12},{9,1},{1... | collective-permute-start | bytes 3538952 | tf_op jit(solution)/shard_map/ppermute | solution.py:79
  117.6 21.8 %collective-permute-start.14 = (f32[1,2,200,256]{3,2,1,0:T(8,128)S(1)}, f32[1,2,200,256]{3,2,1,0:T(8,128)S(1)}, u32[]{:S(2)}, u32[]{:S(2)}) collective-permute-start(f32[1,2,200,256]{3,2,1,0:T(8,128)S(1)} %get-tuple-element.162.refs_8_), channel_id=1, source_target_pairs={{0,2},{1,3},{2,0},{3,1},{4,6},{5,7},{6,4},{7,5},{8,10},{9,11},{10,... | collective-permute-start | bytes 1228808 | tf_op jit(solution)/shard_map/ppermute | solution.py:79
  144.9 29.1 %collective-permute-start.22 = (f32[576,768]{1,0:T(8,128)S(1)}, f32[576,768]{1,0:T(8,128)}, u32[]{:S(2)}, u32[]{:S(2)}) collective-permute-start(f32[576,768]{1,0:T(8,128)S(1)} %get-tuple-element.178), channel_id=1, source_target_pairs={{0,16},{1,3},{2,18},{3,1},{4,20},{5,7},{6,22},{7,5},{8,24},{9,11},... | collective-permute-start | bytes 5308424 | tf_op jit(solution)/shard_map/ppermute | solution.py:79
  153.1 20.9 %collective-permute-start.23 = (f32[192,768]{1,0:T(8,128)S(1)}, f32[192,768]{1,0:T(8,128)S(1)}, u32[]{:S(2)}, u32[]{:S(2)}) collective-permute-start(f32[192,768]{1,0:T(8,128)S(1)} %tie.5), channel_id=1, source_target_pairs={{0,8},{1,5},{2,10},{3,7},{4,12},{5,1},{6,14},{7,3},{8,0},{9,13},{1... | collective-permute-start | bytes 1769480 | tf_op jit(solution)/shard_map/ppermute | solution.py:79
  164.0 14.3 %collective-permute-start.21 = (f32[1,2,200,256]{3,2,1,0:T(8,128)S(1)}, f32[1,2,200,256]{3,2,1,0:T(8,128)S(1)}, u32[]{:S(2)}, u32[]{:S(2)}) collective-permute-start(f32[1,2,200,256]{3,2,1,0:T(8,128)S(1)} %get-tuple-element.176), channel_id=1, source_target_pairs={{0,2},{1,3},{2,0},{3,1},{4,6},{5,7},{6,4},{7,5},{8,10},{9,11},{10,... | collective-permute-start | bytes 1228808 | tf_op jit(solution)/shard_map/ppermute | solution.py:79
  176.4 21.5 %collective-permute-start.24 = (f32[288,768]{1,0:T(8,128)S(1)}, f32[288,768]{1,0:T(8,128)S(1)}, u32[]{:S(2)}, u32[]{:S(2)}) collective-permute-start(f32[288,768]{1,0:T(8,128)S(1)} %get-tuple-element.184), channel_id=1, source_target_pairs={{0,4},{1,9},{2,6},{3,11},{4,0},{5,13},{6,2},{7,15},{8,12},{9,1},{1... | collective-permute-start | bytes 2654216 | tf_op jit(solution)/shard_map/ppermute | solution.py:79
  184.1 40.4 %collective-permute-start.33 = (f32[1664,384]{1,0:T(8,128)S(1)}, f32[1664,384]{1,0:T(8,128)S(1)}, u32[]{:S(2)}, u32[]{:S(2)}) collective-permute-start(f32[1664,384]{1,0:T(8,128)S(1)} %attn_products.2.rest_0_), channel_id=1, source_target_pairs={{0,2},{1,17},{2,0},{3,19},{4,6},{5,21},{6,4},{7,23},{8,10},{9,25},... | collective-permute-start | bytes 7667720 | tf_op jit(solution)/shard_map/ppermute | solution.py:79
  198.6 13.8 %collective-permute-start.27 = (f32[144,768]{1,0:T(8,128)S(1)}, f32[144,768]{1,0:T(8,128)S(1)}, u32[]{:S(2)}, u32[]{:S(2)}) collective-permute-start(f32[144,768]{1,0:T(8,128)S(1)} %get-tuple-element.190), channel_id=1, source_target_pairs={{0,8},{1,5},{2,10},{3,7},{4,12},{5,1},{6,14},{7,3},{8,0},{9,13},{1... | collective-permute-start | bytes 1327112 | tf_op jit(solution)/shard_map/ppermute | solution.py:79
  224.9 19.2 %collective-permute-start.34 = (f32[832,384]{1,0:T(8,128)S(1)}, f32[832,384]{1,0:T(8,128)S(1)}, u32[]{:S(2)}, u32[]{:S(2)}) collective-permute-start(f32[832,384]{1,0:T(8,128)S(1)} %get-tuple-element.197), channel_id=1, source_target_pairs={{0,16},{1,3},{2,18},{3,1},{4,20},{5,7},{6,22},{7,5},{8,24},{9,11},... | collective-permute-start | bytes 3833864 | tf_op jit(solution)/shard_map/ppermute | solution.py:79
  228.9 15.5 %collective-permute-start.32 = (f32[96,768]{1,0:T(8,128)S(1)}, f32[96,768]{1,0:T(8,128)S(1)}, u32[]{:S(2)}, u32[]{:S(2)}) collective-permute-start(f32[96,768]{1,0:T(8,128)S(1)} %bitcast.71), channel_id=1, source_target_pairs={{0,2},{1,3},{2,0},{3,1},{4,6},{5,7},{6,4},{7,5},{8,10},{9,11},{10,... | collective-permute-start | bytes 884744 | tf_op jit(solution)/shard_map/ppermute | solution.py:79
  228.9 20.4 %collective-permute-start.31 = (f32[288,768]{1,0:T(8,128)S(1)}, f32[288,768]{1,0:T(8,128)S(1)}, u32[]{:S(2)}, u32[]{:S(2)}) collective-permute-start(f32[288,768]{1,0:T(8,128)S(1)} %bitcast.60), channel_id=1, source_target_pairs={{0,4},{1,9},{2,6},{3,11},{4,0},{5,13},{6,2},{7,15},{8,12},{9,1},{1... | collective-permute-start | bytes 2654216 | tf_op jit(solution)/shard_map/ppermute | solution.py:79
  244.3 19.1 %collective-permute-start.43 = (f32[416,384]{1,0:T(8,128)S(1)}, f32[416,384]{1,0:T(8,128)S(1)}, u32[]{:S(2)}, u32[]{:S(2)}) collective-permute-start(f32[416,384]{1,0:T(8,128)S(1)} %get-tuple-element.198.refs_4_), channel_id=1, source_target_pairs={{0,4},{1,9},{2,6},{3,11},{4,0},{5,13},{6,2},{7,15},{8,12},{9,1},{1... | collective-permute-start | bytes 1916936 | tf_op jit(solution)/shard_map/ppermute | solution.py:79
  251.2 32.2 %collective-permute-start.39 = (f32[576,768]{1,0:T(8,128)}, f32[576,768]{1,0:T(8,128)}, u32[]{:S(2)}, u32[]{:S(2)}) collective-permute-start(f32[576,768]{1,0:T(8,128)} %bitcast.31.refs_0_), channel_id=1, source_target_pairs={{0,16},{1,3},{2,18},{3,1},{4,20},{5,7},{6,22},{7,5},{8,24},{9,11},... | collective-permute-start | bytes 5308424 | tf_op jit(solution)/shard_map/ppermute | solution.py:79
  264.3 23.7 %collective-permute-start.44 = (f32[576,768]{1,0:T(8,128)S(1)}, f32[576,768]{1,0:T(8,128)}, u32[]{:S(2)}, u32[]{:S(2)}) collective-permute-start(f32[576,768]{1,0:T(8,128)S(1)} %tie.6), channel_id=1, source_target_pairs={{0,1},{1,0},{2,3},{3,2},{4,5},{5,4},{6,7},{7,6},{8,9},{9,8},{10,11... | collective-permute-start | bytes 5308424 | tf_op jit(solution)/shard_map/ppermute | solution.py:79
  266.7 16.8 %collective-permute-start.40 = (f32[192,768]{1,0:T(8,128)S(1)}, f32[192,768]{1,0:T(8,128)}, u32[]{:S(2)}, u32[]{:S(2)}) collective-permute-start(f32[192,768]{1,0:T(8,128)S(1)} %bitcast.49), channel_id=1, source_target_pairs={{0,8},{1,5},{2,10},{3,7},{4,12},{5,1},{6,14},{7,3},{8,0},{9,13},{1... | collective-permute-start | bytes 1769480 | tf_op jit(solution)/shard_map/ppermute | solution.py:79
  267.5 20.5 %collective-permute-start.45 = (f32[192,768]{1,0:T(8,128)S(1)}, f32[192,768]{1,0:T(8,128)}, u32[]{:S(2)}, u32[]{:S(2)}) collective-permute-start(f32[192,768]{1,0:T(8,128)S(1)} %tie.7), channel_id=1, source_target_pairs={{0,1},{1,0},{2,3},{3,2},{4,5},{5,4},{6,7},{7,6},{8,9},{9,8},{10,11... | collective-permute-start | bytes 1769480 | tf_op jit(solution)/shard_map/ppermute | solution.py:79
  267.6 39.3 %collective-permute-start.35 = (f32[576,768]{1,0:T(8,128)}, f32[576,768]{1,0:T(8,128)}, u32[]{:S(2)}, u32[]{:S(2)}) collective-permute-start(f32[576,768]{1,0:T(8,128)} %bitcast.31.refs_0_), channel_id=1, source_target_pairs={{0,2},{1,17},{2,0},{3,19},{4,6},{5,21},{6,4},{7,23},{8,10},{9,25},... | collective-permute-start | bytes 5308424 | tf_op jit(solution)/shard_map/ppermute | solution.py:79
  283.4 23.0 %collective-permute-start.36 = (f32[192,768]{1,0:T(8,128)S(1)}, f32[192,768]{1,0:T(8,128)}, u32[]{:S(2)}, u32[]{:S(2)}) collective-permute-start(f32[192,768]{1,0:T(8,128)S(1)} %bitcast.51), channel_id=1, source_target_pairs={{0,4},{1,9},{2,6},{3,11},{4,0},{5,13},{6,2},{7,15},{8,12},{9,1},{1... | collective-permute-start | bytes 1769480 | tf_op jit(solution)/shard_map/ppermute | solution.py:79
  283.4 19.3 %collective-permute-start.46 = (f32[208,384]{1,0:T(8,128)S(1)}, f32[208,384]{1,0:T(8,128)S(1)}, u32[]{:S(2)}, u32[]{:S(2)}) collective-permute-start(f32[208,384]{1,0:T(8,128)S(1)} %get-tuple-element.202.refs_1_.refs_4_), channel_id=1, source_target_pairs={{0,8},{1,5},{2,10},{3,7},{4,12},{5,1},{6,14},{7,3},{8,0},{9,13},{1... | collective-permute-start | bytes 958472 | tf_op jit(solution)/shard_map/ppermute | solution.py:79
  287.9 26.8 %collective-permute-start.41 = (f32[576,768]{1,0:T(8,128)}, f32[576,768]{1,0:T(8,128)}, u32[]{:S(2)}, u32[]{:S(2)}) collective-permute-start(f32[576,768]{1,0:T(8,128)} %collective-permute-done.39.refs_1_.refs_0_), channel_id=1, source_target_pairs={{0,1},{1,0},{2,3},{3,2},{4,5},{5,4},{6,7},{7,6},{8,9},{9,8},{10,11... | collective-permute-start | bytes 5308424 | tf_op jit(solution)/shard_map/ppermute | solution.py:79
  306.4 27.6 %collective-permute-start.38 = (f32[192,768]{1,0:T(8,128)}, f32[192,768]{1,0:T(8,128)S(1)}, u32[]{:S(2)}, u32[]{:S(2)}) collective-permute-start(f32[192,768]{1,0:T(8,128)} %collective-permute-done.36.refs_1_), channel_id=1, source_target_pairs={{0,1},{1,0},{2,3},{3,2},{4,5},{5,4},{6,7},{7,6},{8,9},{9,8},{10,11... | collective-permute-start | bytes 1769480 | tf_op jit(solution)/shard_map/ppermute | solution.py:79
  306.9 26.6 %collective-permute-start.56 = (f32[576,768]{1,0:T(8,128)}, f32[576,768]{1,0:T(8,128)}, u32[]{:S(2)}, u32[]{:S(2)}) collective-permute-start(f32[576,768]{1,0:T(8,128)} %collective-permute-done.39.refs_1_.refs_0_), channel_id=1, source_target_pairs={{0,2},{1,17},{2,0},{3,19},{4,6},{5,21},{6,4},{7,23},{8,10},{9,25},... | collective-permute-start | bytes 5308424 | tf_op jit(solution)/shard_map/ppermute | solution.py:79
  314.6 19.4 %collective-permute-start.37 = (f32[576,768]{1,0:T(8,128)}, f32[576,768]{1,0:T(8,128)S(1)}, u32[]{:S(2)}, u32[]{:S(2)}) collective-permute-start(f32[576,768]{1,0:T(8,128)} %collective-permute-done.35.refs_0_), channel_id=1, source_target_pairs={{0,1},{1,0},{2,3},{3,2},{4,5},{5,4},{6,7},{7,6},{8,9},{9,8},{10,11... | collective-permute-start | bytes 5308424 | tf_op jit(solution)/shard_map/ppermute | solution.py:79
  314.6 17.3 %collective-permute-start.48 = (f32[416,384]{1,0:T(8,128)S(1)}, f32[416,384]{1,0:T(8,128)S(1)}, u32[]{:S(2)}, u32[]{:S(2)}) collective-permute-start(f32[416,384]{1,0:T(8,128)S(1)} %bitcast.65), channel_id=1, source_target_pairs={{0,4},{1,9},{2,6},{3,11},{4,0},{5,13},{6,2},{7,15},{8,12},{9,1},{1... | collective-permute-start | bytes 1916936 | tf_op jit(solution)/shard_map/ppermute | solution.py:79
  333.1 29.2 %collective-permute-start.50 = (f32[832,384]{1,0:T(8,128)}, f32[832,384]{1,0:T(8,128)S(1)}, u32[]{:S(2)}, u32[]{:S(2)}) collective-permute-start(f32[832,384]{1,0:T(8,128)} %bitcast.40.refs_6_.refs_0_), channel_id=1, source_target_pairs={{0,16},{1,3},{2,18},{3,1},{4,20},{5,7},{6,22},{7,5},{8,24},{9,11},... | collective-permute-start | bytes 3833864 | tf_op jit(solution)/shard_map/ppermute | solution.py:79
  333.5 30.8 %collective-permute-start.58 = (f32[576,768]{1,0:T(8,128)}, f32[576,768]{1,0:T(8,128)}, u32[]{:S(2)}, u32[]{:S(2)}) collective-permute-start(f32[576,768]{1,0:T(8,128)} %collective-permute-done.56.refs_0_), channel_id=1, source_target_pairs={{0,1},{1,0},{2,3},{3,2},{4,5},{5,4},{6,7},{7,6},{8,9},{9,8},{10,11... | collective-permute-start | bytes 5308424 | tf_op jit(solution)/shard_map/ppermute | solution.py:79
  341.7 18.0 %collective-permute-start.49 = (f32[1,256,768]{2,1,0:T(8,128)}, f32[1,256,768]{2,1,0:T(8,128)}, u32[]{:S(2)}, u32[]{:S(2)}) collective-permute-start(f32[1,256,768]{2,1,0:T(8,128)} %get-tuple-element.212.refs_6_), channel_id=1, source_target_pairs={{0,1},{1,0},{2,3},{3,2},{4,5},{5,4},{6,7},{7,6},{8,9},{9,8},{10,11... | collective-permute-start | bytes 2359304 | tf_op jit(solution)/shard_map/ppermute | solution.py:79
  341.8 21.9 %collective-permute-start.52 = (f32[832,384]{1,0:T(8,128)}, f32[832,384]{1,0:T(8,128)}, u32[]{:S(2)}, u32[]{:S(2)}) collective-permute-start(f32[832,384]{1,0:T(8,128)} %bitcast.40.refs_6_.refs_0_), channel_id=1, source_target_pairs={{0,2},{1,17},{2,0},{3,19},{4,6},{5,21},{6,4},{7,23},{8,10},{9,25},... | collective-permute-start | bytes 3833864 | tf_op jit(solution)/shard_map/ppermute | solution.py:79
  343.2 16.5 %collective-permute-start.57 = (f32[192,768]{1,0:T(8,128)}, f32[192,768]{1,0:T(8,128)}, u32[]{:S(2)}, u32[]{:S(2)}) collective-permute-start(f32[192,768]{1,0:T(8,128)} %collective-permute-done.40.refs_2_.refs_1_), channel_id=1, source_target_pairs={{0,4},{1,9},{2,6},{3,11},{4,0},{5,13},{6,2},{7,15},{8,12},{9,1},{1... | collective-permute-start | bytes 1769480 | tf_op jit(solution)/shard_map/ppermute | solution.py:79
  363.1 17.3 %collective-permute-start.51 = (f32[832,384]{1,0:T(8,128)S(1)}, f32[832,384]{1,0:T(8,128)S(1)}, u32[]{:S(2)}, u32[]{:S(2)}) collective-permute-start(f32[832,384]{1,0:T(8,128)S(1)} %collective-permute-done.50.refs_2_), channel_id=1, source_target_pairs={{0,2},{1,17},{2,0},{3,19},{4,6},{5,21},{6,4},{7,23},{8,10},{9,25},... | collective-permute-start | bytes 3833864 | tf_op jit(solution)/shard_map/ppermute | solution.py:79
  (127 other events, 1053.2 us)

commit v2 on v1

--- a/solution.py
+++ b/solution.py
@@ -22,6 +22,8 @@
     "up_products 2": 1, "attn_products": 12, "place_pieces": 13.5, "ffn_forward": 15, "ffn_inner": 8,
     "ffn_back": 3, "keys": 10, "queries": 8, "attend": 6, "grads_one": 3, "grads_two": 12, "grads_three": 8,
     "shares": 9, "join_plane": 3, "split_plane": 3,
+    "join_stage 2": 3,
+    "add_stage 5": 6,
 }
 CALLS = {}
 

time: 393 us -> 392 us (level)
  transfers between devices with their start and end apart: 61 -> 61, of which waited for: 25 -> 27; matrix products, arithmetic and copies ran while one was open for 3% -> 3% of each run, Pallas kernels for 23% -> 23%
where the time goes in v2:
time: 392 us; the launch traced here: 387 us
  waiting for transfers between devices  162 us (41%)
  Pallas kernels  114 us (29%)
  starting transfers between devices  75.1 us (19%)
  local copies, waits for them, and re-layouts  27.5 us (7%)
  other arithmetic  5.59 us (1%)
    ppermute x61, waiting for transfers between devices, send(): return lax.ppermute(value, AXES, self.perm(move))  162 us
    ppermute x61, starting transfers between devices, send(): return lax.ppermute(value, AXES, self.perm(move))  75.1 us
    pallas_call x11, Pallas kernels, row_call(): pl.pallas_call(run, grid_spec=pltpu.PrefetchScalarGridSpec(num_scalar_pre...  39.9 us
    pallas_call x8, Pallas kernels, place_pieces(): pl.pallas_call(kernel, grid_spec=pltpu.PrefetchScalarGridSpec(num_scalar_...  30.8 us
    unnamed x198, local copies, waits for them, and re-layouts  23.7 us
    pallas_call x1, Pallas kernels, ffn_forward(): pl.pallas_call(kernel, grid_spec=pltpu.PrefetchScalarGridSpec(num_scalar_...  8.48 us
  transfers between devices with their start and end apart: 61, of which 27 were waited for; matrix products, arithmetic and copies ran while one was open for 3% of the time, Pallas kernels for 23%

profile of v2, /device:TPU:0, one launch (start us, length us, event | category | flops | bytes accessed | tf_op | source)
XLA Modules:
  0.0 386.6 jit_solution(7709040817505645213)
XLA Ops:
  9.2 6.4 %keys.1 = (bf16[1,512,384]{2,1,0:T(8,128)(2,1)S(1)}, bf16[1,512,384]{2,1,0:T(8,128)(2,1)S(1)}, bf16[1,6,512,256]{3,2,1,0:T(8,128)(2,1)S(1)}, f32[1,2,200,256]{3,2,1,0:T(8,128)S(1)}, f32[1,2,200,256]{3,2,1,0:T(8,128)S(1)}) custom-call(s32[2]{0:T(128)S(1)} %pad_add_fusion.info_ref, bf16[1,256,768]{2,1,0:T(8,128)(2,1)S(1)} %copy-done.2, ...), custom_call_target="tpu_custom_call" | custom-call | flops 10000000000 | bytes 1 | tf_op jit(solution)/shard_map/keys/pallas_call | solution.py:511
  18.5 9.8 %collective-permute-done.2.refs_1_ = f32[1,2,200,256]{3,2,1,0:T(8,128)S(1)} collective-permute-done((f32[1,2,200,256]{3,2,1,0:T(8,128)S(1)}, f32[1,2,200,256]{3,2,1,0:T(8,128)S(1)}, u32[]{:S(2)}, u32[]{:S(2)}) %collective-permute-start.2) | collective-permute-done | bytes 409632 | tf_op jit(solution)/shard_map/ppermute | solution.py:81
  36.5 4.4 %collective-permute-start.4 = (f32[1,200,256]{2,1,0:T(8,128)S(1)}, f32[1,200,256]{2,1,0:T(8,128)S(1)}, u32[]{:S(2)}, u32[]{:S(2)}) collective-permute-start(f32[1,200,256]{2,1,0:T(8,128)S(1)} %collective-permute-done.3.refs_2_), channel_id=1, source_target_pairs={{0,4},{1,5},{2,6},{3,7},{4,8},{5,9},{6,10},{7,11},{8,12},{9,13},{1... | collective-permute-start | bytes 614408 | tf_op jit(solution)/shard_map/ppermute | solution.py:81
  44.2 4.4 %collective-permute-done.6.refs_5_ = f32[1,200,256]{2,1,0:T(8,128)S(1)} collective-permute-done((f32[1,200,256]{2,1,0:T(8,128)S(1)}, f32[1,200,256]{2,1,0:T(8,128)S(1)}, u32[]{:S(2)}, u32[]{:S(2)}) %collective-permute-start.6) | collective-permute-done | bytes 204832 | tf_op jit(solution)/shard_map/ppermute | solution.py:81
  51.0 5.0 %queries.1 = (bf16[1,512,384]{2,1,0:T(8,128)(2,1)S(1)}, bf16[1,6,512,256]{3,2,1,0:T(8,128)(2,1)S(1)}, f32[1,512,384]{2,1,0:T(8,128)S(1)}, f32[1,512,128]{2,1,0:T(8,128)S(1)}) custom-call(s32[2]{0:T(128)S(1)} %pad_add_fusion.info_ref, bf16[1,256,768]{2,1,0:T(8,128)(2,1)S(1)} %copy-done.3, f32[1,256,768]{2,1,0:T(8,128)S(1)} %collective-permute-done.refs_1_, ...), custom_call_target="tpu_custom_call" | custom-call | flops 8000000000 | bytes 1 | tf_op jit(solution)/shard_map/queries/pallas_call | solution.py:511
  64.1 8.5 %ffn_forward.1 = (bf16[256,768]{1,0:T(8,128)(2,1)S(1)}, f32[256,768]{1,0:T(8,128)S(1)}, bf16[256,1536]{1,0:T(8,128)(2,1)S(1)}, f32[256,1536]{1,0:T(8,128)}, f32[...) custom-call(s32[2]{0:T(128)S(1)} %pad_add_fusion.info_ref, ...), custom_call_target="tpu_custom_call" | custom-call | flops 15000000512 | bytes 1 | tf_op jit(solution)/shard_map/ffn_forward/pallas_call | solution.py:967
  79.8 4.4 %down_products.2 = (f32[1152,768]{1,0:T(8,128)}, f32[384,768]{1,0:T(8,128)S(1)}) custom-call(s32[2]{0:T(128)S(1)} %get-tuple-element.236.bits_ref, bf16[256,1536]{1,0:T(8,128)(2,1)S(1)} %copy-done.88, f32[256,1536]{1,0:T(8,128)} %collective-permute-done.11.a0o.a1o, bf16[256,1536]{1,0:T(8,128)(2,1)S(1)} %copy-done.88, ...), custom_call_target="tpu_custom_call" | custom-call | flops 12000000000 | bytes 1 | tf_op jit(solution)/shard_map/down_products/pallas_call | solution.py:282
  100.4 4.2 %ffn_back.1 = (f32[256,768]{1,0:T(8,128)S(1)}, bf16[256,768]{1,0:T(8,128)(2,1)S(1)}, f32[256,768]{1,0:T(8,128)S(1)}, f32[8,768]{1,0:T(8,128)S(1)}) custom-call(s32[2]{0:T(128)S(1)} %copy-done.49, bf16[256,1536]{1,0:T(8,128)(2,1)S(1)} %get-tuple-element.140.rest_0_.gi_r.here_r, f32[256,1536]{1,0:T(8,128)} %get-tuple-element.141.send_r, ...), custom_call_target="tpu_custom_call" | custom-call | flops 3000000000 | bytes 1 | tf_op jit(solution)/shard_map/ffn_back/pallas_call | solution.py:1066
  111.1 6.4 %grads_one.1 = (bf16[1,512,384]{2,1,0:T(8,128)(2,1)S(1)}, f32[1,512,128]{2,1,0:T(8,128)S(1)}, f32[1,2,200,256]{3,2,1,0:T(8,128)S(1)}, f32[1,2,200,256]{3,2,1,0:T(8,128)S(1)}) custom-call(s32[2]{0:T(128)S(1)} %copy-done.50, bf16[1,256,768]{2,1,0:T(8,128)(2,1)S(1)} %bitcast.81, f32[1,256,768]{2,1,0:T(8,128)S(1)} %bitcast.64, bf16[768,768]{1,0:T(8,128)(2,1)S(1)} %copy-done.17, ...), custom_call_target="tpu_custom_call" | custom-call | flops 3000000000 | bytes 1 | tf_op jit(solution)/shard_map/grads_one/pallas_call | solution.py:511
  120.1 14.5 %collective-permute-done.15.refs_1_.refs_5_ = f32[1152,768]{1,0:T(8,128)} collective-permute-done((f32[1152,768]{1,0:T(8,128)}, f32[1152,768]{1,0:T(8,128)}, u32[]{:S(2)}, u32[]{:S(2)}) %collective-permute-start.15) | collective-permute-done | bytes 3538976 | tf_op jit(solution)/shard_map/ppermute | solution.py:81
  146.9 4.4 %collective-permute-start.18 = (f32[1,200,256]{2,1,0:T(8,128)S(1)}, f32[1,200,256]{2,1,0:T(8,128)S(1)}, u32[]{:S(2)}, u32[]{:S(2)}) collective-permute-start(f32[1,200,256]{2,1,0:T(8,128)S(1)} %collective-permute-done.17.refs_2_.refs_1_), channel_id=1, source_target_pairs={{0,4},{1,5},{2,6},{3,7},{4,8},{5,9},{6,10},{7,11},{8,12},{9,13},{1... | collective-permute-start | bytes 614408 | tf_op jit(solution)/shard_map/ppermute | solution.py:81
  156.8 4.4 %collective-permute-done.20.refs_5_ = f32[1,200,256]{2,1,0:T(8,128)} collective-permute-done((f32[1,200,256]{2,1,0:T(8,128)S(1)}, f32[1,200,256]{2,1,0:T(8,128)}, u32[]{:S(2)}, u32[]{:S(2)}) %collective-permute-start.20) | collective-permute-done | bytes 204832 | tf_op jit(solution)/shard_map/ppermute | solution.py:81
  165.6 8.5 %grads_two.1 = (bf16[1,512,384]{2,1,0:T(8,128)(2,1)S(1)}, f32[1,6,512,256]{3,2,1,0:T(8,128)S(1)}, f32[1,512,384]{2,1,0:T(8,128)S(1)}) custom-call(s32[2]{0:T(128)S(1)} %copy-done.51, bf16[1,6,512,256]{3,2,1,0:T(8,128)(2,1)S(1)} %copy-done.61, bf16[1,6,512,256]{3,2,1,0:T(8,128)(2,1)S(1)} %copy-done.73, bf16[1,512,384]{2,1,0:T(8,128)(2,1)S(1)} %copy-done.86, ...), custom_call_target="tpu_custom_call" | custom-call | flops 12000000000 | bytes 1 | tf_op jit(solution)/shard_map/grads_two/pallas_call | solution.py:511
  178.3 4.2 %grads_three.1 = (bf16[1,512,384]{2,1,0:T(8,128)(2,1)S(1)}, bf16[1,512,384]{2,1,0:T(8,128)(2,1)S(1)}) custom-call(s32[2]{0:T(128)S(1)} %copy-done.51, bf16[1,6,512,256]{3,2,1,0:T(8,128)(2,1)S(1)} %copy-done.73, bf16[1,512,384]{2,1,0:T(8,128)(2,1)S(1)} %copy-done.82, bf16[1,512,384]{2,1,0:T(8,128)(2,1)S(1)} %copy-done.84, ...), custom_call_target="tpu_custom_call" | custom-call | flops 8000000000 | bytes 1 | tf_op jit(solution)/shard_map/grads_three/pallas_call | solution.py:511
  186.8 11.1 %collective-permute-done.24.refs_1_.refs_5_ = f32[288,768]{1,0:T(8,128)S(1)} collective-permute-done((f32[288,768]{1,0:T(8,128)S(1)}, f32[288,768]{1,0:T(8,128)S(1)}, u32[]{:S(2)}, u32[]{:S(2)}) %collective-permute-start.24) | collective-permute-done | bytes 884768 | tf_op jit(solution)/shard_map/ppermute | solution.py:81
  203.6 4.8 %collective-permute-done.28.refs_3_ = f32[48,768]{1,0:T(8,128)S(1)} collective-permute-done((f32[48,768]{1,0:T(8,128)S(1)}, f32[48,768]{1,0:T(8,128)S(1)}, u32[]{:S(2)}, u32[]{:S(2)}) %collective-permute-start.28) | collective-permute-done | bytes 147488 | tf_op jit(solution)/shard_map/ppermute | solution.py:81
  208.4 4.0 %collective-permute-done.27.refs_2_ = f32[144,768]{1,0:T(8,128)S(1)} collective-permute-done((f32[144,768]{1,0:T(8,128)S(1)}, f32[144,768]{1,0:T(8,128)S(1)}, u32[]{:S(2)}, u32[]{:S(2)}) %collective-permute-start.27) | collective-permute-done | bytes 442400 | tf_op jit(solution)/shard_map/ppermute | solution.py:81
  212.5 4.1 %collective-permute-start.30 = (f32[48,768]{1,0:T(8,128)S(1)}, f32[48,768]{1,0:T(8,128)S(1)}, u32[]{:S(2)}, u32[]{:S(2)}) collective-permute-start(f32[48,768]{1,0:T(8,128)S(1)} %get-tuple-element.193.refs_2_), channel_id=1, source_target_pairs={{0,16},{1,17},{2,18},{3,19},{4,20},{5,21},{6,22},{7,23},{8,24},{9,... | collective-permute-start | bytes 442376 | tf_op jit(solution)/shard_map/ppermute | solution.py:81
  228.9 15.2 %collective-permute-done.34.refs_1_.refs_3_ = f32[832,384]{1,0:T(8,128)S(1)} collective-permute-done((f32[832,384]{1,0:T(8,128)S(1)}, f32[832,384]{1,0:T(8,128)S(1)}, u32[]{:S(2)}, u32[]{:S(2)}) %collective-permute-start.34) | collective-permute-done | bytes 1277984 | tf_op jit(solution)/shard_map/ppermute | solution.py:81
  244.5 9.5 %collective-permute-done.32.refs_3_ = f32[96,768]{1,0:T(8,128)S(1)} collective-permute-done((f32[96,768]{1,0:T(8,128)S(1)}, f32[96,768]{1,0:T(8,128)S(1)}, u32[]{:S(2)}, u32[]{:S(2)}) %collective-permute-start.32) | collective-permute-done | bytes 294944 | tf_op jit(solution)/shard_map/ppermute | solution.py:81
  258.8 6.3 %collective-permute-done.43.refs_1_.refs_3_ = f32[416,384]{1,0:T(8,128)S(1)} collective-permute-done((f32[416,384]{1,0:T(8,128)S(1)}, f32[416,384]{1,0:T(8,128)S(1)}, u32[]{:S(2)}, u32[]{:S(2)}) %collective-permute-start.43) | collective-permute-done | bytes 639008 | tf_op jit(solution)/shard_map/ppermute | solution.py:81
  268.0 14.9 %collective-permute-done.40.refs_2_.refs_1_ = f32[192,768]{1,0:T(8,128)} collective-permute-done((f32[192,768]{1,0:T(8,128)S(1)}, f32[192,768]{1,0:T(8,128)}, u32[]{:S(2)}, u32[]{:S(2)}) %collective-permute-start.40) | collective-permute-done | bytes 589856 | tf_op jit(solution)/shard_map/ppermute | solution.py:81
  282.9 4.2 %collective-permute-done.39.refs_1_.refs_0_ = f32[576,768]{1,0:T(8,128)} collective-permute-done((f32[576,768]{1,0:T(8,128)}, f32[576,768]{1,0:T(8,128)}, u32[]{:S(2)}, u32[]{:S(2)}) %collective-permute-start.39) | collective-permute-done | bytes 1769504 | tf_op jit(solution)/shard_map/ppermute | solution.py:81
  291.5 4.4 %place_pieces.8 = (f32[768,3072]{1,0:T(8,128)}, f32[3072,768]{1,0:T(8,128)}, f32[8,128]{1,0:T(8,128)S(1)}) custom-call(s32[10]{0:T(128)S(1)} %stack.215.where_ref, f32[576,768]{1,0:T(8,128)} %bitcast.31.refs_0_, f32[192,768]{1,0:T(8,128)S(1)} %bitcast.52, f32[576,768]{1,0:T(8,128)} %collective-permute-done.44.refs_2_, ...), custom_call_target="tpu_custom_call" | custom-call | flops 13500000256 | bytes 1 | tf_op jit(solution)/shard_map/place_pieces/pallas_call | solution.py:419
  295.9 5.2 %collective-permute-done.46.refs_1_ = f32[208,384]{1,0:T(8,128)S(1)} collective-permute-done((f32[208,384]{1,0:T(8,128)S(1)}, f32[208,384]{1,0:T(8,128)S(1)}, u32[]{:S(2)}, u32[]{:S(2)}) %collective-permute-start.46) | collective-permute-done | bytes 319520 | tf_op jit(solution)/shard_map/ppermute | solution.py:81
  307.2 4.2 %collective-permute-done.47.refs_1_ = f32[208,384]{1,0:T(8,128)S(1)} collective-permute-done((f32[208,384]{1,0:T(8,128)S(1)}, f32[208,384]{1,0:T(8,128)S(1)}, u32[]{:S(2)}, u32[]{:S(2)}) %collective-permute-start.47) | collective-permute-done | bytes 319520 | tf_op jit(solution)/shard_map/ppermute | solution.py:81
  313.8 4.4 %place_pieces.9 = (f32[768,3072]{1,0:T(8,128)}, f32[3072,768]{1,0:T(8,128)}, f32[8,128]{1,0:T(8,128)S(1)}) custom-call(s32[10]{0:T(128)S(1)} %stack.214.where_ref, f32[576,768]{1,0:T(8,128)} %collective-permute-done.39.refs_1_.refs_0_, f32[192,768]{1,0:T(8,128)} %collective-permute-done.40.refs_2_.refs_1_, ...), custom_call_target="tpu_custom_call", output_to_operand_aliasing={{0}: (5, {}), {1}: (6, {})} | custom-call | flops 13500000256 | bytes 1 | tf_op jit(solution)/shard_map/place_pieces/pallas_call | solution.py:419
  318.3 12.1 %collective-permute-done.48.refs_1_ = f32[416,384]{1,0:T(8,128)S(1)} collective-permute-done((f32[416,384]{1,0:T(8,128)S(1)}, f32[416,384]{1,0:T(8,128)S(1)}, u32[]{:S(2)}, u32[]{:S(2)}) %collective-permute-start.48) | collective-permute-done | bytes 639008 | tf_op jit(solution)/shard_map/ppermute | solution.py:81
  333.3 4.7 %place_pieces.10 = (f32[768,3072]{1,0:T(8,128)}, f32[3072,768]{1,0:T(8,128)}, f32[8,128]{1,0:T(8,128)S(1)}) custom-call(s32[10]{0:T(128)S(1)} %stack.101.where_ref, f32[576,768]{1,0:T(8,128)} %collective-permute-done.35.refs_0_, f32[192,768]{1,0:T(8,128)} %collective-permute-done.36.refs_1_, ...), custom_call_target="tpu_custom_call", output_to_operand_aliasing={{0}: (5, {}), {1}: (6, {})} | custom-call | flops 13500000256 | bytes 1 | tf_op jit(solution)/shard_map/place_pieces/pallas_call | solution.py:419
  342.4 15.8 %collective-permute-done.57.refs_1_ = f32[192,768]{1,0:T(8,128)} collective-permute-done((f32[192,768]{1,0:T(8,128)}, f32[192,768]{1,0:T(8,128)}, u32[]{:S(2)}, u32[]{:S(2)}) %collective-permute-start.57) | collective-permute-done | bytes 589856 | tf_op jit(solution)/shard_map/ppermute | solution.py:81
  363.6 4.4 %place_pieces.11 = (f32[768,3072]{1,0:T(8,128)}, f32[3072,768]{1,0:T(8,128)}, f32[8,128]{1,0:T(8,128)S(1)}) custom-call(s32[10]{0:T(128)S(1)} %stack.219.where_ref, f32[576,768]{1,0:T(8,128)} %collective-permute-done.56.refs_0_, f32[192,768]{1,0:T(8,128)} %collective-permute-done.57.refs_1_, ...), custom_call_target="tpu_custom_call", output_to_operand_aliasing={{0}: (5, {}), {1}: (6, {})} | custom-call | flops 13500000256 | bytes 1 | tf_op jit(solution)/shard_map/place_pieces/pallas_call | solution.py:419
  368.0 4.3 %place_pieces.12 = (f32[768,768]{1,0:T(8,128)}, f32[768,768]{1,0:T(8,128)}, f32[768,768]{1,0:T(8,128)}, f32[768,768]{1,0:T(8,128)}, f32[8,128]{1,0:T(8,128)S(1)}) custom-call(s32[12]{0:T(128)S(1)} %stack.218.where_ref, f32[832,384]{1,0:T(8,128)} %bitcast.40.refs_6_.refs_0_, f32[832,384]{1,0:T(8,128)S(1)} %collective-permute-done.54.refs_1_, ...), custom_call_target="tpu_custom_call" | custom-call | flops 13500000256 | bytes 1 | tf_op jit(solution)/shard_map/place_pieces/pallas_call | solution.py:419
  (369 shorter events, 161.0 us)
Async XLA Ops:
  15.6 12.7 %collective-permute-start.2 = (f32[1,2,200,256]{3,2,1,0:T(8,128)S(1)}, f32[1,2,200,256]{3,2,1,0:T(8,128)S(1)}, u32[]{:S(2)}, u32[]{:S(2)}) collective-permute-start(f32[1,2,200,256]{3,2,1,0:T(8,128)S(1)} %get-tuple-element.130), channel_id=1, source_target_pairs={{0,2},{1,3},{2,0},{3,1},{4,6},{5,7},{6,4},{7,5},{8,10},{9,11},{10,... | collective-permute-start | bytes 1228808 | tf_op jit(solution)/shard_map/ppermute | solution.py:81
  88.4 46.2 %collective-permute-start.15 = (f32[1152,768]{1,0:T(8,128)}, f32[1152,768]{1,0:T(8,128)}, u32[]{:S(2)}, u32[]{:S(2)}) collective-permute-start(f32[1152,768]{1,0:T(8,128)} %get-tuple-element.166), channel_id=1, source_target_pairs={{0,2},{1,17},{2,0},{3,19},{4,6},{5,21},{6,4},{7,23},{8,10},{9,25},... | collective-permute-start | bytes 10616840 | tf_op jit(solution)/shard_map/ppermute | solution.py:81
  91.3 28.8 %collective-permute-start.16 = (f32[384,768]{1,0:T(8,128)}, f32[384,768]{1,0:T(8,128)S(1)}, u32[]{:S(2)}, u32[]{:S(2)}) collective-permute-start(f32[384,768]{1,0:T(8,128)} %copy-done.24), channel_id=1, source_target_pairs={{0,4},{1,9},{2,6},{3,11},{4,0},{5,13},{6,2},{7,15},{8,12},{9,1},{1... | collective-permute-start | bytes 3538952 | tf_op jit(solution)/shard_map/ppermute | solution.py:81
  117.6 21.8 %collective-permute-start.14 = (f32[1,2,200,256]{3,2,1,0:T(8,128)S(1)}, f32[1,2,200,256]{3,2,1,0:T(8,128)S(1)}, u32[]{:S(2)}, u32[]{:S(2)}) collective-permute-start(f32[1,2,200,256]{3,2,1,0:T(8,128)S(1)} %get-tuple-element.162.refs_8_), channel_id=1, source_target_pairs={{0,2},{1,3},{2,0},{3,1},{4,6},{5,7},{6,4},{7,5},{8,10},{9,11},{10,... | collective-permute-start | bytes 1228808 | tf_op jit(solution)/shard_map/ppermute | solution.py:81
  144.9 29.1 %collective-permute-start.22 = (f32[576,768]{1,0:T(8,128)S(1)}, f32[576,768]{1,0:T(8,128)}, u32[]{:S(2)}, u32[]{:S(2)}) collective-permute-start(f32[576,768]{1,0:T(8,128)S(1)} %get-tuple-element.178), channel_id=1, source_target_pairs={{0,16},{1,3},{2,18},{3,1},{4,20},{5,7},{6,22},{7,5},{8,24},{9,11},... | collective-permute-start | bytes 5308424 | tf_op jit(solution)/shard_map/ppermute | solution.py:81
  153.1 20.9 %collective-permute-start.23 = (f32[192,768]{1,0:T(8,128)S(1)}, f32[192,768]{1,0:T(8,128)S(1)}, u32[]{:S(2)}, u32[]{:S(2)}) collective-permute-start(f32[192,768]{1,0:T(8,128)S(1)} %tie.5), channel_id=1, source_target_pairs={{0,8},{1,5},{2,10},{3,7},{4,12},{5,1},{6,14},{7,3},{8,0},{9,13},{1... | collective-permute-start | bytes 1769480 | tf_op jit(solution)/shard_map/ppermute | solution.py:81
  164.0 14.3 %collective-permute-start.21 = (f32[1,2,200,256]{3,2,1,0:T(8,128)S(1)}, f32[1,2,200,256]{3,2,1,0:T(8,128)S(1)}, u32[]{:S(2)}, u32[]{:S(2)}) collective-permute-start(f32[1,2,200,256]{3,2,1,0:T(8,128)S(1)} %get-tuple-element.176), channel_id=1, source_target_pairs={{0,2},{1,3},{2,0},{3,1},{4,6},{5,7},{6,4},{7,5},{8,10},{9,11},{10,... | collective-permute-start | bytes 1228808 | tf_op jit(solution)/shard_map/ppermute | solution.py:81
  176.4 21.5 %collective-permute-start.24 = (f32[288,768]{1,0:T(8,128)S(1)}, f32[288,768]{1,0:T(8,128)S(1)}, u32[]{:S(2)}, u32[]{:S(2)}) collective-permute-start(f32[288,768]{1,0:T(8,128)S(1)} %get-tuple-element.184), channel_id=1, source_target_pairs={{0,4},{1,9},{2,6},{3,11},{4,0},{5,13},{6,2},{7,15},{8,12},{9,1},{1... | collective-permute-start | bytes 2654216 | tf_op jit(solution)/shard_map/ppermute | solution.py:81
  184.1 40.4 %collective-permute-start.33 = (f32[1664,384]{1,0:T(8,128)S(1)}, f32[1664,384]{1,0:T(8,128)S(1)}, u32[]{:S(2)}, u32[]{:S(2)}) collective-permute-start(f32[1664,384]{1,0:T(8,128)S(1)} %attn_products.2.rest_0_), channel_id=1, source_target_pairs={{0,2},{1,17},{2,0},{3,19},{4,6},{5,21},{6,4},{7,23},{8,10},{9,25},... | collective-permute-start | bytes 7667720 | tf_op jit(solution)/shard_map/ppermute | solution.py:81
  198.6 13.8 %collective-permute-start.27 = (f32[144,768]{1,0:T(8,128)S(1)}, f32[144,768]{1,0:T(8,128)S(1)}, u32[]{:S(2)}, u32[]{:S(2)}) collective-permute-start(f32[144,768]{1,0:T(8,128)S(1)} %get-tuple-element.190), channel_id=1, source_target_pairs={{0,8},{1,5},{2,10},{3,7},{4,12},{5,1},{6,14},{7,3},{8,0},{9,13},{1... | collective-permute-start | bytes 1327112 | tf_op jit(solution)/shard_map/ppermute | solution.py:81
  212.5 11.5 %collective-permute-start.29 = (f32[144,768]{1,0:T(8,128)S(1)}, f32[144,768]{1,0:T(8,128)S(1)}, u32[]{:S(2)}, u32[]{:S(2)}) collective-permute-start(f32[144,768]{1,0:T(8,128)S(1)} %get-tuple-element.192.refs_0_), channel_id=1, source_target_pairs={{0,8},{1,5},{2,10},{3,7},{4,12},{5,1},{6,14},{7,3},{8,0},{9,13},{1... | collective-permute-start | bytes 1327112 | tf_op jit(solution)/shard_map/ppermute | solution.py:81
  224.9 19.2 %collective-permute-start.34 = (f32[832,384]{1,0:T(8,128)S(1)}, f32[832,384]{1,0:T(8,128)S(1)}, u32[]{:S(2)}, u32[]{:S(2)}) collective-permute-start(f32[832,384]{1,0:T(8,128)S(1)} %get-tuple-element.197), channel_id=1, source_target_pairs={{0,16},{1,3},{2,18},{3,1},{4,20},{5,7},{6,22},{7,5},{8,24},{9,11},... | collective-permute-start | bytes 3833864 | tf_op jit(solution)/shard_map/ppermute | solution.py:81
  228.9 25.1 %collective-permute-start.31 = (f32[288,768]{1,0:T(8,128)S(1)}, f32[288,768]{1,0:T(8,128)S(1)}, u32[]{:S(2)}, u32[]{:S(2)}) collective-permute-start(f32[288,768]{1,0:T(8,128)S(1)} %bitcast.60), channel_id=1, source_target_pairs={{0,4},{1,9},{2,6},{3,11},{4,0},{5,13},{6,2},{7,15},{8,12},{9,1},{1... | collective-permute-start | bytes 2654216 | tf_op jit(solution)/shard_map/ppermute | solution.py:81
  244.3 20.8 %collective-permute-start.43 = (f32[416,384]{1,0:T(8,128)S(1)}, f32[416,384]{1,0:T(8,128)S(1)}, u32[]{:S(2)}, u32[]{:S(2)}) collective-permute-start(f32[416,384]{1,0:T(8,128)S(1)} %get-tuple-element.198.refs_4_), channel_id=1, source_target_pairs={{0,4},{1,9},{2,6},{3,11},{4,0},{5,13},{6,2},{7,15},{8,12},{9,1},{1... | collective-permute-start | bytes 1916936 | tf_op jit(solution)/shard_map/ppermute | solution.py:81
  255.9 31.2 %collective-permute-start.39 = (f32[576,768]{1,0:T(8,128)}, f32[576,768]{1,0:T(8,128)}, u32[]{:S(2)}, u32[]{:S(2)}) collective-permute-start(f32[576,768]{1,0:T(8,128)} %bitcast.31.refs_0_), channel_id=1, source_target_pairs={{0,16},{1,3},{2,18},{3,1},{4,20},{5,7},{6,22},{7,5},{8,24},{9,11},... | collective-permute-start | bytes 5308424 | tf_op jit(solution)/shard_map/ppermute | solution.py:81
  265.9 25.5 %collective-permute-start.44 = (f32[576,768]{1,0:T(8,128)S(1)}, f32[576,768]{1,0:T(8,128)}, u32[]{:S(2)}, u32[]{:S(2)}) collective-permute-start(f32[576,768]{1,0:T(8,128)S(1)} %tie.6), channel_id=1, source_target_pairs={{0,1},{1,0},{2,3},{3,2},{4,5},{5,4},{6,7},{7,6},{8,9},{9,8},{10,11... | collective-permute-start | bytes 5308424 | tf_op jit(solution)/shard_map/ppermute | solution.py:81
  265.9 16.9 %collective-permute-start.40 = (f32[192,768]{1,0:T(8,128)S(1)}, f32[192,768]{1,0:T(8,128)}, u32[]{:S(2)}, u32[]{:S(2)}) collective-permute-start(f32[192,768]{1,0:T(8,128)S(1)} %bitcast.49), channel_id=1, source_target_pairs={{0,8},{1,5},{2,10},{3,7},{4,12},{5,1},{6,14},{7,3},{8,0},{9,13},{1... | collective-permute-start | bytes 1769480 | tf_op jit(solution)/shard_map/ppermute | solution.py:81
  266.7 24.7 %collective-permute-start.45 = (f32[192,768]{1,0:T(8,128)S(1)}, f32[192,768]{1,0:T(8,128)}, u32[]{:S(2)}, u32[]{:S(2)}) collective-permute-start(f32[192,768]{1,0:T(8,128)S(1)} %tie.7), channel_id=1, source_target_pairs={{0,1},{1,0},{2,3},{3,2},{4,5},{5,4},{6,7},{7,6},{8,9},{9,8},{10,11... | collective-permute-start | bytes 1769480 | tf_op jit(solution)/shard_map/ppermute | solution.py:81
  266.9 38.8 %collective-permute-start.35 = (f32[576,768]{1,0:T(8,128)}, f32[576,768]{1,0:T(8,128)}, u32[]{:S(2)}, u32[]{:S(2)}) collective-permute-start(f32[576,768]{1,0:T(8,128)} %bitcast.31.refs_0_), channel_id=1, source_target_pairs={{0,2},{1,17},{2,0},{3,19},{4,6},{5,21},{6,4},{7,23},{8,10},{9,25},... | collective-permute-start | bytes 5308424 | tf_op jit(solution)/shard_map/ppermute | solution.py:81
  282.9 22.9 %collective-permute-start.36 = (f32[192,768]{1,0:T(8,128)S(1)}, f32[192,768]{1,0:T(8,128)}, u32[]{:S(2)}, u32[]{:S(2)}) collective-permute-start(f32[192,768]{1,0:T(8,128)S(1)} %bitcast.51), channel_id=1, source_target_pairs={{0,4},{1,9},{2,6},{3,11},{4,0},{5,13},{6,2},{7,15},{8,12},{9,1},{1... | collective-permute-start | bytes 1769480 | tf_op jit(solution)/shard_map/ppermute | solution.py:81
  287.0 14.1 %collective-permute-start.46 = (f32[208,384]{1,0:T(8,128)S(1)}, f32[208,384]{1,0:T(8,128)S(1)}, u32[]{:S(2)}, u32[]{:S(2)}) collective-permute-start(f32[208,384]{1,0:T(8,128)S(1)} %get-tuple-element.202.refs_1_.refs_4_), channel_id=1, source_target_pairs={{0,8},{1,5},{2,10},{3,7},{4,12},{5,1},{6,14},{7,3},{8,0},{9,13},{1... | collective-permute-start | bytes 958472 | tf_op jit(solution)/shard_map/ppermute | solution.py:81
  291.5 22.4 %collective-permute-start.41 = (f32[576,768]{1,0:T(8,128)}, f32[576,768]{1,0:T(8,128)}, u32[]{:S(2)}, u32[]{:S(2)}) collective-permute-start(f32[576,768]{1,0:T(8,128)} %collective-permute-done.39.refs_1_.refs_0_), channel_id=1, source_target_pairs={{0,1},{1,0},{2,3},{3,2},{4,5},{5,4},{6,7},{7,6},{8,9},{9,8},{10,11... | collective-permute-start | bytes 5308424 | tf_op jit(solution)/shard_map/ppermute | solution.py:81
  305.7 27.5 %collective-permute-start.38 = (f32[192,768]{1,0:T(8,128)}, f32[192,768]{1,0:T(8,128)S(1)}, u32[]{:S(2)}, u32[]{:S(2)}) collective-permute-start(f32[192,768]{1,0:T(8,128)} %collective-permute-done.36.refs_1_), channel_id=1, source_target_pairs={{0,1},{1,0},{2,3},{3,2},{4,5},{5,4},{6,7},{7,6},{8,9},{9,8},{10,11... | collective-permute-start | bytes 1769480 | tf_op jit(solution)/shard_map/ppermute | solution.py:81
  305.7 27.5 %collective-permute-start.56 = (f32[576,768]{1,0:T(8,128)}, f32[576,768]{1,0:T(8,128)}, u32[]{:S(2)}, u32[]{:S(2)}) collective-permute-start(f32[576,768]{1,0:T(8,128)} %collective-permute-done.39.refs_1_.refs_0_), channel_id=1, source_target_pairs={{0,2},{1,17},{2,0},{3,19},{4,6},{5,21},{6,4},{7,23},{8,10},{9,25},... | collective-permute-start | bytes 5308424 | tf_op jit(solution)/shard_map/ppermute | solution.py:81
  311.4 21.8 %collective-permute-start.37 = (f32[576,768]{1,0:T(8,128)}, f32[576,768]{1,0:T(8,128)S(1)}, u32[]{:S(2)}, u32[]{:S(2)}) collective-permute-start(f32[576,768]{1,0:T(8,128)} %collective-permute-done.35.refs_0_), channel_id=1, source_target_pairs={{0,1},{1,0},{2,3},{3,2},{4,5},{5,4},{6,7},{7,6},{8,9},{9,8},{10,11... | collective-permute-start | bytes 5308424 | tf_op jit(solution)/shard_map/ppermute | solution.py:81
  313.3 17.1 %collective-permute-start.48 = (f32[416,384]{1,0:T(8,128)S(1)}, f32[416,384]{1,0:T(8,128)S(1)}, u32[]{:S(2)}, u32[]{:S(2)}) collective-permute-start(f32[416,384]{1,0:T(8,128)S(1)} %bitcast.65), channel_id=1, source_target_pairs={{0,4},{1,9},{2,6},{3,11},{4,0},{5,13},{6,2},{7,15},{8,12},{9,1},{1... | collective-permute-start | bytes 1916936 | tf_op jit(solution)/shard_map/ppermute | solution.py:81
  331.6 29.3 %collective-permute-start.50 = (f32[832,384]{1,0:T(8,128)}, f32[832,384]{1,0:T(8,128)S(1)}, u32[]{:S(2)}, u32[]{:S(2)}) collective-permute-start(f32[832,384]{1,0:T(8,128)} %bitcast.40.refs_6_.refs_0_), channel_id=1, source_target_pairs={{0,16},{1,3},{2,18},{3,1},{4,20},{5,7},{6,22},{7,5},{8,24},{9,11},... | collective-permute-start | bytes 3833864 | tf_op jit(solution)/shard_map/ppermute | solution.py:81
  333.2 30.4 %collective-permute-start.58 = (f32[576,768]{1,0:T(8,128)}, f32[576,768]{1,0:T(8,128)}, u32[]{:S(2)}, u32[]{:S(2)}) collective-permute-start(f32[576,768]{1,0:T(8,128)} %collective-permute-done.56.refs_0_), channel_id=1, source_target_pairs={{0,1},{1,0},{2,3},{3,2},{4,5},{5,4},{6,7},{7,6},{8,9},{9,8},{10,11... | collective-permute-start | bytes 5308424 | tf_op jit(solution)/shard_map/ppermute | solution.py:81
  340.9 17.3 %collective-permute-start.49 = (f32[1,256,768]{2,1,0:T(8,128)}, f32[1,256,768]{2,1,0:T(8,128)}, u32[]{:S(2)}, u32[]{:S(2)}) collective-permute-start(f32[1,256,768]{2,1,0:T(8,128)} %get-tuple-element.212.refs_6_), channel_id=1, source_target_pairs={{0,1},{1,0},{2,3},{3,2},{4,5},{5,4},{6,7},{7,6},{8,9},{9,8},{10,11... | collective-permute-start | bytes 2359304 | tf_op jit(solution)/shard_map/ppermute | solution.py:81
  341.4 21.9 %collective-permute-start.52 = (f32[832,384]{1,0:T(8,128)}, f32[832,384]{1,0:T(8,128)}, u32[]{:S(2)}, u32[]{:S(2)}) collective-permute-start(f32[832,384]{1,0:T(8,128)} %bitcast.40.refs_6_.refs_0_), channel_id=1, source_target_pairs={{0,2},{1,17},{2,0},{3,19},{4,6},{5,21},{6,4},{7,23},{8,10},{9,25},... | collective-permute-start | bytes 3833864 | tf_op jit(solution)/shard_map/ppermute | solution.py:81
  341.7 16.5 %collective-permute-start.57 = (f32[192,768]{1,0:T(8,128)}, f32[192,768]{1,0:T(8,128)}, u32[]{:S(2)}, u32[]{:S(2)}) collective-permute-start(f32[192,768]{1,0:T(8,128)} %collective-permute-done.40.refs_2_.refs_1_), channel_id=1, source_target_pairs={{0,4},{1,9},{2,6},{3,11},{4,0},{5,13},{6,2},{7,15},{8,12},{9,1},{1... | collective-permute-start | bytes 1769480 | tf_op jit(solution)/shard_map/ppermute | solution.py:81
  361.6 17.3 %collective-permute-start.51 = (f32[832,384]{1,0:T(8,128)S(1)}, f32[832,384]{1,0:T(8,128)S(1)}, u32[]{:S(2)}, u32[]{:S(2)}) collective-permute-start(f32[832,384]{1,0:T(8,128)S(1)} %collective-permute-done.50.refs_2_), channel_id=1, source_target_pairs={{0,2},{1,17},{2,0},{3,19},{4,6},{5,21},{6,4},{7,23},{8,10},{9,25},... | collective-permute-start | bytes 3833864 | tf_op jit(solution)/shard_map/ppermute | solution.py:81
  (127 other events, 1045.1 us)
